TPU v7x, 32 devices: a whole 2x2x4 slice. The times are simulated.
32 devices in a mesh: slab: 4 (over y, x), dom: 8 (over z, core).
Axes of the slice: x: 2, y: 2, z: 4, core: 2. Of those that a mesh axis runs over, the one named last changes fastest.
Arguments:
- positions: float32 [3, 32768], P(None, ('slab', 'dom')), may hold values from 0 to 8, as said below
- velocities: float32 [3, 32768], P(None, ('slab', 'dom')), may hold values from -3 to 3
- mass: float32 [32768], P(('slab', 'dom')), may hold values from 0.005 to 0.012
- smoothing: float32 [32768], P(('slab', 'dom')), may hold values from 0.25 to 0.4
- energy: float32 [32768], P(('slab', 'dom')), may hold values from 0.5 to 32, as said below
- send_offsets: int32 [4, 32], P(None, ('slab', 'dom')), may hold values from 0 to 7, as said below
- send_counts: int32 [4, 32], P(None, ('slab', 'dom')), may hold values from 1 to 8, as said below
- pair_blocks: int32 [8, 256], P(None, ('slab', 'dom')), may hold values from 0 to 40, as said below
Outputs:
- density: float32 [32768], P(('slab', 'dom'))
- acceleration: float32 [3, 32768], P(None, ('slab', 'dom'))
- heating: float32 [32768], P(('slab', 'dom'))
- step_share: float32 [32768], P(('slab', 'dom'))
Inputs may be any that keep to these rules, and one draw needn't show every extreme that they name: `positions`: particle i of block g lies in the unit cube whose lowest corner is (slab index, domain index, local block index) of g. `energy`: largest near the middle of the box. `send_offsets`: offset plus count never passes 8. `send_counts`: some window holds all 8 blocks in every draw. `pair_blocks`: the first entry of each list is the block itself; an entry 8 (1 + r) + t names only a slot t below the count of the window received from direction r; 40 names no block; no other entry repeats within a list.
All inputs are finite; a program needn't handle non-finite values.
Results may differ from a plain program's by a relative error of at most 0.0003.
Values sent between devices are 32-bit elements; how exact they have to be, the bound alone decides.
No kernel may reach another device: no remote copies, remote signals or barrier semaphores. Data moves between devices by JAX's collectives and lax.ppermute only.
A program may use at most 64 MiB of HBM per device.

v0:
```python
import math

import jax
import jax.numpy as jnp
from jax import lax
from jax.sharding import PartitionSpec as P

gas_gamma = 5.0 / 3.0
visc_alpha = 1.0
visc_beta = 2.0
courant = 0.4
index_pairs = ((0, 0), (1, 1), (2, 2), (0, 1), (0, 2), (1, 2))


def padded(value, sides, width):
    for axis, dim in sides:
        size, length = (lax.axis_size(axis), value.shape[dim])
        up = [(i, (i + 1) % size) for i in range(size - 1)]
        down = [(j, i) for i, j in up]
        last = lax.slice_in_dim(value, length - width, length, axis=dim)
        first = lax.slice_in_dim(value, 0, width, axis=dim)
        before = lax.ppermute(last, axis, up)
        after = lax.ppermute(first, axis, down)
        value = jnp.concatenate([before, value, after], axis=dim)
    return value


def kernel(distance, length):
    ratio = distance / length
    shape = 0.25 * jnp.maximum(2.0 - ratio, 0.0) ** 3 - jnp.maximum(1.0 - ratio, 0.0) ** 3
    return shape / (math.pi * length**3)


def apply_matrix(matrix, vector):
    return jnp.stack(
        [
            matrix[0] * vector[0] + matrix[3] * vector[1] + matrix[4] * vector[2],
            matrix[3] * vector[0] + matrix[1] * vector[1] + matrix[5] * vector[2],
            matrix[4] * vector[0] + matrix[5] * vector[1] + matrix[2] * vector[2],
        ]
    )


def block_density(pos_own, len_own, pos_near, mass_near):
    separation = pos_near[:, :, None] - pos_own[:, None, :]
    dist_sq = jnp.sum(separation * separation, axis=0)
    weight = mass_near[:, None] * kernel(jnp.sqrt(dist_sq), len_own[None, :])
    dens = jnp.sum(weight, axis=0)
    moments = [
        jnp.sum(weight * separation[first] * separation[second], axis=0) / dens
        for first, second in index_pairs
    ]
    floor = 0.05 * len_own * len_own
    axx = moments[0] + floor
    ayy = moments[1] + floor
    azz = moments[2] + floor
    axy, axz, ayz = (moments[3], moments[4], moments[5])
    cof_xx = ayy * azz - ayz * ayz
    cof_yy = axx * azz - axz * axz
    cof_zz = axx * ayy - axy * axy
    cof_xy = axz * ayz - axy * azz
    cof_xz = axy * ayz - ayy * axz
    cof_yz = axy * axz - axx * ayz
    determinant = axx * cof_xx + axy * cof_xy + axz * cof_xz
    matrix = jnp.stack([cof_xx, cof_yy, cof_zz, cof_xy, cof_xz, cof_yz]) / determinant
    return (dens, matrix)


def block_momentum(own_fields, near_fields):
    separation = near_fields[0:3, :, None] - own_fields[0:3, None, :]
    dist_sq = jnp.sum(separation * separation, axis=0)
    mean_len = 0.5 * (near_fields[7][:, None] + own_fields[7][None, :])
    kernel_val = kernel(jnp.sqrt(dist_sq), mean_len)
    grad_own = apply_matrix(own_fields[11:17, None, :], separation) * kernel_val
    grad_near = apply_matrix(near_fields[11:17, :, None], separation) * kernel_val
    grad_sum = grad_own + grad_near
    rel_vel = own_fields[4:7, None, :] - near_fields[4:7, :, None]
    closing = jnp.minimum(-jnp.sum(rel_vel * separation, axis=0), 0.0)
    closing_rate = mean_len * closing / (dist_sq + 0.01 * mean_len * mean_len)
    mean_sound = 0.5 * (own_fields[8][None, :] + near_fields[8][:, None])
    mean_dens = 0.5 * (own_fields[10][None, :] + near_fields[10][:, None])
    viscous = (
        -visc_alpha * mean_sound * closing_rate + visc_beta * closing_rate * closing_rate
    ) / mean_dens
    near_mass = near_fields[3][:, None]
    press_own = own_fields[9][None, :]
    press_near = near_fields[9][:, None]
    acceleration = -jnp.sum(
        near_mass * (press_own * grad_own + press_near * grad_near + 0.5 * viscous * grad_sum),
        axis=1,
    )
    heating = own_fields[9] * jnp.sum(near_mass * jnp.sum(rel_vel * grad_own, axis=0), axis=0)
    heating = heating + 0.25 * jnp.sum(
        near_mass * viscous * jnp.sum(rel_vel * grad_sum, axis=0), axis=0
    )
    signal = jnp.max(own_fields[8][None, :] + near_fields[8][:, None] - 3.0 * closing_rate, axis=0)
    return (acceleration, heating, signal)


def body(positions, velocities, mass, smoothing, energy, send_offsets, send_counts, pair_blocks):
    blocks = pair_blocks.shape[1]
    points = positions.shape[1] // blocks
    slots = jnp.arange(blocks, dtype=jnp.int32)
    chooser = (
        (slots[None, None, :] == send_offsets[:, :, None] + slots[None, :, None])
        & (slots[None, :, None] < send_counts[:, :, None])
    ).astype(jnp.float32)

    def windows(fields):
        shaped = fields.reshape(fields.shape[0], blocks, points)
        return jnp.einsum("rtb,fbk->rftk", chooser, shaped, precision=lax.Precision.HIGHEST)

    def assemble(local, from_slab, from_dom):
        shaped = local.reshape(local.shape[0], blocks, points)
        empty = jnp.zeros((local.shape[0], 1, points), jnp.float32)
        return jnp.concatenate(
            [shaped, from_slab[0], from_slab[3], from_dom[0], from_dom[3], empty], axis=1
        )

    def neighbours(table):
        picked = jnp.take(table, pair_blocks, axis=1)
        return picked.transpose(2, 0, 1, 3).reshape(blocks, table.shape[0], -1)

    def per_block(fields):
        return fields.reshape(fields.shape[0], blocks, points).transpose(1, 0, 2)

    sound = jnp.sqrt(gas_gamma * (gas_gamma - 1.0) * energy)
    first = jnp.concatenate([positions, mass[None]], axis=0)
    outgoing = windows(first)
    slab_first = padded(outgoing[0:2], (("slab", 0),), 1)
    dom_first = padded(outgoing[2:4], (("dom", 0),), 1)
    table_first = assemble(first, slab_first, dom_first)
    near_first = neighbours(table_first)

    def density_item(item):
        own_fields, near = item
        return block_density(own_fields[0:3], own_fields[3], near[0:3], near[3])

    own_first = per_block(jnp.concatenate([positions, smoothing[None]], axis=0))
    dens_parts, matrix_parts = lax.map(density_item, (own_first, near_first))
    density = dens_parts.reshape(-1)
    matrices = matrix_parts.transpose(1, 0, 2).reshape(6, -1)
    pressure = (gas_gamma - 1.0) * energy / density
    second = jnp.concatenate(
        [velocities, smoothing[None], sound[None], pressure[None], density[None], matrices], axis=0
    )
    outgoing_second = windows(second)
    slab_second = padded(outgoing_second[0:2], (("slab", 0),), 1)
    dom_second = padded(outgoing_second[2:4], (("dom", 0),), 1)
    table_second = assemble(second, slab_second, dom_second)
    near_all = neighbours(jnp.concatenate([table_first, table_second], axis=0))
    own_all = jnp.concatenate(
        [
            positions,
            mass[None],
            velocities,
            smoothing[None],
            sound[None],
            pressure[None],
            density[None],
            matrices,
        ],
        axis=0,
    )

    def momentum_item(item):
        own_fields, near = item
        return block_momentum(own_fields, near)

    accel_parts, heat_parts, signal_parts = lax.map(momentum_item, (per_block(own_all), near_all))
    acceleration = accel_parts.transpose(1, 0, 2).reshape(3, -1)
    heating = heat_parts.reshape(-1)
    allowed = courant * smoothing / signal_parts.reshape(-1)
    step = lax.pmin(jnp.min(allowed), ("slab", "dom"))
    return (density, acceleration, heating, step / allowed)


def solution(mesh):
    in_specs = (
        P(None, ("slab", "dom")),
        P(None, ("slab", "dom")),
        P(("slab", "dom")),
        P(("slab", "dom")),
        P(("slab", "dom")),
        P(None, ("slab", "dom")),
        P(None, ("slab", "dom")),
        P(None, ("slab", "dom")),
    )
    out_specs = (
        P(("slab", "dom")),
        P(None, ("slab", "dom")),
        P(("slab", "dom")),
        P(("slab", "dom")),
    )
    return jax.shard_map(body, mesh=mesh, in_specs=in_specs, out_specs=out_specs, check_vma=False)
```

profile of v0, /device:TPU:0, one launch (start us, length us, event | category | flops | bytes accessed | tf_op | source)
XLA Modules:
  0.0 142.3 jit_solution(15507466155164374406)
XLA Ops:
  0.6 0.7 iota_compare_fusion.1
  1.4 0.7 iota_add_fusion
  2.1 0.7 constant_dynamic-update-slice_fusion.29
  2.8 0.9 convolution_bitcast_fusion.1
  3.7 1.3 collective-permute-start.3
  5.0 3.0 %collective-permute-start.2 = (f32[1,4,8,128]{3,2,1,0:T(8,128)S(1)}, f32[1,4,8,128]{3,2,1,0:T(8,128)S(1)}, u32[]{:S(2)}, u32[]{:S(2)}) collective-permute-start(f32[1,4,8,128]{3,2,1,0:T(8,128)S(1)} %get-tuple-element.247), channel_id=1, source_target_pairs={{0,1},{1,2},{2,3},{3,4},{4,5},{5,6},{6,7},{8,9},{9,10},{10,11},{11... | collective-permute-start | bytes 49160 | tf_op jit(solution)/shard_map/ppermute | solution.py:22
  8.1 1.3 collective-permute-start.1
  9.4 5.5 %collective-permute-start = (f32[1,4,8,128]{3,2,1,0:T(8,128)S(1)}, f32[1,4,8,128]{3,2,1,0:T(8,128)S(1)}, u32[]{:S(2)}, u32[]{:S(2)}) collective-permute-start(f32[1,4,8,128]{3,2,1,0:T(8,128)S(1)} %get-tuple-element.249), channel_id=1, source_target_pairs={{0,8},{8,16},{16,24},{1,9},{9,17},{17,25},{2,10},{10,18},{18,26},{... | collective-permute-start | bytes 49160 | tf_op jit(solution)/shard_map/ppermute | solution.py:22
  14.8 0.7 and_bitcast_fusion
  15.5 0.7 compare_select_fusion
  16.3 0.7 constant_dynamic-update-slice_fusion.28
  17.0 0.7 fusion.42
  17.7 0.7 constant_dynamic-update-slice_fusion.27
  18.4 0.7 constant_dynamic-update-slice_fusion.26
  19.1 0.7 constant_dynamic-update-slice_fusion.25
  20.8 11.3 %while.28 = (s32[]{:T(128)}, f32[8,128]{1,0:T(8,128)S(1)}, f32[8,6,128]{2,0,1:T(8,128)S(1)}, f32[8,4,1024]{2,1,0:T(4,128)S(1)}, f32[8,4,128]{2,0,1:T(8,128)S(1)}, /*index=5*/s32[]{:T(128)}, s32[]{:T(128)}, s32[]{}) while((s32[]{:T(128)}, f32[8,128]{1,0:T(8,128)S(1)}, f32[8,6,128]{2,0,1:T(8,128)S(1)}, f32[8,4,1024]{2,1,0:T(4,128)S(1)}, ...), condition=%wide.region_9.10_spmd, body=%wide.region_0.9_spmd.sunk | while | flops 4856067 | bytes 4299393 | solution.py:140
  32.5 4.8 %collective-permute-start.4 = (f32[1,13,8,128]{3,2,1,0:T(8,128)S(1)}, f32[1,13,8,128]{3,2,1,0:T(8,128)S(1)}, u32[]{:S(2)}, u32[]{:S(2)}) collective-permute-start(f32[1,13,8,128]{3,2,1,0:T(8,128)S(1)} %get-tuple-element.245), channel_id=1, source_target_pairs={{0,8},{8,16},{16,24},{1,9},{9,17},{17,25},{2,10},{10,18},{18,26},{... | collective-permute-start | bytes 159752 | tf_op jit(solution)/shard_map/ppermute | solution.py:22
  37.4 1.3 collective-permute-start.7
  38.7 3.0 %collective-permute-start.6 = (f32[1,13,8,128]{3,2,1,0:T(8,128)S(1)}, f32[1,13,8,128]{3,2,1,0:T(8,128)S(1)}, u32[]{:S(2)}, u32[]{:S(2)}) collective-permute-start(f32[1,13,8,128]{3,2,1,0:T(8,128)S(1)} %get-tuple-element.243), channel_id=1, source_target_pairs={{0,1},{1,2},{2,3},{3,4},{4,5},{5,6},{6,7},{8,9},{9,10},{10,11},{11... | collective-permute-start | bytes 159752 | tf_op jit(solution)/shard_map/ppermute | solution.py:22
  41.8 1.3 collective-permute-start.5
  43.1 4.7 %collective-permute-done.5 = f32[1,13,8,128]{3,2,1,0:T(8,128)S(1)} collective-permute-done((f32[1,13,8,128]{3,2,1,0:T(8,128)S(1)}, f32[1,13,8,128]{3,2,1,0:T(8,128)S(1)}, u32[]{:S(2)}, u32[]{:S(2)}) %collective-permute-start.5) | collective-permute-done | bytes 53280 | tf_op jit(solution)/shard_map/ppermute | solution.py:23
  49.2 51.4 %while.29 = (s32[]{:T(128)}, f32[8,3,128]{2,1,0:T(4,128)S(1)}, f32[8,128]{1,0:T(8,128)S(1)}, f32[8,128]{1,0:T(8,128)S(1)}, f32[8,17,1024]{2,0,1:T(8,128)S(1)}, /...) while((s32[]{:T(128)}, f32[8,3,128]{2,1,0:T(4,128)S(1)}, ...), condition=%wide.region_19.20_spmd, body=%wide.region_10.19_spmd.sunk | while | flops 21495820 | bytes 21317580 | solution.py:170
  50.4 1.0 multiply_add_fusion.11
  51.7 1.2 fusion.70
  53.4 1.7 %fusion.71 = (f32[1024,128]{1,0:T(8,128)S(1)}, f32[3,128]{1,0:T(4,128)S(1)}) fusion(f32[1,1024,128]{2,1,0:T(8,128)S(1)} %get-tuple-element.441, f32[1,1024,128]{2,1,0:T(8,128)S(1)} %get-tuple-element.442, f32[1,1024,128]{2,1,0:T(8,128)S(1)} %get-tuple-element.443, f32[3,1024]{1,0:T(4,128)S(1)} %get-tuple-element.444, ...), kind=kLoop, calls=%fused_computation.55.clone.1 | loop fusion | flops 6553216 | bytes 4742656 | tf_op jit(solution)/shard_map/while/body/eval_jaxpr/reduce_sum | solution.py:94
  56.8 1.0 multiply_add_fusion.11
  58.1 1.2 fusion.70
  59.8 1.7 %fusion.71 = (f32[1024,128]{1,0:T(8,128)S(1)}, f32[3,128]{1,0:T(4,128)S(1)}) fusion(f32[1,1024,128]{2,1,0:T(8,128)S(1)} %get-tuple-element.441, f32[1,1024,128]{2,1,0:T(8,128)S(1)} %get-tuple-element.442, f32[1,1024,128]{2,1,0:T(8,128)S(1)} %get-tuple-element.443, f32[3,1024]{1,0:T(4,128)S(1)} %get-tuple-element.444, ...), kind=kLoop, calls=%fused_computation.55.clone.1 | loop fusion | flops 6553216 | bytes 4742656 | tf_op jit(solution)/shard_map/while/body/eval_jaxpr/reduce_sum | solution.py:94
  63.3 1.0 multiply_add_fusion.11
  64.6 1.2 fusion.70
  66.2 1.7 %fusion.71 = (f32[1024,128]{1,0:T(8,128)S(1)}, f32[3,128]{1,0:T(4,128)S(1)}) fusion(f32[1,1024,128]{2,1,0:T(8,128)S(1)} %get-tuple-element.441, f32[1,1024,128]{2,1,0:T(8,128)S(1)} %get-tuple-element.442, f32[1,1024,128]{2,1,0:T(8,128)S(1)} %get-tuple-element.443, f32[3,1024]{1,0:T(4,128)S(1)} %get-tuple-element.444, ...), kind=kLoop, calls=%fused_computation.55.clone.1 | loop fusion | flops 6553216 | bytes 4742656 | tf_op jit(solution)/shard_map/while/body/eval_jaxpr/reduce_sum | solution.py:94
  69.7 1.0 multiply_add_fusion.11
  71.0 1.2 fusion.70
  72.6 1.7 %fusion.71 = (f32[1024,128]{1,0:T(8,128)S(1)}, f32[3,128]{1,0:T(4,128)S(1)}) fusion(f32[1,1024,128]{2,1,0:T(8,128)S(1)} %get-tuple-element.441, f32[1,1024,128]{2,1,0:T(8,128)S(1)} %get-tuple-element.442, f32[1,1024,128]{2,1,0:T(8,128)S(1)} %get-tuple-element.443, f32[3,1024]{1,0:T(4,128)S(1)} %get-tuple-element.444, ...), kind=kLoop, calls=%fused_computation.55.clone.1 | loop fusion | flops 6553216 | bytes 4742656 | tf_op jit(solution)/shard_map/while/body/eval_jaxpr/reduce_sum | solution.py:94
  76.1 1.0 multiply_add_fusion.11
  77.4 1.2 fusion.70
  79.1 1.7 %fusion.71 = (f32[1024,128]{1,0:T(8,128)S(1)}, f32[3,128]{1,0:T(4,128)S(1)}) fusion(f32[1,1024,128]{2,1,0:T(8,128)S(1)} %get-tuple-element.441, f32[1,1024,128]{2,1,0:T(8,128)S(1)} %get-tuple-element.442, f32[1,1024,128]{2,1,0:T(8,128)S(1)} %get-tuple-element.443, f32[3,1024]{1,0:T(4,128)S(1)} %get-tuple-element.444, ...), kind=kLoop, calls=%fused_computation.55.clone.1 | loop fusion | flops 6553216 | bytes 4742656 | tf_op jit(solution)/shard_map/while/body/eval_jaxpr/reduce_sum | solution.py:94
  82.5 1.0 multiply_add_fusion.11
  83.8 1.2 fusion.70
  85.5 1.7 %fusion.71 = (f32[1024,128]{1,0:T(8,128)S(1)}, f32[3,128]{1,0:T(4,128)S(1)}) fusion(f32[1,1024,128]{2,1,0:T(8,128)S(1)} %get-tuple-element.441, f32[1,1024,128]{2,1,0:T(8,128)S(1)} %get-tuple-element.442, f32[1,1024,128]{2,1,0:T(8,128)S(1)} %get-tuple-element.443, f32[3,1024]{1,0:T(4,128)S(1)} %get-tuple-element.444, ...), kind=kLoop, calls=%fused_computation.55.clone.1 | loop fusion | flops 6553216 | bytes 4742656 | tf_op jit(solution)/shard_map/while/body/eval_jaxpr/reduce_sum | solution.py:94
  89.0 1.0 multiply_add_fusion.11
  90.3 1.2 fusion.70
  91.9 1.7 %fusion.71 = (f32[1024,128]{1,0:T(8,128)S(1)}, f32[3,128]{1,0:T(4,128)S(1)}) fusion(f32[1,1024,128]{2,1,0:T(8,128)S(1)} %get-tuple-element.441, f32[1,1024,128]{2,1,0:T(8,128)S(1)} %get-tuple-element.442, f32[1,1024,128]{2,1,0:T(8,128)S(1)} %get-tuple-element.443, f32[3,1024]{1,0:T(4,128)S(1)} %get-tuple-element.444, ...), kind=kLoop, calls=%fused_computation.55.clone.1 | loop fusion | flops 6553216 | bytes 4742656 | tf_op jit(solution)/shard_map/while/body/eval_jaxpr/reduce_sum | solution.py:94
  95.4 1.0 multiply_add_fusion.11
  96.7 1.2 fusion.70
  98.4 1.7 %fusion.71 = (f32[1024,128]{1,0:T(8,128)S(1)}, f32[3,128]{1,0:T(4,128)S(1)}) fusion(f32[1,1024,128]{2,1,0:T(8,128)S(1)} %get-tuple-element.441, f32[1,1024,128]{2,1,0:T(8,128)S(1)} %get-tuple-element.442, f32[1,1024,128]{2,1,0:T(8,128)S(1)} %get-tuple-element.443, f32[3,1024]{1,0:T(4,128)S(1)} %get-tuple-element.444, ...), kind=kLoop, calls=%fused_computation.55.clone.1 | loop fusion | flops 6553216 | bytes 4742656 | tf_op jit(solution)/shard_map/while/body/eval_jaxpr/reduce_sum | solution.py:94
  101.3 39.7 %pmin.7 = f32[]{:T(128)} all-reduce(f32[]{:T(128)} %fusion.52), channel_id=1, replica_groups=mesh['slab'=4,'dom'=8] {'slab','dom'}, use_global_device_ids=true, to_apply=%region_21.22 | all-reduce | flops 1 | bytes 8 | tf_op jit(solution)/shard_map/pmin | solution.py:174
  141.0 1.3 fusion.53
  (292 shorter events, 33.3 us)
Async XLA Ops:
  3.7 16.2 %collective-permute-start.3 = (f32[1,4,8,128]{3,2,1,0:T(8,128)S(1)}, f32[1,4,8,128]{3,2,1,0:T(8,128)S(1)}, u32[]{:S(2)}, u32[]{:S(2)}) collective-permute-start(f32[1,4,8,128]{3,2,1,0:T(8,128)S(1)} %get-tuple-element.246), channel_id=1, source_target_pairs={{1,0},{2,1},{3,2},{4,3},{5,4},{6,5},{7,6},{9,8},{10,9},{11,10},{12... | collective-permute-start | bytes 49160 | tf_op jit(solution)/shard_map/ppermute | solution.py:23
  5.0 14.8 %collective-permute-start.2 = (f32[1,4,8,128]{3,2,1,0:T(8,128)S(1)}, f32[1,4,8,128]{3,2,1,0:T(8,128)S(1)}, u32[]{:S(2)}, u32[]{:S(2)}) collective-permute-start(f32[1,4,8,128]{3,2,1,0:T(8,128)S(1)} %get-tuple-element.247), channel_id=1, source_target_pairs={{0,1},{1,2},{2,3},{3,4},{4,5},{5,6},{6,7},{8,9},{9,10},{10,11},{11... | collective-permute-start | bytes 49160 | tf_op jit(solution)/shard_map/ppermute | solution.py:22
  8.1 11.8 %collective-permute-start.1 = (f32[1,4,8,128]{3,2,1,0:T(8,128)S(1)}, f32[1,4,8,128]{3,2,1,0:T(8,128)S(1)}, u32[]{:S(2)}, u32[]{:S(2)}) collective-permute-start(f32[1,4,8,128]{3,2,1,0:T(8,128)S(1)} %get-tuple-element.248), channel_id=1, source_target_pairs={{8,0},{16,8},{24,16},{9,1},{17,9},{25,17},{10,2},{18,10},{26,18},{... | collective-permute-start | bytes 49160 | tf_op jit(solution)/shard_map/ppermute | solution.py:23
  9.4 10.5 %collective-permute-start = (f32[1,4,8,128]{3,2,1,0:T(8,128)S(1)}, f32[1,4,8,128]{3,2,1,0:T(8,128)S(1)}, u32[]{:S(2)}, u32[]{:S(2)}) collective-permute-start(f32[1,4,8,128]{3,2,1,0:T(8,128)S(1)} %get-tuple-element.249), channel_id=1, source_target_pairs={{0,8},{8,16},{16,24},{1,9},{9,17},{17,25},{2,10},{10,18},{18,26},{... | collective-permute-start | bytes 49160 | tf_op jit(solution)/shard_map/ppermute | solution.py:22
  20.8 11.3 %copy-start.2 = (f32[1024]{0:T(1024)S(1)}, f32[1024]{0:T(1024)}, u32[]{:S(2)}) copy-start(f32[1024]{0:T(1024)} %param.16) | copy-start | bytes 12292
  32.1 16.6 %copy-start.1 = (f32[8,128]{1,0:T(8,128)}, f32[8,128]{1,0:T(8,128)S(1)}, u32[]{:S(2)}) copy-start(f32[8,128]{1,0:T(8,128)S(1)} %get-tuple-element.112) | copy-start | bytes 12292
  32.5 10.6 %collective-permute-start.4 = (f32[1,13,8,128]{3,2,1,0:T(8,128)S(1)}, f32[1,13,8,128]{3,2,1,0:T(8,128)S(1)}, u32[]{:S(2)}, u32[]{:S(2)}) collective-permute-start(f32[1,13,8,128]{3,2,1,0:T(8,128)S(1)} %get-tuple-element.245), channel_id=1, source_target_pairs={{0,8},{8,16},{16,24},{1,9},{9,17},{17,25},{2,10},{10,18},{18,26},{... | collective-permute-start | bytes 159752 | tf_op jit(solution)/shard_map/ppermute | solution.py:22
  37.4 10.4 %collective-permute-start.7 = (f32[1,13,8,128]{3,2,1,0:T(8,128)S(1)}, f32[1,13,8,128]{3,2,1,0:T(8,128)S(1)}, u32[]{:S(2)}, u32[]{:S(2)}) collective-permute-start(f32[1,13,8,128]{3,2,1,0:T(8,128)S(1)} %get-tuple-element.242), channel_id=1, source_target_pairs={{1,0},{2,1},{3,2},{4,3},{5,4},{6,5},{7,6},{9,8},{10,9},{11,10},{12... | collective-permute-start | bytes 159752 | tf_op jit(solution)/shard_map/ppermute | solution.py:23
  38.7 9.1 %collective-permute-start.6 = (f32[1,13,8,128]{3,2,1,0:T(8,128)S(1)}, f32[1,13,8,128]{3,2,1,0:T(8,128)S(1)}, u32[]{:S(2)}, u32[]{:S(2)}) collective-permute-start(f32[1,13,8,128]{3,2,1,0:T(8,128)S(1)} %get-tuple-element.243), channel_id=1, source_target_pairs={{0,1},{1,2},{2,3},{3,4},{4,5},{5,6},{6,7},{8,9},{9,10},{10,11},{11... | collective-permute-start | bytes 159752 | tf_op jit(solution)/shard_map/ppermute | solution.py:22
  41.8 6.0 %collective-permute-start.5 = (f32[1,13,8,128]{3,2,1,0:T(8,128)S(1)}, f32[1,13,8,128]{3,2,1,0:T(8,128)S(1)}, u32[]{:S(2)}, u32[]{:S(2)}) collective-permute-start(f32[1,13,8,128]{3,2,1,0:T(8,128)S(1)} %get-tuple-element.244), channel_id=1, source_target_pairs={{8,0},{16,8},{24,16},{9,1},{17,9},{25,17},{10,2},{18,10},{26,18},{... | collective-permute-start | bytes 159752 | tf_op jit(solution)/shard_map/ppermute | solution.py:23
  49.2 51.5 %copy-start = (f32[1024]{0:T(1024)S(1)}, f32[1024]{0:T(1024)}, u32[]{:S(2)}) copy-start(f32[1024]{0:T(1024)} %param.15) | copy-start | bytes 12292
  100.7 41.7 %copy-start.3 = (f32[8,128]{1,0:T(8,128)}, f32[8,128]{1,0:T(8,128)S(1)}, u32[]{:S(2)}) copy-start(f32[8,128]{1,0:T(8,128)S(1)} %get-tuple-element.115) | copy-start | bytes 12292
  100.7 41.7 %copy-start.4 = (f32[8,3,128]{2,1,0:T(4,128)}, f32[8,3,128]{2,1,0:T(4,128)S(1)}, u32[]{:S(2)}) copy-start(f32[8,3,128]{2,1,0:T(4,128)S(1)} %get-tuple-element.114) | copy-start | bytes 36868
where the time goes:
time: 143 us; the launch traced here: 142 us
  other arithmetic  64.6 us (45%)
  blocking collectives  39.7 us (28%)
  starting transfers between devices  21.5 us (15%)
  local copies, waits for them, and re-layouts  7.66 us (5%)
  waiting for transfers between devices  4.72 us (3%)
  loops' own time  1.8 us (1%)
    pmin x1, blocking collectives, body(): step = lax.pmin(jnp.min(allowed), ('slab', 'dom'))  39.7 us
    ppermute x4, starting transfers between devices, padded(): before = lax.ppermute(last, axis, up)  16.4 us
    reduce_sum x8, other arithmetic, block_momentum(): jnp.sum(rel_vel * grad_sum, axis=0)  13.5 us
    add x16, other arithmetic, apply_matrix(): matrix[0] * vector[0] + matrix[3] * vector[1] + matrix[4] * vector[2]  10.3 us
    reduce_sum x8, other arithmetic, block_momentum(): jnp.sum(rel_vel * grad_own, axis=0)  9.27 us
    ppermute x4, starting transfers between devices, padded(): after = lax.ppermute(first, axis, down)  5.16 us
    reduce_sum x8, other arithmetic, block_density(): jnp.sum(weight * separation[first] * separation[second], axis=0) / dens  5.08 us
    ppermute x4, waiting for transfers between devices, padded(): after = lax.ppermute(first, axis, down)  4.71 us
  transfers between devices with their start and end apart: 8, of which 1 were waited for; matrix products, arithmetic and copies ran while one was open for 4% of the time, Pallas kernels for 0%

commit v1 on v0

v1 whole, which is shorter than its diff:
```python
import functools
import math

import jax
import jax.numpy as jnp
from jax import lax
from jax.experimental import pallas as pl
from jax.experimental.pallas import tpu as pltpu
from jax.sharding import PartitionSpec as P

gas_gamma = 5.0 / 3.0
courant = 0.4
f32 = jnp.float32
bf16 = jnp.bfloat16
rows = 8
lanes = 128
tiny = 1e-12
swaps = (("dom", 0, 2), ("slab", 0, 0), ("dom", 1, 2), ("slab", 1, 0))
vmem_spec = pl.BlockSpec(memory_space=pltpu.VMEM)
smem_spec = pl.BlockSpec(memory_space=pltpu.SMEM)


def partner(axis, odd, base):
    place = lax.axis_index(axis)
    size = lax.axis_size(axis)
    upward = lax.rem(place + odd, 2) == 0
    direction = base + jnp.where(upward, 1, 0)
    exists = jnp.where(upward, place < size - 1, place > 0)
    return direction, exists


def swap(value, axis, odd):
    size = lax.axis_size(axis)
    pairs = [
        (i, (i + 1) % size if (i - odd) % 2 == 0 else (i - 1) % size) for i in range(size)
    ]
    return lax.ppermute(value, axis, pairs)


def split2(value):
    high = value.astype(bf16)
    low = (value - high.astype(f32)).astype(bf16)
    return high, low


def split3(value):
    first = value.astype(bf16).astype(f32)
    rest = value - first
    second = rest.astype(bf16).astype(f32)
    return first, second, rest - second


def row_ids():
    return lax.broadcasted_iota(jnp.int32, (rows, lanes), 0)


def centre_of(tile):
    corner = jnp.floor(tile[:, 0:1]) + 0.5
    return jnp.where(row_ids() < 3, jnp.broadcast_to(corner, tile.shape), 0.0)


def sum_xyz(tile, start):
    return tile[start : start + 1] + tile[start + 1 : start + 2] + tile[start + 2 : start + 3]


def placed(tile, at, row):
    return jnp.where(row_ids() == at, jnp.broadcast_to(row, tile.shape), tile)


def near_operand(tile):
    norm = sum_xyz(tile * tile, 0)
    drift = (
        tile[0:1] * tile[4:5] + tile[1:2] * tile[5:6] + tile[2:3] * tile[6:7]
    )
    first, second, third = split3(placed(placed(tile, 3, norm), 7, drift))
    ones = jnp.where(row_ids() < 3, 1.0, 0.0)
    stacked = [first, second, third, first, second, first, ones, jnp.zeros_like(ones)]
    return jnp.concatenate(stacked, axis=0).astype(bf16)


def own_operand(tile, own_term):
    first, second, third = split3(tile)
    parts = split3(own_term)
    ones = jnp.zeros((rows, lanes), f32)
    for at in range(3):
        ones = placed(ones, at, parts[at])
    stacked = [first, first, first, second, second, third, ones, jnp.zeros_like(ones)]
    return jnp.concatenate(stacked, axis=0).T.astype(bf16)


def own_distance(tile, scale):
    norm = sum_xyz(tile * tile, 0)
    ids = row_ids()
    left = jnp.where(ids < 3, -2.0 * tile, jnp.where(ids == 3, 1.0, 0.0))
    if scale is None:
        return own_operand(left, norm)
    return own_operand(left * scale, norm * scale)


def own_closing(tile, scale):
    drift = (
        tile[0:1] * tile[4:5] + tile[1:2] * tile[5:6] + tile[2:3] * tile[6:7]
    )
    ids = row_ids()
    left = jnp.concatenate([-tile[4:8], -tile[0:4]], axis=0)
    left = jnp.where(ids == 3, 0.0, jnp.where(ids == 7, 1.0, left))
    return own_operand(left * scale, drift * scale)


def fill_table(own, received, table, width):
    table[0 : 8 * width, :] = own[0 : 8 * width, :]
    for message, (axis, odd, base) in zip(received, swaps):
        direction, _ = partner(axis, odd, base)
        start = pl.multiple_of((direction + 1) * (8 * width), 8 * width)
        table[pl.ds(start, 8 * width), :] = message[0 : 8 * width, :]
    table[40 * width : 40 * width + 8, :] = jnp.zeros((8, lanes), f32)


def fill_mass(own, received, masses):
    masses[0:8, :] = own[64:72, :]
    for message, (axis, odd, base) in zip(received, swaps):
        direction, _ = partner(axis, odd, base)
        start = pl.multiple_of((direction + 1) * 8, 8)
        masses[pl.ds(start, 8), :] = message[64:72, :]
    masses[40:48, :] = jnp.zeros((8, lanes), f32)


def tile_at(table, entry):
    return table[pl.ds(pl.multiple_of(entry * rows, rows), rows), :]


def cut_windows(offsets, counts, source, outgoing, masses):
    for target, (axis, odd, base) in zip(outgoing, swaps):
        direction, exists = partner(axis, odd, base)
        offset = offsets[direction, 0]
        count = jnp.where(exists, counts[direction, 0], 0)
        for slot in range(8):
            block = jnp.minimum(offset + slot, 7)
            keep = slot < count
            tile = tile_at(source, block)
            target[slot * rows : (slot + 1) * rows, :] = jnp.where(keep, tile, 0.0)
            if masses:
                row = source[pl.ds(64 + block, 1), :]
                target[64 + slot : 65 + slot, :] = jnp.where(keep, row, 0.0)


def pack_kernel(positions, velocities, mass, smoothing, energy, offsets, counts, own, *outgoing):
    sound = jnp.sqrt(gas_gamma * (gas_gamma - 1.0) * energy[...])
    for block in range(8):
        part = slice(block * lanes, (block + 1) * lanes)
        at = block * rows
        own[at : at + 3, :] = positions[:, part]
        own[at + 3 : at + 4, :] = smoothing[block : block + 1, :]
        own[at + 4 : at + 7, :] = velocities[:, part]
        own[at + 7 : at + 8, :] = sound[block : block + 1, :]
    own[64:72, :] = mass[...]
    cut_windows(offsets, counts, own, outgoing, True)


def signal_kernel(pairs, own, m0, m1, m2, m3, allowed, smallest, table, near, dots, best):
    fill_table(own, (m0, m1, m2, m3), table, rows)

    def block_step(block, _):
        own_tile = tile_at(table, block)
        centre = centre_of(own_tile)
        centred = own_tile - centre
        left = jnp.concatenate([own_distance(centred, None), own_closing(centred, 30.0)], axis=0)
        columns = own_tile.T
        len_own = jnp.broadcast_to(columns[:, 3:4] * 0.05, (lanes, lanes))
        sound_own = jnp.broadcast_to(columns[:, 7:8], (lanes, lanes))
        for k in range(8):
            tile = tile_at(table, pairs[k, block]) - centre
            near[:, k * lanes : (k + 1) * lanes] = near_operand(tile)
        dots[...] = jnp.dot(left, near[...], preferred_element_type=f32)
        for k in range(8):
            tile = tile_at(table, pairs[k, block])
            part = slice(k * lanes, (k + 1) * lanes)
            mean_len = len_own + tile[3:4] * 0.05
            closing = jnp.minimum(dots[lanes:, part], 0.0)
            rate = closing * mean_len / (dots[0:lanes, part] + mean_len * mean_len)
            signal = sound_own + tile[7:8] - rate
            best[...] = signal if k == 0 else jnp.maximum(best[...], signal)
        top = jnp.max(best[...].T, axis=0, keepdims=True)
        allowed[pl.ds(block, 1), :] = courant * own_tile[3:4] / top
        return 0

    lax.fori_loop(0, 8, block_step, 0)
    least = jnp.min(allowed[...], axis=(0, 1), keepdims=True)
    smallest[...] = jnp.broadcast_to(least, (rows, lanes))


def density_kernel(
    pairs, offsets, counts, energy, own, m0, m1, m2, m3, density, second, *rest
):
    outgoing = rest[0:4]
    table, masses, near, feats, dots, weights, sums = rest[4:]
    fill_table(own, (m0, m1, m2, m3), table, rows)
    fill_mass(own, (m0, m1, m2, m3), masses)

    def block_step(block, _):
        own_tile = tile_at(table, block)
        centre = centre_of(own_tile)
        centred = own_tile - centre
        scale = 0.25 / (own_tile[3:4] * own_tile[3:4])
        left = own_distance(centred, scale)
        ids = row_ids()
        for k in range(8):
            entry = pairs[k, block]
            part = slice(k * lanes, (k + 1) * lanes)
            tile = tile_at(table, entry) - centre
            near[:, part] = near_operand(tile)
            weighed = jnp.where(ids == 3, 1.0, tile) * masses[pl.ds(entry, 1), :]
            stacked = jnp.concatenate(
                [weighed, weighed * tile[0:1], weighed * tile[1:2], weighed * tile[2:3]], axis=0
            )
            high, low = split2(stacked)
            feats[0:32, part] = high
            feats[32:64, part] = low
        dots[...] = jnp.dot(left, near[...], preferred_element_type=f32)
        for k in range(8):
            part = slice(k * lanes, (k + 1) * lanes)
            dist_sq = jnp.maximum(dots[:, part], tiny)
            ratio = dist_sq * lax.rsqrt(dist_sq)
            wide = jnp.maximum(1.0 - ratio, 0.0)
            narrow = jnp.maximum(0.5 - ratio, 0.0)
            twice = narrow + narrow
            high, low = split2(wide * wide * wide - twice * twice * narrow)
            weights[0:lanes, part] = high
            weights[lanes:, part] = low
        out = lax.dot_general(
            weights[...], feats[...], (((1,), (1,)), ((), ())), preferred_element_type=f32
        )
        out = (out[0:lanes] + out[lanes:]).T
        sums[pl.ds(pl.multiple_of(block * 32, 32), 32), :] = out[0:32] + out[32:64]
        return 0

    lax.fori_loop(0, 8, block_step, 0)

    def total(field):
        return sums[pl.ds(field, 8, stride=32), :]

    def mine(field):
        return own[pl.ds(field, 8, stride=rows), :]

    length = mine(3)
    place = [mine(a) for a in range(3)]
    place = [value - (jnp.floor(value[:, 0:1]) + 0.5) for value in place]
    whole = total(3)
    dens = whole * (2.0 / math.pi) / (length * length * length)
    first = [total(a) for a in range(3)]
    inverse = 1.0 / whole
    floor = 0.05 * length * length

    def moment(a, b):
        raw = total(8 + 8 * a + b) - place[a] * first[b] - place[b] * first[a]
        return (raw + place[a] * place[b] * whole) * inverse

    axx = moment(0, 0) + floor
    ayy = moment(1, 1) + floor
    azz = moment(2, 2) + floor
    axy, axz, ayz = moment(0, 1), moment(0, 2), moment(1, 2)
    cof_xx = ayy * azz - ayz * ayz
    cof_yy = axx * azz - axz * axz
    cof_zz = axx * ayy - axy * axy
    cof_xy = axz * ayz - axy * azz
    cof_xz = axy * ayz - ayy * axz
    cof_yz = axy * axz - axx * ayz
    inv_det = 1.0 / (axx * cof_xx + axy * cof_xy + axz * cof_xz)
    density[...] = dens
    pressure = (gas_gamma - 1.0) * energy[...] / dens
    fields = [dens, pressure, cof_xx * inv_det, cof_yy * inv_det, cof_zz * inv_det]
    fields += [cof_xy * inv_det, cof_xz * inv_det, cof_yz * inv_det]
    for field in range(8):
        for block in range(8):
            at = block * rows + field
            second[at : at + 1, :] = fields[field][block : block + 1, :]
    cut_windows(offsets, counts, second, outgoing, False)


def momentum_kernel(pairs, own, m0, m1, m2, m3, second, s0, s1, s2, s3, accel, heating, *scratch):
    table, masses, table2, near, feats, dots, weights, sums = scratch
    fill_table(own, (m0, m1, m2, m3), table, rows)
    fill_mass(own, (m0, m1, m2, m3), masses)
    fill_table(second, (s0, s1, s2, s3), table2, rows)
    ids = row_ids()

    def features(tile, extra, mass):
        cols = [
            jnp.concatenate([extra[i : i + 1] for i in picked], axis=0)
            for picked in ((2, 5, 6, 2, 2, 5, 6, 2), (5, 3, 7, 3, 5, 3, 7, 3), (6, 7, 4, 4, 6, 7, 4, 4))
        ]
        heavy = tile * mass
        applied = None
        for axis in range(3):
            operand = jnp.where(ids < 4, tile[axis : axis + 1], tile[4 + axis : 5 + axis])
            term = cols[axis] * operand
            applied = term if applied is None else applied + term
        swirl = (
            applied[0:1] * tile[4:5] + applied[1:2] * tile[5:6] + applied[2:3] * tile[6:7]
        )
        applied = placed(applied, 3, swirl)
        press = extra[1:2] * mass
        parts = [jnp.where(ids == 3, mass, heavy)]
        parts += [heavy * tile[4 + axis : 5 + axis] for axis in range(3)]
        parts += [extra * mass, extra * press, applied * mass, applied * press]
        return jnp.concatenate(parts, axis=0)

    def block_step(block, _):
        own_tile = tile_at(table, block)
        centre = centre_of(own_tile)
        centred = own_tile - centre
        left = jnp.concatenate([own_distance(centred, None), own_closing(centred, 40.0)], axis=0)
        columns = own_tile.T
        columns2 = tile_at(table2, block).T
        len_own = jnp.broadcast_to(columns[:, 3:4] * 0.05, (lanes, lanes))
        sound_own = jnp.broadcast_to(columns[:, 7:8], (lanes, lanes))
        dens_own = jnp.broadcast_to(columns2[:, 0:1], (lanes, lanes))
        for k in range(8):
            entry = pairs[k, block]
            part = slice(k * lanes, (k + 1) * lanes)
            tile = tile_at(table, entry) - centre
            near[:, part] = near_operand(tile)
            high, low = split2(
                features(tile, tile_at(table2, entry), masses[pl.ds(entry, 1), :])
            )
            feats[0:64, part] = high
            feats[64:128, part] = low
        dots[...] = jnp.dot(left, near[...], preferred_element_type=f32)
        for k in range(8):
            entry = pairs[k, block]
            part = slice(k * lanes, (k + 1) * lanes)
            tile = tile_at(table, entry)
            extra = tile_at(table2, entry)
            len_row = tile[3:4] * 0.05
            for start in range(0, lanes, 32):
                chunk = slice(start, start + 32)
                dist_sq = jnp.maximum(dots[chunk, part], tiny)
                dist = dist_sq * lax.rsqrt(dist_sq)
                mean_len = len_own[chunk] + len_row
                inv_len = 1.0 / mean_len
                ratio = dist * inv_len
                wide = jnp.maximum(20.0 - ratio, 0.0) * inv_len
                narrow = jnp.maximum(10.0 - ratio, 0.0) * inv_len
                twice = narrow + narrow
                weight = wide * wide * wide - twice * twice * narrow
                closing = jnp.minimum(dots[lanes + start : lanes + start + 32, part], 0.0)
                rate = closing * mean_len / (dist_sq + mean_len * mean_len)
                viscous = rate * (rate - (sound_own[chunk] + tile[7:8]))
                viscous = viscous / (dens_own[chunk] + extra[0:1])
                high, low = split2(weight)
                weights[start : start + 32, part] = high
                weights[lanes + start : lanes + start + 32, part] = low
                high, low = split2(weight * viscous)
                weights[2 * lanes + start : 2 * lanes + start + 32, part] = high
                weights[3 * lanes + start : 3 * lanes + start + 32, part] = low
        out = lax.dot_general(
            weights[...], feats[...], (((1,), (1,)), ((), ())), preferred_element_type=f32
        )
        plain = (out[0:lanes] + out[lanes : 2 * lanes]).T
        damped = (out[2 * lanes : 3 * lanes] + out[3 * lanes :]).T
        at = pl.multiple_of(block * lanes, lanes)
        sums[pl.ds(at, 64), :] = plain[0:64] + plain[64:]
        sums[pl.ds(at + 64, 64), :] = damped[0:64] + damped[64:]
        return 0

    lax.fori_loop(0, 8, block_step, 0)

    def mine(ref, field):
        return ref[pl.ds(field, 8, stride=rows), :]

    place = [mine(own, a) for a in range(3)]
    place = [value - (jnp.floor(value[:, 0:1]) + 0.5) for value in place]
    speed = [mine(own, 4 + a) for a in range(3)]
    pressure = mine(second, 1)
    order = ((2, 5, 6), (5, 3, 7), (6, 7, 4))
    matrix = [[mine(second, order[a][b]) for b in range(3)] for a in range(3)]

    def pieces(base):
        def total(field):
            return sums[pl.ds(base + field, 8, stride=lanes), :]

        mass = total(3)
        offset = [total(a) - place[a] * mass for a in range(3)]
        mass_v = [total(4 + a) for a in range(3)]
        applied = [
            matrix[a][0] * offset[0] + matrix[a][1] * offset[1] + matrix[a][2] * offset[2]
            for a in range(3)
        ]
        work = None
        for a in range(3):
            for b in range(3):
                cross = speed[a] * offset[b] - total(8 + 8 * a + b) + mass_v[a] * place[b]
                term = matrix[a][b] * cross
                work = term if work is None else work + term
        return total, applied, work

    def near_force(total, matrices, vectors):
        return [
            total(vectors + a)
            - total(matrices + order[a][0]) * place[0]
            - total(matrices + order[a][1]) * place[1]
            - total(matrices + order[a][2]) * place[2]
            for a in range(3)
        ]

    norm = 16.0 / math.pi / 20.0**6
    total, applied, work = pieces(0)
    pushed = near_force(total, 40, 56)
    total2, applied2, work2 = pieces(64)
    pushed2 = near_force(total2, 32, 48)
    for a in range(3):
        value = -norm * (
            pressure * applied[a] + pushed[a] + 0.125 * (applied2[a] + pushed2[a])
        )
        for block in range(8):
            part = slice(block * lanes, (block + 1) * lanes)
            accel[a : a + 1, part] = value[block : block + 1, :]
    near_work = (
        speed[0] * pushed2[0]
        + speed[1] * pushed2[1]
        + speed[2] * pushed2[2]
        - total2(51)
        + place[0] * total2(52)
        + place[1] * total2(53)
        + place[2] * total2(54)
    )
    heating[...] = norm * (pressure * work + 0.0625 * (work2 + near_work))


def call(kernel, outs, scratch, smem, args, flops):
    return pl.pallas_call(
        kernel,
        out_shape=[jax.ShapeDtypeStruct(shape, f32) for shape in outs],
        in_specs=[smem_spec] * smem + [vmem_spec] * (len(args) - smem),
        out_specs=[vmem_spec] * len(outs),
        scratch_shapes=[pltpu.VMEM(shape, kind) for shape, kind in scratch],
        compiler_params=pltpu.CompilerParams(vmem_limit_bytes=24 * 1024 * 1024),
        cost_estimate=pl.CostEstimate(flops=flops, bytes_accessed=200000, transcendentals=0),
    )(*args)


def body(positions, velocities, mass, smoothing, energy, send_offsets, send_counts, pair_blocks):
    points = positions.shape[1]
    packed = (72, lanes)
    energy = energy.reshape(8, lanes)
    own, *outgoing = pl.pallas_call(
        pack_kernel,
        out_shape=[jax.ShapeDtypeStruct(packed, f32)] * 5,
        in_specs=[vmem_spec] * 5 + [smem_spec] * 2,
        out_specs=[vmem_spec] * 5,
    )(
        positions,
        velocities,
        mass.reshape(8, lanes),
        smoothing.reshape(8, lanes),
        energy,
        send_offsets,
        send_counts,
    )
    received = [swap(value, axis, odd) for value, (axis, odd, _) in zip(outgoing, swaps)]
    table = ((328, lanes), f32)
    masses = ((48, lanes), f32)
    near = ((64, 8 * lanes), bf16)
    allowed, smallest = call(
        signal_kernel,
        [(8, lanes), (rows, lanes)],
        [table, near, ((2 * lanes, 8 * lanes), f32), ((lanes, lanes), f32)],
        1,
        (pair_blocks, own, *received),
        4 * 10**9,
    )
    density, second, *outgoing2 = call(
        density_kernel,
        [(8, lanes), (64, lanes)] + [(64, lanes)] * 4,
        [
            table,
            masses,
            near,
            ((64, 8 * lanes), bf16),
            ((lanes, 8 * lanes), f32),
            ((2 * lanes, 8 * lanes), bf16),
            ((8 * 32, lanes), f32),
        ],
        3,
        (pair_blocks, send_offsets, send_counts, energy, own, *received),
        4 * 10**9,
    )
    received2 = [swap(value, axis, odd) for value, (axis, odd, _) in zip(outgoing2, swaps)]
    accel, heating = call(
        momentum_kernel,
        [(3, points), (8, lanes)],
        [
            table,
            masses,
            table,
            near,
            ((lanes, 8 * lanes), bf16),
            ((2 * lanes, 8 * lanes), f32),
            ((4 * lanes, 8 * lanes), bf16),
            ((8 * lanes, lanes), f32),
        ],
        1,
        (pair_blocks, own, *received, second, *received2),
        8 * 10**9,
    )
    for axis in ("dom", "slab"):
        size = lax.axis_size(axis)
        step = 1
        while step < size:
            moved = lax.ppermute(smallest, axis, [(i, i ^ step) for i in range(size)])
            smallest = jnp.minimum(smallest, moved)
            step *= 2
    share = smallest / allowed
    return (density.reshape(points), accel, heating.reshape(points), share.reshape(points))


def solution(mesh):
    both = ("slab", "dom")
    wide, flat = P(None, both), P(both)
    in_specs = (wide, wide, flat, flat, flat, wide, wide, wide)
    out_specs = (flat, wide, flat, flat)
    return jax.shard_map(body, mesh=mesh, in_specs=in_specs, out_specs=out_specs, check_vma=False)
```

time: 143 us -> 64.9 us (0.45)
  other arithmetic: 64.6 us -> 0.61 us
  blocking collectives: 39.7 us -> 0 us
  Pallas kernels: 0 us -> 29.5 us
  waiting for transfers between devices: 4.72 us -> 18.7 us
  starting transfers between devices: 21.5 us -> 12.4 us
  local copies, waits for them, and re-layouts: 7.66 us -> 2.77 us
  loops' own time: 1.8 us -> 0 us
    pmin x1 -> x0, blocking collectives: 39.7 us -> none  [body(): step = lax.pmin(jnp.min(allowed), ('slab', 'dom'))]
    reduce_sum x40 -> x0, other arithmetic: 35.5 us -> none  [the longest x8 13.5 us: block_momentum(): jnp.sum(rel_vel * grad_sum, axis=0)]
    pallas_call x0 -> x4, Pallas kernels: none -> 29.5 us  [the longest x3 27.9 us: call(): pl.pallas_call(kernel, out_shape=[jax.ShapeDtypeStruct(shape, f32) for sh...]
    ppermute x8 -> x13, waiting for transfers between devices: 4.72 us -> 18.7 us  [the longest x5 12.3 us: body(): moved = lax.ppermute(smallest, axis, [(i, i ^ step) for i in range(size)])]
    add x33 -> x0, other arithmetic: 11.2 us -> none  [the longest x16 10.3 us: apply_matrix(): matrix[0] * vector[0] + matrix[3] * vector[1] + matrix[4] * vector[2]]
    ppermute x8 -> x13, starting transfers between devices: 21.5 us -> 12.4 us  [the longest x8 10.2 us: swap(): return lax.ppermute(value, axis, pairs)]
    div x17 -> x0, other arithmetic: 5.25 us -> none  [the longest x8 3.9 us: kernel(): return shape / (math.pi * length ** 3)]
    reduce_max x8 -> x0, other arithmetic: 3.95 us -> none  [block_momentum(): jnp.max(own_fields[8][None, :] + near_fields[8][:, None] - 3.0 * closing_...]
  transfers between devices with their start and end apart: 8 -> 13, of which waited for: 1 -> 8; matrix products, arithmetic and copies ran while one was open for 4% -> 1% of each run, Pallas kernels for 0% -> 13%
where the time goes in v1:
time: 64.9 us; the launch traced here: 64.6 us
  Pallas kernels  29.5 us (45%)
  waiting for transfers between devices  18.7 us (29%)
  starting transfers between devices  12.4 us (19%)
  local copies, waits for them, and re-layouts  2.77 us (4%)
  between operations  0.69 us (1%)
    pallas_call x3, Pallas kernels, call(): pl.pallas_call(kernel, out_shape=[jax.ShapeDtypeStruct(shape, f32) for sh...  27.9 us
    ppermute x5, waiting for transfers between devices, body(): moved = lax.ppermute(smallest, axis, [(i, i ^ step) for i in range(size)])  12.3 us
    ppermute x8, starting transfers between devices, swap(): return lax.ppermute(value, axis, pairs)  10.2 us
    ppermute x8, waiting for transfers between devices, swap(): return lax.ppermute(value, axis, pairs)  6.38 us
    unnamed x16, local copies, waits for them, and re-layouts  2.77 us
    ppermute x5, starting transfers between devices, body(): moved = lax.ppermute(smallest, axis, [(i, i ^ step) for i in range(size)])  2.2 us
    pallas_call x1, Pallas kernels, body(): pl.pallas_call(pack_kernel, out_shape=[jax.ShapeDtypeStruct(packed, f32)]...  1.6 us
  transfers between devices with their start and end apart: 13, of which 8 were waited for; matrix products, arithmetic and copies ran while one was open for 1% of the time, Pallas kernels for 13%

profile of v1, /device:TPU:0, one launch (start us, length us, event | category | flops | bytes accessed | tf_op | source)
XLA Modules:
  0.0 64.6 jit_solution(6199311430474085032)
XLA Ops:
  0.6 0.0 copy-start.6
  0.6 1.3 %copy.14.offsets = s32[4,1]{1,0:T(4,128)} copy(s32[4,1]{0,1:T(1,128)} %param.13) | data formatting | bytes 32 | tf_op args[5]
  2.0 0.0 copy-done.6
  2.0 0.7 %copy.15.counts = s32[4,1]{1,0:T(4,128)} copy(s32[4,1]{0,1:T(1,128)S(1)} %copy-done.6) | data formatting | bytes 32 | tf_op args[6]
  2.6 1.6 %shard_map.111 = (f32[72,128]{1,0:T(8,128)}, f32[72,128]{1,0:T(8,128)}, f32[72,128]{1,0:T(8,128)}, f32[72,128]{1,0:T(8,128)}, f32[72,128]{1,0:T(8,128)}) custom-call(f32[3,1024]{1,0:T(4,128)} %positions.1, f32[3,1024]{1,0:T(4,128)} %velocities.1, f32[8,128]{1,0:T(8,128)} %bitcast.9, f32[8,128]{1,0:T(8,128)} %bitcast.10, f32[8,128]{1,0:T(8,128)} %bitcast.7, ...), custom_call_target="tpu_custom_call" | custom-call | tf_op jit(solution)/shard_map/pallas_call | solution.py:446
  4.2 0.0 copy-start.5
  4.2 0.5 collective-permute-start
  4.7 2.6 %collective-permute-start.1 = (f32[72,128]{1,0:T(8,128)}, f32[72,128]{1,0:T(8,128)S(1)}, u32[]{:S(2)}, u32[]{:S(2)}) collective-permute-start(f32[72,128]{1,0:T(8,128)} %get-tuple-element.21), channel_id=1, source_target_pairs={{0,8},{8,0},{16,24},{24,16},{1,9},{9,1},{17,25},{25,17},{2,10},{10... | collective-permute-start | bytes 110600 | tf_op jit(solution)/shard_map/ppermute | solution.py:37
  7.3 3.4 %collective-permute-start.2 = (f32[72,128]{1,0:T(8,128)}, f32[72,128]{1,0:T(8,128)S(1)}, u32[]{:S(2)}, u32[]{:S(2)}) collective-permute-start(f32[72,128]{1,0:T(8,128)} %get-tuple-element.22), channel_id=1, source_target_pairs={{0,7},{1,2},{2,1},{3,4},{4,3},{5,6},{6,5},{7,0},{8,15},{9,10},{10,... | collective-permute-start | bytes 110600 | tf_op jit(solution)/shard_map/ppermute | solution.py:37
  10.7 1.5 %collective-permute-start.3 = (f32[72,128]{1,0:T(8,128)}, f32[72,128]{1,0:T(8,128)S(1)}, u32[]{:S(2)}, u32[]{:S(2)}) collective-permute-start(f32[72,128]{1,0:T(8,128)} %get-tuple-element.23), channel_id=1, source_target_pairs={{0,24},{8,16},{16,8},{24,0},{1,25},{9,17},{17,9},{25,1},{2,26},{10... | collective-permute-start | bytes 110600 | tf_op jit(solution)/shard_map/ppermute | solution.py:37
  12.1 0.0 collective-permute-done.m0
  12.2 0.0 collective-permute-done.1.m1
  12.2 0.5 collective-permute-done.2.m2
  12.7 3.0 %collective-permute-done.3.m3 = f32[72,128]{1,0:T(8,128)S(1)} collective-permute-done((f32[72,128]{1,0:T(8,128)}, f32[72,128]{1,0:T(8,128)S(1)}, u32[]{:S(2)}, u32[]{:S(2)}) %collective-permute-start.3) | collective-permute-done | bytes 36896 | tf_op jit(solution)/shard_map/ppermute | solution.py:37
  15.7 0.0 copy-done.5
  15.7 0.0 copy-start.3
  15.7 0.8 %copy-done.3 = f32[72,128]{1,0:T(8,128)S(1)} copy-done((f32[72,128]{1,0:T(8,128)S(1)}, f32[72,128]{1,0:T(8,128)}, u32[]{:S(2)}) %copy-start.3) | copy-done | bytes 36888
  16.5 5.6 %shard_map.114 = (f32[8,128]{1,0:T(8,128)S(1)}, f32[8,128]{1,0:T(8,128)S(1)}) custom-call(s32[8,8]{1,0:T(8,128)S(1)} %copy-done.5, f32[72,128]{1,0:T(8,128)S(1)} %copy-done.3, f32[72,128]{1,0:T(8,128)S(1)} %collective-permute-done.m0, f32[72,128]{1,0:T(8,128)S(1)} %collective-permute-done.1.m1, f32[72,128]{1,0:T(8,128)S(1)} %collective-permute-done.2.m2, ...), custom_call_target="tpu_custom_call" | custom-call | flops 4000000000 | bytes 200000 | tf_op jit(solution)/shard_map/pallas_call | solution.py:431
  22.1 0.0 copy-start.4
  22.1 0.1 collective-permute-start.8
  22.2 1.2 %collective-permute-done.8 = f32[8,128]{1,0:T(8,128)S(1)} collective-permute-done((f32[8,128]{1,0:T(8,128)S(1)}, f32[8,128]{1,0:T(8,128)S(1)}, u32[]{:S(2)}, u32[]{:S(2)}) %collective-permute-start.8) | collective-permute-done | bytes 4128 | tf_op jit(solution)/shard_map/ppermute | solution.py:510
  23.3 0.0 collective-permute-start.9
  23.3 3.6 %collective-permute-done.9 = f32[8,128]{1,0:T(8,128)S(1)} collective-permute-done((f32[8,128]{1,0:T(8,128)S(1)}, f32[8,128]{1,0:T(8,128)S(1)}, u32[]{:S(2)}, u32[]{:S(2)}) %collective-permute-start.9) | collective-permute-done | bytes 4128 | tf_op jit(solution)/shard_map/ppermute | solution.py:510
  26.9 0.0 collective-permute-start.10
  26.9 4.5 %collective-permute-done.10 = f32[8,128]{1,0:T(8,128)S(1)} collective-permute-done((f32[8,128]{1,0:T(8,128)S(1)}, f32[8,128]{1,0:T(8,128)S(1)}, u32[]{:S(2)}, u32[]{:S(2)}) %collective-permute-start.10) | collective-permute-done | bytes 4128 | tf_op jit(solution)/shard_map/ppermute | solution.py:510
  31.4 0.0 copy-start
  31.5 0.0 copy-start.1
  31.5 0.0 copy-start.2
  31.5 0.6 collective-permute-start.11
  32.1 3.1 %collective-permute-done.11 = f32[8,128]{1,0:T(8,128)S(1)} collective-permute-done((f32[8,128]{1,0:T(8,128)S(1)}, f32[8,128]{1,0:T(8,128)S(1)}, u32[]{:S(2)}, u32[]{:S(2)}) %collective-permute-start.11) | collective-permute-done | bytes 4128 | tf_op jit(solution)/shard_map/ppermute | solution.py:510
  35.1 1.5 %collective-permute-start.12 = (f32[8,128]{1,0:T(8,128)S(1)}, f32[8,128]{1,0:T(8,128)S(1)}, u32[]{:S(2)}, u32[]{:S(2)}) collective-permute-start(f32[8,128]{1,0:T(8,128)S(1)} %min.18), channel_id=1, source_target_pairs={{0,16},{8,24},{16,0},{24,8},{1,17},{9,25},{17,1},{25,9},{2,18},{10... | collective-permute-start | bytes 12296 | tf_op jit(solution)/shard_map/ppermute | solution.py:510
  36.7 0.0 copy-done.4
  36.7 0.0 copy-done
  36.7 0.0 copy-done.1
  36.7 0.0 copy-done.2
  36.7 8.6 %shard_map.112 = (f32[8,128]{1,0:T(8,128)}, f32[64,128]{1,0:T(8,128)S(1)}, f32[64,128]{1,0:T(8,128)S(1)}, f32[64,128]{1,0:T(8,128)S(1)}, f32[64,128]{1,0:T(8,128)S(1)}, /*index=5*/f32[64,128]{1,0:T(8,128)S(1)}) custom-call(s32[8,8]{1,0:T(8,128)S(1)} %copy-done.5, s32[4,1]{1,0:T(4,128)S(1)} %copy-done, s32[4,1]{1,0:T(4,128)S(1)} %copy-done.1, ...), custom_call_target="tpu_custom_call" | custom-call | flops 4000000000 | bytes 200000 | tf_op jit(solution)/shard_map/pallas_call | solution.py:431
  45.3 0.0 collective-permute-start.4
  45.3 0.5 collective-permute-start.5
  45.9 0.3 collective-permute-start.6
  46.1 1.4 %collective-permute-start.7 = (f32[64,128]{1,0:T(8,128)S(1)}, f32[64,128]{1,0:T(8,128)S(1)}, u32[]{:S(2)}, u32[]{:S(2)}) collective-permute-start(f32[64,128]{1,0:T(8,128)S(1)} %get-tuple-element.29), channel_id=1, source_target_pairs={{0,24},{8,16},{16,8},{24,0},{1,25},{9,17},{17,9},{25,1},{2,26},{10... | collective-permute-start | bytes 98312 | tf_op jit(solution)/shard_map/ppermute | solution.py:37
  47.6 0.0 collective-permute-done.12
  47.6 0.6 divide_bitcast_fusion
  48.2 0.0 collective-permute-done.4.s0
  48.2 1.3 %collective-permute-done.5.s1 = f32[64,128]{1,0:T(8,128)S(1)} collective-permute-done((f32[64,128]{1,0:T(8,128)S(1)}, f32[64,128]{1,0:T(8,128)S(1)}, u32[]{:S(2)}, u32[]{:S(2)}) %collective-permute-start.5) | collective-permute-done | bytes 32800 | tf_op jit(solution)/shard_map/ppermute | solution.py:37
  49.5 1.5 %collective-permute-done.6.s2 = f32[64,128]{1,0:T(8,128)S(1)} collective-permute-done((f32[64,128]{1,0:T(8,128)S(1)}, f32[64,128]{1,0:T(8,128)S(1)}, u32[]{:S(2)}, u32[]{:S(2)}) %collective-permute-start.6) | collective-permute-done | bytes 32800 | tf_op jit(solution)/shard_map/ppermute | solution.py:37
  51.0 0.0 collective-permute-done.7.s3
  51.0 13.6 %shard_map.113 = (f32[3,1024]{1,0:T(4,128)}, f32[8,128]{1,0:T(8,128)}) custom-call(s32[8,8]{1,0:T(8,128)S(1)} %copy-done.5, f32[72,128]{1,0:T(8,128)S(1)} %copy-done.4, f32[72,128]{1,0:T(8,128)S(1)} %collective-permute-done.m0, f32[72,128]{1,0:T(8,128)S(1)} %collective-permute-done.1.m1, f32[72,128]{1,0:T(8,128)S(1)} %collective-permute-done.2.m2, ...), custom_call_target="tpu_custom_call" | custom-call | flops 8000000000 | bytes 200000 | tf_op jit(solution)/shard_map/pallas_call | solution.py:431
  (4 shorter events, 0.0 us)
Async XLA Ops:
  0.6 1.3 %copy-start.6 = (s32[4,1]{0,1:T(1,128)S(1)}, s32[4,1]{0,1:T(1,128)}, u32[]{:S(2)}) copy-start(s32[4,1]{0,1:T(1,128)} %param.14) | copy-start | bytes 52
  4.2 11.5 %copy-start.5 = (s32[8,8]{1,0:T(8,128)S(1)}, s32[8,8]{1,0:T(8,128)}, u32[]{:S(2)}) copy-start(s32[8,8]{1,0:T(8,128)} %pairs.5) | copy-start | bytes 772
  4.2 7.9 %collective-permute-start = (f32[72,128]{1,0:T(8,128)}, f32[72,128]{1,0:T(8,128)S(1)}, u32[]{:S(2)}, u32[]{:S(2)}) collective-permute-start(f32[72,128]{1,0:T(8,128)} %get-tuple-element.20), channel_id=1, source_target_pairs={{0,1},{1,0},{2,3},{3,2},{4,5},{5,4},{6,7},{7,6},{8,9},{9,8},{10,11... | collective-permute-start | bytes 110600 | tf_op jit(solution)/shard_map/ppermute | solution.py:37
  4.7 7.4 %collective-permute-start.1 = (f32[72,128]{1,0:T(8,128)}, f32[72,128]{1,0:T(8,128)S(1)}, u32[]{:S(2)}, u32[]{:S(2)}) collective-permute-start(f32[72,128]{1,0:T(8,128)} %get-tuple-element.21), channel_id=1, source_target_pairs={{0,8},{8,0},{16,24},{24,16},{1,9},{9,1},{17,25},{25,17},{2,10},{10... | collective-permute-start | bytes 110600 | tf_op jit(solution)/shard_map/ppermute | solution.py:37
  7.3 5.4 %collective-permute-start.2 = (f32[72,128]{1,0:T(8,128)}, f32[72,128]{1,0:T(8,128)S(1)}, u32[]{:S(2)}, u32[]{:S(2)}) collective-permute-start(f32[72,128]{1,0:T(8,128)} %get-tuple-element.22), channel_id=1, source_target_pairs={{0,7},{1,2},{2,1},{3,4},{4,3},{5,6},{6,5},{7,0},{8,15},{9,10},{10,... | collective-permute-start | bytes 110600 | tf_op jit(solution)/shard_map/ppermute | solution.py:37
  10.7 5.1 %collective-permute-start.3 = (f32[72,128]{1,0:T(8,128)}, f32[72,128]{1,0:T(8,128)S(1)}, u32[]{:S(2)}, u32[]{:S(2)}) collective-permute-start(f32[72,128]{1,0:T(8,128)} %get-tuple-element.23), channel_id=1, source_target_pairs={{0,24},{8,16},{16,8},{24,0},{1,25},{9,17},{17,9},{25,1},{2,26},{10... | collective-permute-start | bytes 110600 | tf_op jit(solution)/shard_map/ppermute | solution.py:37
  15.7 0.8 %copy-start.3 = (f32[72,128]{1,0:T(8,128)S(1)}, f32[72,128]{1,0:T(8,128)}, u32[]{:S(2)}) copy-start(f32[72,128]{1,0:T(8,128)} %get-tuple-element.19.own) | copy-start | bytes 110596
  22.1 14.6 %copy-start.4 = (f32[72,128]{1,0:T(8,128)S(1)}, f32[72,128]{1,0:T(8,128)}, u32[]{:S(2)}) copy-start(f32[72,128]{1,0:T(8,128)} %get-tuple-element.19.own) | copy-start | bytes 110596
  22.1 1.2 %collective-permute-start.8 = (f32[8,128]{1,0:T(8,128)S(1)}, f32[8,128]{1,0:T(8,128)S(1)}, u32[]{:S(2)}, u32[]{:S(2)}) collective-permute-start(f32[8,128]{1,0:T(8,128)S(1)} %get-tuple-element.32), channel_id=1, source_target_pairs={{0,1},{1,0},{2,3},{3,2},{4,5},{5,4},{6,7},{7,6},{8,9},{9,8},{10,11... | collective-permute-start | bytes 12296 | tf_op jit(solution)/shard_map/ppermute | solution.py:510
  23.3 3.6 %collective-permute-start.9 = (f32[8,128]{1,0:T(8,128)S(1)}, f32[8,128]{1,0:T(8,128)S(1)}, u32[]{:S(2)}, u32[]{:S(2)}) collective-permute-start(f32[8,128]{1,0:T(8,128)S(1)} %min.15), channel_id=1, source_target_pairs={{0,2},{1,3},{2,0},{3,1},{4,6},{5,7},{6,4},{7,5},{8,10},{9,11},{10,... | collective-permute-start | bytes 12296 | tf_op jit(solution)/shard_map/ppermute | solution.py:510
  26.9 4.5 %collective-permute-start.10 = (f32[8,128]{1,0:T(8,128)S(1)}, f32[8,128]{1,0:T(8,128)S(1)}, u32[]{:S(2)}, u32[]{:S(2)}) collective-permute-start(f32[8,128]{1,0:T(8,128)S(1)} %min.16), channel_id=1, source_target_pairs={{0,4},{1,5},{2,6},{3,7},{4,0},{5,1},{6,2},{7,3},{8,12},{9,13},{10,... | collective-permute-start | bytes 12296 | tf_op jit(solution)/shard_map/ppermute | solution.py:510
  31.4 5.2 %copy-start = (s32[4,1]{1,0:T(4,128)S(1)}, s32[4,1]{1,0:T(4,128)}, u32[]{:S(2)}) copy-start(s32[4,1]{1,0:T(4,128)} %copy.14.offsets) | copy-start | bytes 52
  31.5 5.2 %copy-start.1 = (s32[4,1]{1,0:T(4,128)S(1)}, s32[4,1]{1,0:T(4,128)}, u32[]{:S(2)}) copy-start(s32[4,1]{1,0:T(4,128)} %copy.15.counts) | copy-start | bytes 52
  31.5 5.2 %copy-start.2 = (f32[1024]{0:T(1024)S(1)}, f32[1024]{0:T(1024)}, u32[]{:S(2)}) copy-start(f32[1024]{0:T(1024)} %param.12) | copy-start | bytes 12292
  31.5 3.7 %collective-permute-start.11 = (f32[8,128]{1,0:T(8,128)S(1)}, f32[8,128]{1,0:T(8,128)S(1)}, u32[]{:S(2)}, u32[]{:S(2)}) collective-permute-start(f32[8,128]{1,0:T(8,128)S(1)} %min.17), channel_id=1, source_target_pairs={{0,8},{8,0},{16,24},{24,16},{1,9},{9,1},{17,25},{25,17},{2,10},{10... | collective-permute-start | bytes 12296 | tf_op jit(solution)/shard_map/ppermute | solution.py:510
  35.1 12.5 %collective-permute-start.12 = (f32[8,128]{1,0:T(8,128)S(1)}, f32[8,128]{1,0:T(8,128)S(1)}, u32[]{:S(2)}, u32[]{:S(2)}) collective-permute-start(f32[8,128]{1,0:T(8,128)S(1)} %min.18), channel_id=1, source_target_pairs={{0,16},{8,24},{16,0},{24,8},{1,17},{9,25},{17,1},{25,9},{2,18},{10... | collective-permute-start | bytes 12296 | tf_op jit(solution)/shard_map/ppermute | solution.py:510
  45.3 2.9 %collective-permute-start.4 = (f32[64,128]{1,0:T(8,128)S(1)}, f32[64,128]{1,0:T(8,128)S(1)}, u32[]{:S(2)}, u32[]{:S(2)}) collective-permute-start(f32[64,128]{1,0:T(8,128)S(1)} %get-tuple-element.26), channel_id=1, source_target_pairs={{0,1},{1,0},{2,3},{3,2},{4,5},{5,4},{6,7},{7,6},{8,9},{9,8},{10,11... | collective-permute-start | bytes 98312 | tf_op jit(solution)/shard_map/ppermute | solution.py:37
  45.3 4.2 %collective-permute-start.5 = (f32[64,128]{1,0:T(8,128)S(1)}, f32[64,128]{1,0:T(8,128)S(1)}, u32[]{:S(2)}, u32[]{:S(2)}) collective-permute-start(f32[64,128]{1,0:T(8,128)S(1)} %get-tuple-element.27), channel_id=1, source_target_pairs={{0,8},{8,0},{16,24},{24,16},{1,9},{9,1},{17,25},{25,17},{2,10},{10... | collective-permute-start | bytes 98312 | tf_op jit(solution)/shard_map/ppermute | solution.py:37
  45.9 5.1 %collective-permute-start.6 = (f32[64,128]{1,0:T(8,128)S(1)}, f32[64,128]{1,0:T(8,128)S(1)}, u32[]{:S(2)}, u32[]{:S(2)}) collective-permute-start(f32[64,128]{1,0:T(8,128)S(1)} %get-tuple-element.28), channel_id=1, source_target_pairs={{0,7},{1,2},{2,1},{3,4},{4,3},{5,6},{6,5},{7,0},{8,15},{9,10},{10,... | collective-permute-start | bytes 98312 | tf_op jit(solution)/shard_map/ppermute | solution.py:37
  46.1 4.9 %collective-permute-start.7 = (f32[64,128]{1,0:T(8,128)S(1)}, f32[64,128]{1,0:T(8,128)S(1)}, u32[]{:S(2)}, u32[]{:S(2)}) collective-permute-start(f32[64,128]{1,0:T(8,128)S(1)} %get-tuple-element.29), channel_id=1, source_target_pairs={{0,24},{8,16},{16,8},{24,0},{1,25},{9,17},{17,9},{25,1},{2,26},{10... | collective-permute-start | bytes 98312 | tf_op jit(solution)/shard_map/ppermute | solution.py:37

commit v2 on v1

v2 whole, which is shorter than its diff:
```python
import functools
import math

import jax
import jax.numpy as jnp
from jax import lax
from jax.experimental import pallas as pl
from jax.experimental.pallas import tpu as pltpu
from jax.sharding import PartitionSpec as P

gas_gamma = 5.0 / 3.0
courant = 0.4
f32 = jnp.float32
bf16 = jnp.bfloat16
rows = 8
lanes = 128
tiny = 1e-12
chunk = 32
swaps = (("dom", 0, 2), ("slab", 0, 0), ("dom", 1, 2), ("slab", 1, 0))
vmem_spec = pl.BlockSpec(memory_space=pltpu.VMEM)
smem_spec = pl.BlockSpec(memory_space=pltpu.SMEM)


def partner(axis, odd, base):
    place = lax.axis_index(axis)
    size = lax.axis_size(axis)
    upward = lax.rem(place + odd, 2) == 0
    direction = base + jnp.where(upward, 1, 0)
    exists = jnp.where(upward, place < size - 1, place > 0)
    return direction, exists


def swap(value, axis, odd):
    size = lax.axis_size(axis)
    pairs = [
        (i, (i + 1) % size if (i - odd) % 2 == 0 else (i - 1) % size) for i in range(size)
    ]
    return lax.ppermute(value, axis, pairs)


def split2(value):
    high = value.astype(bf16)
    low = (value - high.astype(f32)).astype(bf16)
    return high, low


def split3(value):
    first = value.astype(bf16).astype(f32)
    rest = value - first
    second = rest.astype(bf16).astype(f32)
    return first, second, rest - second


def row_ids():
    return lax.broadcasted_iota(jnp.int32, (rows, lanes), 0)


def centre_of(tile):
    corner = jnp.floor(tile[:, 0:1]) + 0.5
    return jnp.where(row_ids() < 3, jnp.broadcast_to(corner, tile.shape), 0.0)


def sum_xyz(tile, start):
    return tile[start : start + 1] + tile[start + 1 : start + 2] + tile[start + 2 : start + 3]


def placed(tile, at, row):
    return jnp.where(row_ids() == at, jnp.broadcast_to(row, tile.shape), tile)


def near_operand(tile):
    norm = sum_xyz(tile * tile, 0)
    drift = (
        tile[0:1] * tile[4:5] + tile[1:2] * tile[5:6] + tile[2:3] * tile[6:7]
    )
    first, second, third = split3(placed(placed(tile, 3, norm), 7, drift))
    ones = jnp.where(row_ids() < 3, 1.0, 0.0)
    stacked = [first, second, third, first, second, first, ones, jnp.zeros_like(ones)]
    return jnp.concatenate(stacked, axis=0).astype(bf16)


def own_operand(tile, own_term):
    first, second, third = split3(tile)
    parts = split3(own_term)
    ones = jnp.zeros((rows, lanes), f32)
    for at in range(3):
        ones = placed(ones, at, parts[at])
    stacked = [first, first, first, second, second, third, ones, jnp.zeros_like(ones)]
    return jnp.concatenate(stacked, axis=0)


def own_distance(tile):
    norm = sum_xyz(tile * tile, 0)
    ids = row_ids()
    left = jnp.where(ids < 3, -2.0 * tile, jnp.where(ids == 3, 1.0, 0.0))
    return own_operand(left, norm)


def own_closing(tile, scale):
    drift = (
        tile[0:1] * tile[4:5] + tile[1:2] * tile[5:6] + tile[2:3] * tile[6:7]
    )
    ids = row_ids()
    left = jnp.concatenate([-tile[4:8], -tile[0:4]], axis=0)
    left = jnp.where(ids == 3, 0.0, jnp.where(ids == 7, 1.0, left))
    return own_operand(left * scale, drift * scale)


def fill_table(own, received, table, width):
    table[0 : 8 * width, :] = own[0 : 8 * width, :]
    for message, (axis, odd, base) in zip(received, swaps):
        direction, _ = partner(axis, odd, base)
        start = pl.multiple_of((direction + 1) * (8 * width), 8 * width)
        table[pl.ds(start, 8 * width), :] = message[0 : 8 * width, :]
    table[40 * width : 40 * width + 8, :] = jnp.zeros((8, lanes), f32)


def fill_mass(own, received, masses):
    masses[0:8, :] = own[64:72, :]
    for message, (axis, odd, base) in zip(received, swaps):
        direction, _ = partner(axis, odd, base)
        start = pl.multiple_of((direction + 1) * 8, 8)
        masses[pl.ds(start, 8), :] = message[64:72, :]
    masses[40:48, :] = jnp.zeros((8, lanes), f32)


def tile_at(table, entry):
    return table[pl.ds(pl.multiple_of(entry * rows, rows), rows), :]


def cut_windows(offset_of, count_of, source, outgoing, masses):
    for target, (axis, odd, base) in zip(outgoing, swaps):
        direction, exists = partner(axis, odd, base)
        offset = offset_of(direction)
        count = jnp.where(exists, count_of(direction), 0)
        for slot in range(8):
            block = jnp.minimum(offset + slot, 7)
            keep = slot < count
            tile = tile_at(source, block)
            target[slot * rows : (slot + 1) * rows, :] = jnp.where(keep, tile, 0.0)
            if masses:
                row = source[pl.ds(64 + block, 1), :]
                target[64 + slot : 65 + slot, :] = jnp.where(keep, row, 0.0)


def pack_kernel(positions, velocities, mass, smoothing, energy, offsets, counts, own, *outgoing):
    sound = jnp.sqrt(gas_gamma * (gas_gamma - 1.0) * energy[...])
    for block in range(8):
        part = slice(block * lanes, (block + 1) * lanes)
        at = block * rows
        own[at : at + 3, :] = positions[:, part]
        own[at + 3 : at + 4, :] = smoothing[block : block + 1, :]
        own[at + 4 : at + 7, :] = velocities[:, part]
        own[at + 7 : at + 8, :] = sound[block : block + 1, :]
    own[64:72, :] = mass[...]
    own[72:80, :] = energy[...]
    cut_windows(lambda r: offsets[0, r], lambda r: counts[0, r], own, outgoing, True)


def two_deep(prepare, finish, first=0, last=8):
    prepare(first, 0)

    def step(half, _):
        block = first + half * 2
        prepare(block + 1, 1)
        finish(block, 0)
        prepare(jnp.minimum(block + 2, last - 1), 0)
        finish(block + 1, 1)
        return 0

    lax.fori_loop(0, (last - first) // 2, step, 0)


def own_kernel(own, left, columns, table):
    table[...] = own[...]

    def step(block, _):
        tile = tile_at(own, block)
        centred = tile - centre_of(tile)
        stacked = jnp.concatenate([own_distance(centred), own_closing(centred, 30.0)], axis=0)
        at = pl.ds(pl.multiple_of(block * lanes, lanes), lanes)
        left[at, :] = stacked.T.astype(bf16)
        turned = tile.T
        length = turned[:, 3:4]
        columns[at, 0:lanes] = jnp.broadcast_to(length * 0.05, (lanes, lanes))
        columns[at, lanes : 2 * lanes] = jnp.broadcast_to(turned[:, 7:8] * 0.75, (lanes, lanes))
        columns[at, 2 * lanes :] = jnp.broadcast_to(0.5 / length, (lanes, lanes))
        return 0

    lax.fori_loop(0, 8, step, 0)


def put_near(near, k, tile):
    operand = near_operand(tile)
    at = 2 * k * lanes
    near[0:64, at : at + lanes] = operand
    near[64:128, at + lanes : at + 2 * lanes] = operand


def clear_near(buffers):
    for near in buffers:
        near[...] = jnp.zeros(near.shape, bf16)


def pair_dots(left, near, block, start, k):
    at = pl.ds(pl.multiple_of(block * lanes + start, chunk), chunk)
    part = slice(2 * k * lanes, 2 * (k + 1) * lanes)
    both = jnp.dot(left[at, :], near[:, part], preferred_element_type=f32)
    return both[:, 0:lanes], both[:, lanes:]


def signal_kernel(
    plan, left, columns, own, m0, m1, m2, m3, allowed, smallest, distance, rates, table, *near
):
    clear_near(near)
    fill_table(own, (m0, m1, m2, m3), table, rows)

    def prepare(block, buf):
        centre = centre_of(tile_at(table, block))
        for k in range(8):
            put_near(near[buf], k, tile_at(table, plan[k, block]) - centre)

    def finish(block, buf):
        tops = [None] * (lanes // chunk)
        sounds = None
        for k in range(8):
            tile = tile_at(table, plan[k, block])
            len_row, sound_row = tile[3:4] * 0.05, tile[7:8]
            sounds = sound_row if k == 0 else jnp.maximum(sounds, sound_row)
            part = slice(k * lanes, (k + 1) * lanes)
            for c in range(lanes // chunk):
                start = c * chunk
                at = pl.ds(pl.multiple_of(block * lanes + start, chunk), chunk)
                dist_sq, closing = pair_dots(left, near[buf], block, start, k)
                dist_sq = jnp.maximum(dist_sq, tiny)
                distance[at, part] = dist_sq * lax.rsqrt(dist_sq)
                mean_len = columns[at, 0:lanes] + len_row
                rate = closing * mean_len / (dist_sq + mean_len * mean_len)
                rates[at, part] = rate
                signal = sound_row - rate
                tops[c] = signal if k == 0 else jnp.maximum(tops[c], signal)
        top = jnp.max(jnp.concatenate(tops, axis=0).T, axis=0, keepdims=True)
        top = jnp.maximum(top, jnp.max(sounds, axis=1, keepdims=True))
        own_tile = tile_at(table, block)
        allowed[pl.ds(block, 1), :] = courant * own_tile[3:4] / (own_tile[7:8] + top)

    two_deep(prepare, finish)
    least = jnp.min(allowed[...], axis=(0, 1), keepdims=True)
    smallest[...] = jnp.broadcast_to(least, (rows, lanes))


def density_kernel(
    plan, offsets, counts, columns, distance, own, m0, m1, m2, m3, density, second, *rest
):
    outgoing = rest[0:4]
    table, masses, sums, *scratch = rest[4:]
    feats, weights = scratch[0:2], scratch[2:4]
    fill_table(own, (m0, m1, m2, m3), table, rows)
    fill_mass(own, (m0, m1, m2, m3), masses)

    def prepare(block, buf):
        centre = centre_of(tile_at(table, block))
        ids = row_ids()
        for k in range(8):
            entry = plan[k, block]
            part = slice(k * lanes, (k + 1) * lanes)
            tile = tile_at(table, entry) - centre
            weighed = jnp.where(ids == 3, 1.0, tile) * masses[pl.ds(entry, 1), :]
            stacked = jnp.concatenate(
                [weighed, weighed * tile[0:1], weighed * tile[1:2], weighed * tile[2:3]], axis=0
            )
            high, low = split2(stacked)
            feats[buf][0:32, part] = high
            feats[buf][32:64, part] = low

    def finish(block, buf):
        for start in range(0, lanes, chunk):
            at = pl.ds(pl.multiple_of(block * lanes + start, chunk), chunk)
            scale = columns[at, 2 * lanes :]
            for k in range(8):
                part = slice(k * lanes, (k + 1) * lanes)
                ratio = distance[at, part] * scale
                wide = jnp.maximum(1.0 - ratio, 0.0)
                narrow = jnp.maximum(0.5 - ratio, 0.0)
                twice = narrow + narrow
                high, low = split2(wide * wide * wide - twice * twice * narrow)
                weights[buf][start : start + chunk, part] = high
                weights[buf][lanes + start : lanes + start + chunk, part] = low
        out = lax.dot_general(
            feats[buf][...], weights[buf][...], (((1,), (1,)), ((), ())), preferred_element_type=f32
        )
        out = out[0:32] + out[32:64]
        at = pl.ds(pl.multiple_of(block * 32, 32), 32)
        sums[at, :] = out[:, 0:lanes] + out[:, lanes:]

    two_deep(prepare, finish)

    def total(field):
        return sums[pl.ds(field, 8, stride=32), :]

    def mine(field):
        return own[pl.ds(field, 8, stride=rows), :]

    length = mine(3)
    place = [mine(a) for a in range(3)]
    place = [value - (jnp.floor(value[:, 0:1]) + 0.5) for value in place]
    whole = total(3)
    dens = whole * (2.0 / math.pi) / (length * length * length)
    first = [total(a) for a in range(3)]
    inverse = 1.0 / whole
    floor = 0.05 * length * length

    def moment(a, b):
        raw = total(8 + 8 * a + b) - place[a] * first[b] - place[b] * first[a]
        return (raw + place[a] * place[b] * whole) * inverse

    axx = moment(0, 0) + floor
    ayy = moment(1, 1) + floor
    azz = moment(2, 2) + floor
    axy, axz, ayz = moment(0, 1), moment(0, 2), moment(1, 2)
    cof_xx = ayy * azz - ayz * ayz
    cof_yy = axx * azz - axz * axz
    cof_zz = axx * ayy - axy * axy
    cof_xy = axz * ayz - axy * azz
    cof_xz = axy * ayz - ayy * axz
    cof_yz = axy * axz - axx * ayz
    inv_det = 1.0 / (axx * cof_xx + axy * cof_xy + axz * cof_xz)
    density[...] = dens
    pressure = (gas_gamma - 1.0) * own[72:80, :] / dens
    fields = [dens, pressure, cof_xx * inv_det, cof_yy * inv_det, cof_zz * inv_det]
    fields += [cof_xy * inv_det, cof_xz * inv_det, cof_yz * inv_det]
    for field in range(8):
        for block in range(8):
            at = block * rows + field
            second[at : at + 1, :] = fields[field][block : block + 1, :]
    cut_windows(lambda r: offsets[0, r], lambda r: counts[0, r], second, outgoing, False)


def weight_kernel(
    first, plan, columns, distance, rates, density, own, m0, m1, m2, m3,
    weights, damping, dens_col, table
):
    fill_table(own, (m0, m1, m2, m3), table, rows)

    def step(place, _):
        block = first + place
        turned = jnp.broadcast_to(density[pl.ds(block, 1), :], (lanes, lanes)).T
        dens_col[pl.ds(pl.multiple_of(place * lanes, lanes), lanes), :] = turned
        tiles = [tile_at(table, plan[k, block]) for k in range(8)]
        for start in range(0, lanes, chunk):
            at = pl.ds(pl.multiple_of(block * lanes + start, chunk), chunk)
            to = pl.ds(pl.multiple_of(place * lanes + start, chunk), chunk)
            len_own = columns[at, 0:lanes]
            sound_own = columns[at, lanes : 2 * lanes]
            for k in range(8):
                part = slice(k * lanes, (k + 1) * lanes)
                inv_len = 1.0 / (len_own + tiles[k][3:4] * 0.05)
                ratio = distance[at, part] * inv_len
                wide = jnp.maximum(20.0 - ratio, 0.0) * inv_len
                narrow = jnp.maximum(10.0 - ratio, 0.0) * inv_len
                twice = narrow + narrow
                weight = wide * wide * wide - twice * twice * narrow
                rate = jnp.minimum(rates[at, part], 0.0)
                sounds = sound_own + tiles[k][7:8] * 0.75
                damping[to, part] = weight * rate * (rate - sounds)
                high, low = split2(weight)
                base = pl.multiple_of(place * 2 * lanes + start, chunk)
                weights[pl.ds(base, chunk), part] = high
                weights[pl.ds(base + lanes, chunk), part] = low
        return 0

    lax.fori_loop(0, 4, step, 0, unroll=2)


def momentum_kernel(
    plan, weights_a, damping_a, dens_col_a, weights_b, damping_b, dens_col_b,
    own, m0, m1, m2, m3, second, s0, s1, s2, s3, accel, heating, *scratch
):
    table, masses, table2, sums, *scratch = scratch
    feats, damped = scratch[0:2], scratch[2:4]
    fill_table(own, (m0, m1, m2, m3), table, rows)
    fill_mass(own, (m0, m1, m2, m3), masses)
    fill_table(second, (s0, s1, s2, s3), table2, rows)
    ids = row_ids()

    def features(tile, extra, mass):
        cols = [
            jnp.concatenate([extra[i : i + 1] for i in picked], axis=0)
            for picked in ((2, 5, 6, 2, 2, 5, 6, 2), (5, 3, 7, 3, 5, 3, 7, 3), (6, 7, 4, 4, 6, 7, 4, 4))
        ]
        heavy = tile * mass
        applied = None
        for axis in range(3):
            operand = jnp.where(ids < 4, tile[axis : axis + 1], tile[4 + axis : 5 + axis])
            term = cols[axis] * operand
            applied = term if applied is None else applied + term
        swirl = (
            applied[0:1] * tile[4:5] + applied[1:2] * tile[5:6] + applied[2:3] * tile[6:7]
        )
        applied = placed(applied, 3, swirl)
        press = extra[1:2] * mass
        parts = [jnp.where(ids == 3, mass, heavy)]
        parts += [heavy * tile[4 + axis : 5 + axis] for axis in range(3)]
        parts += [extra * mass, extra * press, applied * mass, applied * press]
        return jnp.concatenate(parts, axis=0)

    def prepare(block, buf):
        centre = centre_of(tile_at(table, block))
        for k in range(8):
            entry = plan[k, block]
            part = slice(k * lanes, (k + 1) * lanes)
            tile = tile_at(table, entry) - centre
            high, low = split2(
                features(tile, tile_at(table2, entry), masses[pl.ds(entry, 1), :])
            )
            feats[buf][0:64, part] = high
            feats[buf][64:128, part] = low

    def finish_part(weights, damping, dens_col, first, block, buf):
        place = block - first
        for start in range(0, lanes, chunk):
            at = pl.ds(pl.multiple_of(place * lanes + start, chunk), chunk)
            for k in range(8):
                dens_row = tile_at(table2, plan[k, block])[0:1]
                part = slice(k * lanes, (k + 1) * lanes)
                high, low = split2(damping[at, part] / (dens_col[at, :] + dens_row))
                damped[buf][start : start + chunk, part] = high
                damped[buf][lanes + start : lanes + start + chunk, part] = low
        own_weights = weights[pl.ds(pl.multiple_of(place * 2 * lanes, lanes), 2 * lanes), :]
        for base, value in ((0, own_weights), (64, damped[buf][...])):
            out = lax.dot_general(
                feats[buf][...], value, (((1,), (1,)), ((), ())), preferred_element_type=f32
            )
            out = out[0:64] + out[64:128]
            at = pl.ds(pl.multiple_of(block * lanes + base, 64), 64)
            sums[at, :] = out[:, 0:lanes] + out[:, lanes:]

    two_deep(prepare, functools.partial(finish_part, weights_a, damping_a, dens_col_a, 0), 0, 4)
    two_deep(prepare, functools.partial(finish_part, weights_b, damping_b, dens_col_b, 4), 4, 8)

    def mine(ref, field):
        return ref[pl.ds(field, 8, stride=rows), :]

    place = [mine(own, a) for a in range(3)]
    place = [value - (jnp.floor(value[:, 0:1]) + 0.5) for value in place]
    speed = [mine(own, 4 + a) for a in range(3)]
    pressure = mine(second, 1)
    order = ((2, 5, 6), (5, 3, 7), (6, 7, 4))
    matrix = [[mine(second, order[a][b]) for b in range(3)] for a in range(3)]

    def pieces(base):
        def total(field):
            return sums[pl.ds(base + field, 8, stride=lanes), :]

        mass = total(3)
        offset = [total(a) - place[a] * mass for a in range(3)]
        mass_v = [total(4 + a) for a in range(3)]
        applied = [
            matrix[a][0] * offset[0] + matrix[a][1] * offset[1] + matrix[a][2] * offset[2]
            for a in range(3)
        ]
        work = None
        for a in range(3):
            for b in range(3):
                cross = speed[a] * offset[b] - total(8 + 8 * a + b) + mass_v[a] * place[b]
                term = matrix[a][b] * cross
                work = term if work is None else work + term
        return total, applied, work

    def near_force(total, matrices, vectors):
        return [
            total(vectors + a)
            - total(matrices + order[a][0]) * place[0]
            - total(matrices + order[a][1]) * place[1]
            - total(matrices + order[a][2]) * place[2]
            for a in range(3)
        ]

    norm = 16.0 / math.pi / 20.0**6
    total, applied, work = pieces(0)
    pushed = near_force(total, 40, 56)
    total2, applied2, work2 = pieces(64)
    pushed2 = near_force(total2, 32, 48)
    for a in range(3):
        value = -norm * (
            pressure * applied[a] + pushed[a] + (2.0 / 9.0) * (applied2[a] + pushed2[a])
        )
        for block in range(8):
            part = slice(block * lanes, (block + 1) * lanes)
            accel[a : a + 1, part] = value[block : block + 1, :]
    near_work = (
        speed[0] * pushed2[0]
        + speed[1] * pushed2[1]
        + speed[2] * pushed2[2]
        - total2(51)
        + place[0] * total2(52)
        + place[1] * total2(53)
        + place[2] * total2(54)
    )
    heating[...] = norm * (pressure * work + (1.0 / 9.0) * (work2 + near_work))


def call(kernel, outs, scratch, smem, args, flops, limit):
    return pl.pallas_call(
        kernel,
        out_shape=[jax.ShapeDtypeStruct(shape, kind) for shape, kind in outs],
        in_specs=[smem_spec] * smem + [vmem_spec] * (len(args) - smem),
        out_specs=[vmem_spec] * len(outs),
        scratch_shapes=[pltpu.VMEM(shape, kind) for shape, kind in scratch],
        compiler_params=pltpu.CompilerParams(vmem_limit_bytes=limit * 1024 * 1024),
        cost_estimate=pl.CostEstimate(flops=flops, bytes_accessed=200000, transcendentals=0),
    )(*args)


def fold(value, axis, step):
    size = lax.axis_size(axis)
    return jnp.minimum(value, lax.ppermute(value, axis, [(i, i ^ step) for i in range(size)]))


def body(positions, velocities, mass, smoothing, energy, send_offsets, send_counts, pair_blocks):
    points = positions.shape[1]
    send_offsets, send_counts = send_offsets.reshape(1, 4), send_counts.reshape(1, 4)
    tile = ((rows, lanes), f32)
    packed = ((72, lanes), f32)
    own, *outgoing = pl.pallas_call(
        pack_kernel,
        out_shape=[jax.ShapeDtypeStruct((80, lanes), f32)] + [jax.ShapeDtypeStruct(*packed)] * 4,
        in_specs=[vmem_spec] * 5 + [smem_spec] * 2,
        out_specs=[vmem_spec] * 5,
    )(
        positions,
        velocities,
        mass.reshape(8, lanes),
        smoothing.reshape(8, lanes),
        energy.reshape(8, lanes),
        send_offsets,
        send_counts,
    )
    received = [swap(value, axis, odd) for value, (axis, odd, _) in zip(outgoing, swaps)]
    steps = [
        (axis, 1 << bit)
        for axis in ("slab", "dom")
        for bit in reversed(range(lax.axis_size(axis).bit_length() - 1))
    ]
    left, columns, own = pl.pallas_call(
        own_kernel,
        out_shape=[
            jax.ShapeDtypeStruct((8 * lanes, lanes), bf16),
            jax.ShapeDtypeStruct((8 * lanes, 3 * lanes), f32),
            jax.ShapeDtypeStruct((80, lanes), f32),
        ],
        in_specs=[vmem_spec],
        out_specs=[vmem_spec] * 3,
        compiler_params=pltpu.CompilerParams(vmem_limit_bytes=8 * 1024 * 1024),
    )(own)
    table = ((328, lanes), f32)
    masses = ((48, lanes), f32)
    near = ((lanes, 16 * lanes), bf16)
    feats = ((64, 8 * lanes), bf16)
    halves = ((2 * lanes, 8 * lanes), bf16)
    square = ((8 * lanes, 8 * lanes), f32)
    allowed, smallest, distance, rates = call(
        signal_kernel,
        [tile, tile, square, square],
        [table, near, near],
        1,
        (pair_blocks, left, columns, own, *received),
        3 * 10**9,
        20,
    )
    smallest = fold(smallest, *steps[0])
    density, second, *outgoing2 = call(
        density_kernel,
        [tile] + [((64, lanes), f32)] * 5,
        [table, masses, ((8 * 32, lanes), f32)] + [feats] * 2 + [halves] * 2,
        3,
        (pair_blocks, send_offsets, send_counts, columns, distance, own, *received),
        5 * 10**9,
        20,
    )
    smallest, outgoing2 = lax.optimization_barrier((smallest, outgoing2))
    received2 = [swap(value, axis, odd) for value, (axis, odd, _) in zip(outgoing2, swaps)]
    parts = []
    for first in (0, 4):
        step, steps_left = steps[1], steps[2:]
        smallest = fold(smallest, *step)
        steps = steps[:1] + steps_left
        weights, damping, dens_col = call(
            functools.partial(weight_kernel, first),
            [((8 * lanes, 8 * lanes), bf16), ((4 * lanes, 8 * lanes), f32), ((4 * lanes, lanes), f32)],
            [table],
            1,
            (pair_blocks, columns, distance, rates, density, own, *received),
            10**8,
            20,
        )
        smallest, distance, weights = lax.optimization_barrier((smallest, distance, weights))
        parts += [weights, damping, dens_col]
    for step in steps[1:-2]:
        smallest = fold(smallest, *step)
    smallest, received2 = lax.optimization_barrier((smallest, received2))
    accel, heating = call(
        momentum_kernel,
        [((3, points), f32), tile],
        [table, masses, table, ((8 * lanes, lanes), f32)]
        + [((lanes, 8 * lanes), bf16)] * 2
        + [halves] * 2,
        1,
        (pair_blocks, *parts, own, *received, second, *received2),
        5 * 10**9,
        20,
    )
    smallest = fold(smallest, *steps[-2])
    smallest, accel = lax.optimization_barrier((smallest, accel))
    smallest = fold(smallest, *steps[-1])
    share = smallest / allowed
    return (density.reshape(points), accel, heating.reshape(points), share.reshape(points))


def solution(mesh):
    both = ("slab", "dom")
    wide, flat = P(None, both), P(both)
    in_specs = (wide, wide, flat, flat, flat, wide, wide, wide)
    out_specs = (flat, wide, flat, flat)
    return jax.shard_map(body, mesh=mesh, in_specs=in_specs, out_specs=out_specs, check_vma=False)
```

time: 64.9 us -> 45.5 us (0.70)
  waiting for transfers between devices: 18.7 us -> 3.86 us
  Pallas kernels: 29.5 us -> 23.4 us
  starting transfers between devices: 12.4 us -> 14.4 us
    ppermute x5, waiting for transfers between devices: 12.3 us -> 3.19 us  [fold(): lax.ppermute(value, axis, [(i, i ^ step) for i in range(size)])]
    pallas_call x4 -> x7, Pallas kernels: 29.5 us -> 23.4 us  [the longest x5 19.7 us: call(): pl.pallas_call(kernel, out_shape=[jax.ShapeDtypeStruct(shape, kind) for s...]
    ppermute x8, waiting for transfers between devices: 6.38 us -> 0.67 us  [swap(): return lax.ppermute(value, axis, pairs)]
    ppermute x5, starting transfers between devices: 2.2 us -> 4.27 us  [fold(): lax.ppermute(value, axis, [(i, i ^ step) for i in range(size)])]
    unnamed x16 -> x14, local copies, waits for them, and re-layouts: 2.77 us -> 2.17 us
  transfers between devices with their start and end apart: 13 -> 13, of which waited for: 8 -> 3; matrix products, arithmetic and copies ran while one was open for 1% -> 0% of each run, Pallas kernels for 13% -> 39%
where the time goes in v2:
time: 45.5 us; the launch traced here: 45.2 us
  Pallas kernels  23.4 us (51%)
  starting transfers between devices  14.4 us (32%)
  waiting for transfers between devices  3.86 us (8%)
  local copies, waits for them, and re-layouts  2.17 us (5%)
  between operations  0.75 us (2%)
  other arithmetic  0.61 us (1%)
    pallas_call x5, Pallas kernels, call(): pl.pallas_call(kernel, out_shape=[jax.ShapeDtypeStruct(shape, kind) for s...  19.7 us
    ppermute x8, starting transfers between devices, swap(): return lax.ppermute(value, axis, pairs)  10.1 us
    ppermute x5, starting transfers between devices, fold(): lax.ppermute(value, axis, [(i, i ^ step) for i in range(size)])  4.27 us
    ppermute x5, waiting for transfers between devices, fold(): lax.ppermute(value, axis, [(i, i ^ step) for i in range(size)])  3.19 us
    unnamed x14, local copies, waits for them, and re-layouts  2.17 us
    pallas_call x1, Pallas kernels, body(): pl.pallas_call(own_kernel, out_shape=[jax.ShapeDtypeStruct((8 * lanes, la...  2.13 us
    pallas_call x1, Pallas kernels, body(): pl.pallas_call(pack_kernel, out_shape=[jax.ShapeDtypeStruct((80, lanes),...  1.57 us
  transfers between devices with their start and end apart: 13, of which 3 were waited for; matrix products, arithmetic and copies ran while one was open for 0% of the time, Pallas kernels for 39%

profile of v2, /device:TPU:0, one launch (start us, length us, event | category | flops | bytes accessed | tf_op | source)
XLA Modules:
  0.0 45.2 jit_solution(2964773615939026014)
XLA Ops:
  0.6 1.6 %shard_map.111 = (f32[80,128]{1,0:T(8,128)}, f32[72,128]{1,0:T(8,128)}, f32[72,128]{1,0:T(8,128)}, f32[72,128]{1,0:T(8,128)}, f32[72,128]{1,0:T(8,128)}) custom-call(f32[3,1024]{1,0:T(4,128)} %positions.1, f32[3,1024]{1,0:T(4,128)} %velocities.1, f32[8,128]{1,0:T(8,128)} %bitcast.14, f32[8,128]{1,0:T(8,128)} %bitcast.15, f32[8,128]{1,0:T(8,128)} %bitcast.16, ...), custom_call_target="tpu_custom_call" | custom-call | tf_op jit(solution)/shard_map/pallas_call | solution.py:525
  2.2 0.5 %collective-permute-start = (f32[72,128]{1,0:T(8,128)}, f32[72,128]{1,0:T(8,128)S(1)}, u32[]{:S(2)}, u32[]{:S(2)}) collective-permute-start(f32[72,128]{1,0:T(8,128)} %get-tuple-element.51), channel_id=1, source_target_pairs={{0,1},{1,0},{2,3},{3,2},{4,5},{5,4},{6,7},{7,6},{8,9},{9,8},{10,11... | collective-permute-start | bytes 110600 | tf_op jit(solution)/shard_map/ppermute | solution.py:38
  2.7 2.5 %collective-permute-start.1 = (f32[72,128]{1,0:T(8,128)}, f32[72,128]{1,0:T(8,128)S(1)}, u32[]{:S(2)}, u32[]{:S(2)}) collective-permute-start(f32[72,128]{1,0:T(8,128)} %get-tuple-element.52), channel_id=1, source_target_pairs={{0,8},{8,0},{16,24},{24,16},{1,9},{9,1},{17,25},{25,17},{2,10},{10... | collective-permute-start | bytes 110600 | tf_op jit(solution)/shard_map/ppermute | solution.py:38
  5.2 3.4 %collective-permute-start.2 = (f32[72,128]{1,0:T(8,128)}, f32[72,128]{1,0:T(8,128)S(1)}, u32[]{:S(2)}, u32[]{:S(2)}) collective-permute-start(f32[72,128]{1,0:T(8,128)} %get-tuple-element.53), channel_id=1, source_target_pairs={{0,7},{1,2},{2,1},{3,4},{4,3},{5,6},{6,5},{7,0},{8,15},{9,10},{10,... | collective-permute-start | bytes 110600 | tf_op jit(solution)/shard_map/ppermute | solution.py:38
  8.6 1.5 %collective-permute-start.3 = (f32[72,128]{1,0:T(8,128)}, f32[72,128]{1,0:T(8,128)S(1)}, u32[]{:S(2)}, u32[]{:S(2)}) collective-permute-start(f32[72,128]{1,0:T(8,128)} %get-tuple-element.54), channel_id=1, source_target_pairs={{0,24},{8,16},{16,8},{24,0},{1,25},{9,17},{17,9},{25,1},{2,26},{10... | collective-permute-start | bytes 110600 | tf_op jit(solution)/shard_map/ppermute | solution.py:38
  10.1 0.0 copy-start
  10.1 0.8 %copy-done = f32[80,128]{1,0:T(8,128)S(1)} copy-done((f32[80,128]{1,0:T(8,128)S(1)}, f32[80,128]{1,0:T(8,128)}, u32[]{:S(2)}) %copy-start) | copy-done | bytes 40984
  10.8 2.1 %shard_map.112 = (bf16[1024,128]{1,0:T(8,128)(2,1)S(1)}, f32[1024,384]{1,0:T(8,128)S(1)}, f32[80,128]{1,0:T(8,128)S(1)}) custom-call(f32[80,128]{1,0:T(8,128)S(1)} %copy-done), custom_call_target="tpu_custom_call" | custom-call | tf_op jit(solution)/shard_map/pallas_call | solution.py:545
  13.0 0.0 collective-permute-done.m0
  13.0 0.0 collective-permute-done.1.m1
  13.0 0.0 collective-permute-done.2.m2
  13.0 0.6 %collective-permute-done.3.m3 = f32[72,128]{1,0:T(8,128)S(1)} collective-permute-done((f32[72,128]{1,0:T(8,128)}, f32[72,128]{1,0:T(8,128)S(1)}, u32[]{:S(2)}, u32[]{:S(2)}) %collective-permute-start.3) | collective-permute-done | bytes 36896 | tf_op jit(solution)/shard_map/ppermute | solution.py:38
  13.6 0.0 copy-start.1
  13.7 0.7 %copy-done.1 = s32[8,8]{1,0:T(8,128)S(1)} copy-done((s32[8,8]{1,0:T(8,128)S(1)}, s32[8,8]{1,0:T(8,128)}, u32[]{:S(2)}) %copy-start.1) | copy-done | bytes 280
  14.3 0.0 copy-start.5
  14.3 0.0 copy-start.6
  14.3 4.4 %shard_map.113 = (f32[8,128]{1,0:T(8,128)S(1)}, f32[8,128]{1,0:T(8,128)S(1)}, f32[1024,1024]{1,0:T(8,128)S(1)}, f32[1024,1024]{1,0:T(8,128)S(1)}) custom-call(s32[8,8]{1,0:T(8,128)S(1)} %copy-done.1, bf16[1024,128]{1,0:T(8,128)(2,1)S(1)} %get-tuple-element.49.left, f32[1024,384]{1,0:T(8,128)S(1)} %get-tuple-element.48.columns, ...), custom_call_target="tpu_custom_call" | custom-call | flops 3000000000 | bytes 200000 | tf_op jit(solution)/shard_map/pallas_call | solution.py:504
  18.8 1.6 %collective-permute-start.4 = (f32[8,128]{1,0:T(8,128)S(1)}, f32[8,128]{1,0:T(8,128)S(1)}, u32[]{:S(2)}, u32[]{:S(2)}) collective-permute-start(f32[8,128]{1,0:T(8,128)S(1)} %get-tuple-element.57), channel_id=1, source_target_pairs={{0,16},{8,24},{16,0},{24,8},{1,17},{9,25},{17,1},{25,9},{2,18},{10... | collective-permute-start | bytes 12296 | tf_op jit(solution)/shard_map/ppermute | solution.py:517
  20.4 0.0 copy-done.5
  20.4 0.0 copy-done.6
  20.4 5.1 %shard_map.114 = (f32[8,128]{1,0:T(8,128)}, f32[64,128]{1,0:T(8,128)S(1)}, f32[64,128]{1,0:T(8,128)S(1)}, f32[64,128]{1,0:T(8,128)S(1)}, f32[64,128]{1,0:T(8,128)S(1)}, /*index=5*/f32[64,128]{1,0:T(8,128)S(1)}) custom-call(s32[8,8]{1,0:T(8,128)S(1)} %copy-done.1, s32[1,4]{1,0:T(1,128)S(1)} %bitcast.11, s32[1,4]{1,0:T(1,128)S(1)} %bitcast.13, ...), custom_call_target="tpu_custom_call" | custom-call | flops 5000000000 | bytes 200000 | tf_op jit(solution)/shard_map/pallas_call | solution.py:504
  25.5 0.0 collective-permute-done.4
  25.5 0.0 collective-permute-start.7
  25.6 0.6 %collective-permute-start.8 = (f32[64,128]{1,0:T(8,128)S(1)}, f32[64,128]{1,0:T(8,128)S(1)}, u32[]{:S(2)}, u32[]{:S(2)}) collective-permute-start(f32[64,128]{1,0:T(8,128)S(1)} %get-tuple-element.70), channel_id=1, source_target_pairs={{0,8},{8,0},{16,24},{24,16},{1,9},{9,1},{17,25},{25,17},{2,10},{10... | collective-permute-start | bytes 98312 | tf_op jit(solution)/shard_map/ppermute | solution.py:38
  26.2 0.2 collective-permute-start.9
  26.4 1.4 %collective-permute-start.10 = (f32[64,128]{1,0:T(8,128)S(1)}, f32[64,128]{1,0:T(8,128)S(1)}, u32[]{:S(2)}, u32[]{:S(2)}) collective-permute-start(f32[64,128]{1,0:T(8,128)S(1)} %get-tuple-element.72), channel_id=1, source_target_pairs={{0,24},{8,16},{16,8},{24,0},{1,25},{9,17},{17,9},{25,1},{2,26},{10... | collective-permute-start | bytes 98312 | tf_op jit(solution)/shard_map/ppermute | solution.py:38
  27.8 0.9 %collective-permute-start.5 = (f32[8,128]{1,0:T(8,128)S(1)}, f32[8,128]{1,0:T(8,128)S(1)}, u32[]{:S(2)}, u32[]{:S(2)}) collective-permute-start(f32[8,128]{1,0:T(8,128)S(1)} %min.15), channel_id=1, source_target_pairs={{0,8},{8,0},{16,24},{24,16},{1,9},{9,1},{17,25},{25,17},{2,10},{10... | collective-permute-start | bytes 12296 | tf_op jit(solution)/shard_map/ppermute | solution.py:517
  28.7 0.0 copy-start.3
  28.7 0.7 %copy-done.3 = f32[8,128]{1,0:T(8,128)S(1)} copy-done((f32[8,128]{1,0:T(8,128)S(1)}, f32[8,128]{1,0:T(8,128)}, u32[]{:S(2)}) %copy-start.3) | copy-done | bytes 4120
  29.4 0.0 copy-start.4
  29.4 2.4 %shard_map.115 = (bf16[1024,1024]{1,0:T(8,128)(2,1)S(1)}, f32[512,1024]{1,0:T(8,128)S(1)}, f32[512,128]{1,0:T(8,128)S(1)}) custom-call(s32[8,8]{1,0:T(8,128)S(1)} %copy-done.1, f32[1024,384]{1,0:T(8,128)S(1)} %get-tuple-element.48.columns, f32[1024,1024]{1,0:T(8,128)S(1)} %get-tuple-element.66.distance, f32[1024,1024]{1,0:T(8,128)S(1)} %get-tuple-element.63.rates, ...), custom_call_target="tpu_custom_call" | custom-call | flops 100000000 | bytes 200000 | tf_op jit(solution)/shard_map/pallas_call | solution.py:504
  31.8 0.0 collective-permute-done.5
  31.8 0.0 copy-start.2
  31.8 0.1 collective-permute-start.6
  31.9 0.0 copy-done.4
  31.9 2.4 %shard_map.116 = (bf16[1024,1024]{1,0:T(8,128)(2,1)S(1)}, f32[512,1024]{1,0:T(8,128)S(1)}, f32[512,128]{1,0:T(8,128)S(1)}) custom-call(s32[8,8]{1,0:T(8,128)S(1)} %copy-done.1, f32[1024,384]{1,0:T(8,128)S(1)} %get-tuple-element.48.columns, f32[1024,1024]{1,0:T(8,128)S(1)} %get-tuple-element.66.distance, f32[1024,1024]{1,0:T(8,128)S(1)} %get-tuple-element.63.rates, ...), custom_call_target="tpu_custom_call" | custom-call | flops 100000000 | bytes 200000 | tf_op jit(solution)/shard_map/pallas_call | solution.py:504
  34.4 2.0 %collective-permute-done.6 = f32[8,128]{1,0:T(8,128)S(1)} collective-permute-done((f32[8,128]{1,0:T(8,128)S(1)}, f32[8,128]{1,0:T(8,128)S(1)}, u32[]{:S(2)}, u32[]{:S(2)}) %collective-permute-start.6) | collective-permute-done | bytes 4128 | tf_op jit(solution)/shard_map/ppermute | solution.py:517
  36.4 0.0 collective-permute-done.7.s0
  36.4 0.0 collective-permute-done.8.s1
  36.4 0.0 collective-permute-done.9.s2
  36.4 0.0 collective-permute-done.10.s3
  36.4 1.6 %collective-permute-start.11 = (f32[8,128]{1,0:T(8,128)S(1)}, f32[8,128]{1,0:T(8,128)S(1)}, u32[]{:S(2)}, u32[]{:S(2)}) collective-permute-start(f32[8,128]{1,0:T(8,128)S(1)} %min.17), channel_id=1, source_target_pairs={{0,2},{1,3},{2,0},{3,1},{4,6},{5,7},{6,4},{7,5},{8,10},{9,11},{10,... | collective-permute-start | bytes 12296 | tf_op jit(solution)/shard_map/ppermute | solution.py:517
  38.1 0.0 copy-done.2
  38.1 5.3 %shard_map.117 = (f32[3,1024]{1,0:T(4,128)}, f32[8,128]{1,0:T(8,128)}) custom-call(s32[8,8]{1,0:T(8,128)S(1)} %copy-done.2, bf16[1024,1024]{1,0:T(8,128)(2,1)S(1)} %get-tuple-element.74.weights_a, f32[512,1024]{1,0:T(8,128)S(1)} %get-tuple-element.75.damping_a, f32[512,128]{1,0:T(8,128)S(1)} %get-tuple-element.76.dens_col_a, ...), custom_call_target="tpu_custom_call" | custom-call | flops 5000000000 | bytes 200000 | tf_op jit(solution)/shard_map/pallas_call | solution.py:504
  43.4 0.0 collective-permute-done.11
  43.4 0.1 collective-permute-start.12
  43.5 1.2 %collective-permute-done.12 = f32[8,128]{1,0:T(8,128)S(1)} collective-permute-done((f32[8,128]{1,0:T(8,128)S(1)}, f32[8,128]{1,0:T(8,128)S(1)}, u32[]{:S(2)}, u32[]{:S(2)}) %collective-permute-start.12) | collective-permute-done | bytes 4128 | tf_op jit(solution)/shard_map/ppermute | solution.py:517
  44.6 0.6 %divide_bitcast_fusion = f32[1024]{0:T(1024)} fusion(f32[8,128]{1,0:T(8,128)S(1)} %get-tuple-element.89, f32[8,128]{1,0:T(8,128)S(1)} %min.18, f32[8,128]{1,0:T(8,128)S(1)} %collective-permute-done.12), kind=kLoop, calls=%fused_computation | loop fusion | flops 2048 | bytes 16384 | tf_op jit(solution)/shard_map/reshape | solution.py:617
  (4 shorter events, 0.0 us)
Async XLA Ops:
  2.2 10.8 %collective-permute-start = (f32[72,128]{1,0:T(8,128)}, f32[72,128]{1,0:T(8,128)S(1)}, u32[]{:S(2)}, u32[]{:S(2)}) collective-permute-start(f32[72,128]{1,0:T(8,128)} %get-tuple-element.51), channel_id=1, source_target_pairs={{0,1},{1,0},{2,3},{3,2},{4,5},{5,4},{6,7},{7,6},{8,9},{9,8},{10,11... | collective-permute-start | bytes 110600 | tf_op jit(solution)/shard_map/ppermute | solution.py:38
  2.7 10.3 %collective-permute-start.1 = (f32[72,128]{1,0:T(8,128)}, f32[72,128]{1,0:T(8,128)S(1)}, u32[]{:S(2)}, u32[]{:S(2)}) collective-permute-start(f32[72,128]{1,0:T(8,128)} %get-tuple-element.52), channel_id=1, source_target_pairs={{0,8},{8,0},{16,24},{24,16},{1,9},{9,1},{17,25},{25,17},{2,10},{10... | collective-permute-start | bytes 110600 | tf_op jit(solution)/shard_map/ppermute | solution.py:38
  5.2 7.8 %collective-permute-start.2 = (f32[72,128]{1,0:T(8,128)}, f32[72,128]{1,0:T(8,128)S(1)}, u32[]{:S(2)}, u32[]{:S(2)}) collective-permute-start(f32[72,128]{1,0:T(8,128)} %get-tuple-element.53), channel_id=1, source_target_pairs={{0,7},{1,2},{2,1},{3,4},{4,3},{5,6},{6,5},{7,0},{8,15},{9,10},{10,... | collective-permute-start | bytes 110600 | tf_op jit(solution)/shard_map/ppermute | solution.py:38
  8.6 5.1 %collective-permute-start.3 = (f32[72,128]{1,0:T(8,128)}, f32[72,128]{1,0:T(8,128)S(1)}, u32[]{:S(2)}, u32[]{:S(2)}) collective-permute-start(f32[72,128]{1,0:T(8,128)} %get-tuple-element.54), channel_id=1, source_target_pairs={{0,24},{8,16},{16,8},{24,0},{1,25},{9,17},{17,9},{25,1},{2,26},{10... | collective-permute-start | bytes 110600 | tf_op jit(solution)/shard_map/ppermute | solution.py:38
  10.1 0.8 %copy-start = (f32[80,128]{1,0:T(8,128)S(1)}, f32[80,128]{1,0:T(8,128)}, u32[]{:S(2)}) copy-start(f32[80,128]{1,0:T(8,128)} %get-tuple-element.47.own) | copy-start | bytes 122884
  13.6 0.7 %copy-start.1 = (s32[8,8]{1,0:T(8,128)S(1)}, s32[8,8]{1,0:T(8,128)}, u32[]{:S(2)}) copy-start(s32[8,8]{1,0:T(8,128)} %plan.9) | copy-start | bytes 772
  14.3 6.1 %copy-start.5 = (s32[4,1]{0,1:T(1,128)S(1)}, s32[4,1]{0,1:T(1,128)}, u32[]{:S(2)}) copy-start(s32[4,1]{0,1:T(1,128)} %param.13) | copy-start | bytes 52
  14.3 6.1 %copy-start.6 = (s32[4,1]{0,1:T(1,128)S(1)}, s32[4,1]{0,1:T(1,128)}, u32[]{:S(2)}) copy-start(s32[4,1]{0,1:T(1,128)} %param.14) | copy-start | bytes 52
  18.8 6.7 %collective-permute-start.4 = (f32[8,128]{1,0:T(8,128)S(1)}, f32[8,128]{1,0:T(8,128)S(1)}, u32[]{:S(2)}, u32[]{:S(2)}) collective-permute-start(f32[8,128]{1,0:T(8,128)S(1)} %get-tuple-element.57), channel_id=1, source_target_pairs={{0,16},{8,24},{16,0},{24,8},{1,17},{9,25},{17,1},{25,9},{2,18},{10... | collective-permute-start | bytes 12296 | tf_op jit(solution)/shard_map/ppermute | solution.py:517
  25.5 10.9 %collective-permute-start.7 = (f32[64,128]{1,0:T(8,128)S(1)}, f32[64,128]{1,0:T(8,128)S(1)}, u32[]{:S(2)}, u32[]{:S(2)}) collective-permute-start(f32[64,128]{1,0:T(8,128)S(1)} %get-tuple-element.69), channel_id=1, source_target_pairs={{0,1},{1,0},{2,3},{3,2},{4,5},{5,4},{6,7},{7,6},{8,9},{9,8},{10,11... | collective-permute-start | bytes 98312 | tf_op jit(solution)/shard_map/ppermute | solution.py:38
  25.6 10.8 %collective-permute-start.8 = (f32[64,128]{1,0:T(8,128)S(1)}, f32[64,128]{1,0:T(8,128)S(1)}, u32[]{:S(2)}, u32[]{:S(2)}) collective-permute-start(f32[64,128]{1,0:T(8,128)S(1)} %get-tuple-element.70), channel_id=1, source_target_pairs={{0,8},{8,0},{16,24},{24,16},{1,9},{9,1},{17,25},{25,17},{2,10},{10... | collective-permute-start | bytes 98312 | tf_op jit(solution)/shard_map/ppermute | solution.py:38
  26.2 10.3 %collective-permute-start.9 = (f32[64,128]{1,0:T(8,128)S(1)}, f32[64,128]{1,0:T(8,128)S(1)}, u32[]{:S(2)}, u32[]{:S(2)}) collective-permute-start(f32[64,128]{1,0:T(8,128)S(1)} %get-tuple-element.71), channel_id=1, source_target_pairs={{0,7},{1,2},{2,1},{3,4},{4,3},{5,6},{6,5},{7,0},{8,15},{9,10},{10,... | collective-permute-start | bytes 98312 | tf_op jit(solution)/shard_map/ppermute | solution.py:38
  26.4 10.1 %collective-permute-start.10 = (f32[64,128]{1,0:T(8,128)S(1)}, f32[64,128]{1,0:T(8,128)S(1)}, u32[]{:S(2)}, u32[]{:S(2)}) collective-permute-start(f32[64,128]{1,0:T(8,128)S(1)} %get-tuple-element.72), channel_id=1, source_target_pairs={{0,24},{8,16},{16,8},{24,0},{1,25},{9,17},{17,9},{25,1},{2,26},{10... | collective-permute-start | bytes 98312 | tf_op jit(solution)/shard_map/ppermute | solution.py:38
  27.8 4.0 %collective-permute-start.5 = (f32[8,128]{1,0:T(8,128)S(1)}, f32[8,128]{1,0:T(8,128)S(1)}, u32[]{:S(2)}, u32[]{:S(2)}) collective-permute-start(f32[8,128]{1,0:T(8,128)S(1)} %min.15), channel_id=1, source_target_pairs={{0,8},{8,0},{16,24},{24,16},{1,9},{9,1},{17,25},{25,17},{2,10},{10... | collective-permute-start | bytes 12296 | tf_op jit(solution)/shard_map/ppermute | solution.py:517
  28.7 0.7 %copy-start.3 = (f32[8,128]{1,0:T(8,128)S(1)}, f32[8,128]{1,0:T(8,128)}, u32[]{:S(2)}) copy-start(f32[8,128]{1,0:T(8,128)} %get-tuple-element.56.density) | copy-start | bytes 12292
  29.4 2.6 %copy-start.4 = (f32[8,128]{1,0:T(8,128)S(1)}, f32[8,128]{1,0:T(8,128)}, u32[]{:S(2)}) copy-start(f32[8,128]{1,0:T(8,128)} %get-tuple-element.56.density) | copy-start | bytes 12292
  31.8 6.3 %copy-start.2 = (s32[8,8]{1,0:T(8,128)S(1)}, s32[8,8]{1,0:T(8,128)}, u32[]{:S(2)}) copy-start(s32[8,8]{1,0:T(8,128)} %plan.9) | copy-start | bytes 772
  31.8 4.6 %collective-permute-start.6 = (f32[8,128]{1,0:T(8,128)S(1)}, f32[8,128]{1,0:T(8,128)S(1)}, u32[]{:S(2)}, u32[]{:S(2)}) collective-permute-start(f32[8,128]{1,0:T(8,128)S(1)} %min.16), channel_id=1, source_target_pairs={{0,4},{1,5},{2,6},{3,7},{4,0},{5,1},{6,2},{7,3},{8,12},{9,13},{10,... | collective-permute-start | bytes 12296 | tf_op jit(solution)/shard_map/ppermute | solution.py:517
  36.4 7.0 %collective-permute-start.11 = (f32[8,128]{1,0:T(8,128)S(1)}, f32[8,128]{1,0:T(8,128)S(1)}, u32[]{:S(2)}, u32[]{:S(2)}) collective-permute-start(f32[8,128]{1,0:T(8,128)S(1)} %min.17), channel_id=1, source_target_pairs={{0,2},{1,3},{2,0},{3,1},{4,6},{5,7},{6,4},{7,5},{8,10},{9,11},{10,... | collective-permute-start | bytes 12296 | tf_op jit(solution)/shard_map/ppermute | solution.py:517
  43.4 1.2 %collective-permute-start.12 = (f32[8,128]{1,0:T(8,128)S(1)}, f32[8,128]{1,0:T(8,128)S(1)}, u32[]{:S(2)}, u32[]{:S(2)}) collective-permute-start(f32[8,128]{1,0:T(8,128)S(1)} %min.18), channel_id=1, source_target_pairs={{0,1},{1,0},{2,3},{3,2},{4,5},{5,4},{6,7},{7,6},{8,9},{9,8},{10,11... | collective-permute-start | bytes 12296 | tf_op jit(solution)/shard_map/ppermute | solution.py:517

commit v3 on v2

--- a/solution.py
+++ b/solution.py
@@ -168,11 +168,12 @@
         finish(block + 1, 1)
         return 0
 
-    lax.fori_loop(0, (last - first) // 2, step, 0)
-
-
-def own_kernel(own, left, columns, table):
+    lax.fori_loop(0, (last - first) // 2, step, 0, unroll=True)
+
+
+def own_kernel(pairs, own, left, columns, table, plan):
     table[...] = own[...]
+    plan[...] = pairs[...]
 
     def step(block, _):
         tile = tile_at(own, block)
@@ -287,11 +288,11 @@
                 weights[buf][start : start + chunk, part] = high
                 weights[buf][lanes + start : lanes + start + chunk, part] = low
         out = lax.dot_general(
-            feats[buf][...], weights[buf][...], (((1,), (1,)), ((), ())), preferred_element_type=f32
+            weights[buf][...], feats[buf][...], (((1,), (1,)), ((), ())), preferred_element_type=f32
         )
-        out = out[0:32] + out[32:64]
+        out = (out[0:lanes] + out[lanes:]).T
         at = pl.ds(pl.multiple_of(block * 32, 32), 32)
-        sums[at, :] = out[:, 0:lanes] + out[:, lanes:]
+        sums[at, :] = out[0:32] + out[32:64]
 
     two_deep(prepare, finish)
 
@@ -337,14 +338,14 @@
 
 
 def weight_kernel(
-    first, plan, columns, distance, rates, density, own, m0, m1, m2, m3,
+    first, plan, columns, distance, rates, second, own, m0, m1, m2, m3,
     weights, damping, dens_col, table
 ):
     fill_table(own, (m0, m1, m2, m3), table, rows)
 
     def step(place, _):
         block = first + place
-        turned = jnp.broadcast_to(density[pl.ds(block, 1), :], (lanes, lanes)).T
+        turned = jnp.broadcast_to(second[pl.ds(block * rows, 1), :], (lanes, lanes)).T
         dens_col[pl.ds(pl.multiple_of(place * lanes, lanes), lanes), :] = turned
         tiles = [tile_at(table, plan[k, block]) for k in range(8)]
         for start in range(0, lanes, chunk):
@@ -429,11 +430,11 @@
         own_weights = weights[pl.ds(pl.multiple_of(place * 2 * lanes, lanes), 2 * lanes), :]
         for base, value in ((0, own_weights), (64, damped[buf][...])):
             out = lax.dot_general(
-                feats[buf][...], value, (((1,), (1,)), ((), ())), preferred_element_type=f32
+                value, feats[buf][...], (((1,), (1,)), ((), ())), preferred_element_type=f32
             )
-            out = out[0:64] + out[64:128]
+            out = (out[0:lanes] + out[lanes:]).T
             at = pl.ds(pl.multiple_of(block * lanes + base, 64), 64)
-            sums[at, :] = out[:, 0:lanes] + out[:, lanes:]
+            sums[at, :] = out[0:64] + out[64:128]
 
     two_deep(prepare, functools.partial(finish_part, weights_a, damping_a, dens_col_a, 0), 0, 4)
     two_deep(prepare, functools.partial(finish_part, weights_b, damping_b, dens_col_b, 4), 4, 8)
@@ -537,22 +538,22 @@
         send_counts,
     )
     received = [swap(value, axis, odd) for value, (axis, odd, _) in zip(outgoing, swaps)]
-    steps = [
-        (axis, 1 << bit)
-        for axis in ("slab", "dom")
-        for bit in reversed(range(lax.axis_size(axis).bit_length() - 1))
-    ]
-    left, columns, own = pl.pallas_call(
+    steps = [("dom", 1 << bit) for bit in range(lax.axis_size("dom").bit_length() - 1)]
+    steps = steps[::-1][:1] + steps[:-1]
+    steps += [("slab", 1 << bit) for bit in reversed(range(lax.axis_size("slab").bit_length() - 1))]
+    steps = steps[:2] + steps[3:] + steps[2:3]
+    left, columns, own, plan = pl.pallas_call(
         own_kernel,
         out_shape=[
             jax.ShapeDtypeStruct((8 * lanes, lanes), bf16),
             jax.ShapeDtypeStruct((8 * lanes, 3 * lanes), f32),
             jax.ShapeDtypeStruct((80, lanes), f32),
+            jax.ShapeDtypeStruct(pair_blocks.shape, jnp.int32),
         ],
-        in_specs=[vmem_spec],
-        out_specs=[vmem_spec] * 3,
+        in_specs=[vmem_spec] * 2,
+        out_specs=[vmem_spec] * 4,
         compiler_params=pltpu.CompilerParams(vmem_limit_bytes=8 * 1024 * 1024),
-    )(own)
+    )(pair_blocks, own)
     table = ((328, lanes), f32)
     masses = ((48, lanes), f32)
     near = ((lanes, 16 * lanes), bf16)
@@ -564,7 +565,7 @@
         [tile, tile, square, square],
         [table, near, near],
         1,
-        (pair_blocks, left, columns, own, *received),
+        (plan, left, columns, own, *received),
         3 * 10**9,
         20,
     )
@@ -574,29 +575,28 @@
         [tile] + [((64, lanes), f32)] * 5,
         [table, masses, ((8 * 32, lanes), f32)] + [feats] * 2 + [halves] * 2,
         3,
-        (pair_blocks, send_offsets, send_counts, columns, distance, own, *received),
+        (plan, send_offsets, send_counts, columns, distance, own, *received),
         5 * 10**9,
         20,
     )
     smallest, outgoing2 = lax.optimization_barrier((smallest, outgoing2))
     received2 = [swap(value, axis, odd) for value, (axis, odd, _) in zip(outgoing2, swaps)]
+    smallest = fold(smallest, *steps[1])
     parts = []
     for first in (0, 4):
-        step, steps_left = steps[1], steps[2:]
-        smallest = fold(smallest, *step)
-        steps = steps[:1] + steps_left
+        smallest = fold(smallest, *steps[2 + first // 4])
         weights, damping, dens_col = call(
             functools.partial(weight_kernel, first),
             [((8 * lanes, 8 * lanes), bf16), ((4 * lanes, 8 * lanes), f32), ((4 * lanes, lanes), f32)],
             [table],
             1,
-            (pair_blocks, columns, distance, rates, density, own, *received),
+            (plan, columns, distance, rates, second, own, *received),
             10**8,
             20,
         )
         smallest, distance, weights = lax.optimization_barrier((smallest, distance, weights))
         parts += [weights, damping, dens_col]
-    for step in steps[1:-2]:
+    for step in steps[4:-1]:
         smallest = fold(smallest, *step)
     smallest, received2 = lax.optimization_barrier((smallest, received2))
     accel, heating = call(
@@ -606,12 +606,10 @@
         + [((lanes, 8 * lanes), bf16)] * 2
         + [halves] * 2,
         1,
-        (pair_blocks, *parts, own, *received, second, *received2),
+        (plan, *parts, own, *received, second, *received2),
         5 * 10**9,
         20,
     )
-    smallest = fold(smallest, *steps[-2])
-    smallest, accel = lax.optimization_barrier((smallest, accel))
     smallest = fold(smallest, *steps[-1])
     share = smallest / allowed
     return (density.reshape(points), accel, heating.reshape(points), share.reshape(points))

time: 45.5 us -> 43.4 us (0.954)
  waiting for transfers between devices: 3.86 us -> 1.01 us
  starting transfers between devices: 14.4 us -> 16.3 us
  local copies, waits for them, and re-layouts: 2.17 us -> 1.48 us
    ppermute x5, waiting for transfers between devices: 3.19 us -> 0.99 us  [fold(): lax.ppermute(value, axis, [(i, i ^ step) for i in range(size)])]
    ppermute x8, starting transfers between devices: 10.1 us -> 11.4 us  [swap(): return lax.ppermute(value, axis, pairs)]
    unnamed x14 -> x8, local copies, waits for them, and re-layouts: 2.17 us -> 1.48 us
    ppermute x5, starting transfers between devices: 4.27 us -> 4.92 us  [fold(): lax.ppermute(value, axis, [(i, i ^ step) for i in range(size)])]
    ppermute x8, waiting for transfers between devices: 0.67 us -> 0.02 us  [swap(): return lax.ppermute(value, axis, pairs)]
    pallas_call x5, Pallas kernels: 19.7 us -> 19.3 us  [call(): pl.pallas_call(kernel, out_shape=[jax.ShapeDtypeStruct(shape, kind) for s...]
  transfers between devices with their start and end apart: 13 -> 13, of which waited for: 3 -> 2; matrix products, arithmetic and copies ran while one was open for 0% -> 0% of each run, Pallas kernels for 39% -> 41%
where the time goes in v3:
time: 43.4 us; the launch traced here: 43.1 us
  Pallas kernels  23 us (53%)
  starting transfers between devices  16.3 us (38%)
  local copies, waits for them, and re-layouts  1.48 us (3%)
  waiting for transfers between devices  1.01 us (2%)
  between operations  0.78 us (2%)
  other arithmetic  0.62 us (1%)
    pallas_call x5, Pallas kernels, call(): pl.pallas_call(kernel, out_shape=[jax.ShapeDtypeStruct(shape, kind) for s...  19.3 us
    ppermute x8, starting transfers between devices, swap(): return lax.ppermute(value, axis, pairs)  11.4 us
    ppermute x5, starting transfers between devices, fold(): lax.ppermute(value, axis, [(i, i ^ step) for i in range(size)])  4.92 us
    pallas_call x1, Pallas kernels, body(): pl.pallas_call(own_kernel, out_shape=[jax.ShapeDtypeStruct((8 * lanes, la...  2.13 us
    pallas_call x1, Pallas kernels, body(): pl.pallas_call(pack_kernel, out_shape=[jax.ShapeDtypeStruct((80, lanes),...  1.56 us
    unnamed x8, local copies, waits for them, and re-layouts  1.48 us
    ppermute x5, waiting for transfers between devices, fold(): lax.ppermute(value, axis, [(i, i ^ step) for i in range(size)])  0.99 us
  transfers between devices with their start and end apart: 13, of which 2 were waited for; matrix products, arithmetic and copies ran while one was open for 0% of the time, Pallas kernels for 41%

profile of v3, /device:TPU:0, one launch (start us, length us, event | category | flops | bytes accessed | tf_op | source)
XLA Modules:
  0.0 43.1 jit_solution(2196998698973682556)
XLA Ops:
  0.6 1.6 %shard_map.111 = (f32[80,128]{1,0:T(8,128)}, f32[72,128]{1,0:T(8,128)}, f32[72,128]{1,0:T(8,128)}, f32[72,128]{1,0:T(8,128)}, f32[72,128]{1,0:T(8,128)}) custom-call(f32[3,1024]{1,0:T(4,128)} %positions.1, f32[3,1024]{1,0:T(4,128)} %velocities.1, f32[8,128]{1,0:T(8,128)} %bitcast.13, f32[8,128]{1,0:T(8,128)} %bitcast.14, f32[8,128]{1,0:T(8,128)} %bitcast.15, ...), custom_call_target="tpu_custom_call" | custom-call | tf_op jit(solution)/shard_map/pallas_call | solution.py:526
  2.2 0.5 %collective-permute-start = (f32[72,128]{1,0:T(8,128)}, f32[72,128]{1,0:T(8,128)S(1)}, u32[]{:S(2)}, u32[]{:S(2)}) collective-permute-start(f32[72,128]{1,0:T(8,128)} %get-tuple-element.51), channel_id=1, source_target_pairs={{0,1},{1,0},{2,3},{3,2},{4,5},{5,4},{6,7},{7,6},{8,9},{9,8},{10,11... | collective-permute-start | bytes 110600 | tf_op jit(solution)/shard_map/ppermute | solution.py:38
  2.6 2.5 %collective-permute-start.1 = (f32[72,128]{1,0:T(8,128)}, f32[72,128]{1,0:T(8,128)S(1)}, u32[]{:S(2)}, u32[]{:S(2)}) collective-permute-start(f32[72,128]{1,0:T(8,128)} %get-tuple-element.52), channel_id=1, source_target_pairs={{0,8},{8,0},{16,24},{24,16},{1,9},{9,1},{17,25},{25,17},{2,10},{10... | collective-permute-start | bytes 110600 | tf_op jit(solution)/shard_map/ppermute | solution.py:38
  5.2 3.4 %collective-permute-start.2 = (f32[72,128]{1,0:T(8,128)}, f32[72,128]{1,0:T(8,128)S(1)}, u32[]{:S(2)}, u32[]{:S(2)}) collective-permute-start(f32[72,128]{1,0:T(8,128)} %get-tuple-element.53), channel_id=1, source_target_pairs={{0,7},{1,2},{2,1},{3,4},{4,3},{5,6},{6,5},{7,0},{8,15},{9,10},{10,... | collective-permute-start | bytes 110600 | tf_op jit(solution)/shard_map/ppermute | solution.py:38
  8.6 1.5 %collective-permute-start.3 = (f32[72,128]{1,0:T(8,128)}, f32[72,128]{1,0:T(8,128)S(1)}, u32[]{:S(2)}, u32[]{:S(2)}) collective-permute-start(f32[72,128]{1,0:T(8,128)} %get-tuple-element.54), channel_id=1, source_target_pairs={{0,24},{8,16},{16,8},{24,0},{1,25},{9,17},{17,9},{25,1},{2,26},{10... | collective-permute-start | bytes 110600 | tf_op jit(solution)/shard_map/ppermute | solution.py:38
  10.1 0.0 copy-start
  10.1 0.8 %copy-done = f32[80,128]{1,0:T(8,128)S(1)} copy-done((f32[80,128]{1,0:T(8,128)S(1)}, f32[80,128]{1,0:T(8,128)}, u32[]{:S(2)}) %copy-start) | copy-done | bytes 40984
  10.8 0.0 copy-start.1
  10.8 0.7 %copy-done.1 = s32[8,8]{1,0:T(8,128)S(1)} copy-done((s32[8,8]{1,0:T(8,128)S(1)}, s32[8,8]{1,0:T(8,128)}, u32[]{:S(2)}) %copy-start.1) | copy-done | bytes 280
  11.5 2.1 %shard_map.112 = (bf16[1024,128]{1,0:T(8,128)(2,1)S(1)}, f32[1024,384]{1,0:T(8,128)S(1)}, f32[80,128]{1,0:T(8,128)S(1)}, s32[8,8]{1,0:T(8,128)S(1)}) custom-call(s32[8,8]{1,0:T(8,128)S(1)} %copy-done.1, f32[80,128]{1,0:T(8,128)S(1)} %copy-done), custom_call_target="tpu_custom_call" | custom-call | tf_op jit(solution)/shard_map/pallas_call | solution.py:545
  13.7 0.0 collective-permute-done.m0
  13.7 0.0 collective-permute-done.1.m1
  13.7 0.0 collective-permute-done.2.m2
  13.7 0.0 collective-permute-done.3.m3
  13.7 0.0 copy-start.2
  13.7 0.0 copy-start.3
  13.7 3.9 %shard_map.113 = (f32[8,128]{1,0:T(8,128)S(1)}, f32[8,128]{1,0:T(8,128)S(1)}, f32[1024,1024]{1,0:T(8,128)S(1)}, f32[1024,1024]{1,0:T(8,128)S(1)}) custom-call(s32[8,8]{1,0:T(8,128)S(1)} %get-tuple-element.47.plan, bf16[1024,128]{1,0:T(8,128)(2,1)S(1)} %get-tuple-element.49.left, f32[1024,384]{1,0:T(8,128)S(1)} %get-tuple-element.48.columns, ...), custom_call_target="tpu_custom_call" | custom-call | flops 3000000000 | bytes 200000 | tf_op jit(solution)/shard_map/pallas_call | solution.py:505
  17.6 0.1 collective-permute-start.4
  17.7 0.0 copy-done.2
  17.7 0.0 copy-done.3
  17.7 4.9 %shard_map.114 = (f32[8,128]{1,0:T(8,128)}, f32[64,128]{1,0:T(8,128)S(1)}, f32[64,128]{1,0:T(8,128)S(1)}, f32[64,128]{1,0:T(8,128)S(1)}, f32[64,128]{1,0:T(8,128)S(1)}, /*index=5*/f32[64,128]{1,0:T(8,128)S(1)}) custom-call(s32[8,8]{1,0:T(8,128)S(1)} %get-tuple-element.47.plan, s32[1,4]{1,0:T(1,128)S(1)} %bitcast.10, s32[1,4]{1,0:T(1,128)S(1)} %bitcast.12, ...), custom_call_target="tpu_custom_call" | custom-call | flops 5000000000 | bytes 200000 | tf_op jit(solution)/shard_map/pallas_call | solution.py:505
  22.6 0.0 collective-permute-done.4
  22.6 0.3 collective-permute-start.8
  22.9 1.5 %collective-permute-start.9 = (f32[64,128]{1,0:T(8,128)S(1)}, f32[64,128]{1,0:T(8,128)S(1)}, u32[]{:S(2)}, u32[]{:S(2)}) collective-permute-start(f32[64,128]{1,0:T(8,128)S(1)} %get-tuple-element.77), channel_id=1, source_target_pairs={{0,8},{8,0},{16,24},{24,16},{1,9},{9,1},{17,25},{25,17},{2,10},{10... | collective-permute-start | bytes 98312 | tf_op jit(solution)/shard_map/ppermute | solution.py:38
  24.4 0.8 %collective-permute-start.10 = (f32[64,128]{1,0:T(8,128)S(1)}, f32[64,128]{1,0:T(8,128)S(1)}, u32[]{:S(2)}, u32[]{:S(2)}) collective-permute-start(f32[64,128]{1,0:T(8,128)S(1)} %get-tuple-element.78), channel_id=1, source_target_pairs={{0,7},{1,2},{2,1},{3,4},{4,3},{5,6},{6,5},{7,0},{8,15},{9,10},{10,... | collective-permute-start | bytes 98312 | tf_op jit(solution)/shard_map/ppermute | solution.py:38
  25.1 0.9 %collective-permute-start.11 = (f32[64,128]{1,0:T(8,128)S(1)}, f32[64,128]{1,0:T(8,128)S(1)}, u32[]{:S(2)}, u32[]{:S(2)}) collective-permute-start(f32[64,128]{1,0:T(8,128)S(1)} %get-tuple-element.79), channel_id=1, source_target_pairs={{0,24},{8,16},{16,8},{24,0},{1,25},{9,17},{17,9},{25,1},{2,26},{10... | collective-permute-start | bytes 98312 | tf_op jit(solution)/shard_map/ppermute | solution.py:38
  26.1 0.3 collective-permute-start.5
  26.4 0.9 %collective-permute-done.5 = f32[8,128]{1,0:T(8,128)S(1)} collective-permute-done((f32[8,128]{1,0:T(8,128)S(1)}, f32[8,128]{1,0:T(8,128)S(1)}, u32[]{:S(2)}, u32[]{:S(2)}) %collective-permute-start.5) | collective-permute-done | bytes 4128 | tf_op jit(solution)/shard_map/ppermute | solution.py:518
  27.2 1.1 %collective-permute-start.6 = (f32[8,128]{1,0:T(8,128)S(1)}, f32[8,128]{1,0:T(8,128)S(1)}, u32[]{:S(2)}, u32[]{:S(2)}) collective-permute-start(f32[8,128]{1,0:T(8,128)S(1)} %min.16), channel_id=1, source_target_pairs={{0,16},{8,24},{16,0},{24,8},{1,17},{9,25},{17,1},{25,9},{2,18},{10... | collective-permute-start | bytes 12296 | tf_op jit(solution)/shard_map/ppermute | solution.py:518
  28.3 2.4 %shard_map.115 = (bf16[1024,1024]{1,0:T(8,128)(2,1)S(1)}, f32[512,1024]{1,0:T(8,128)S(1)}, f32[512,128]{1,0:T(8,128)S(1)}) custom-call(s32[8,8]{1,0:T(8,128)S(1)} %get-tuple-element.47.plan, f32[1024,384]{1,0:T(8,128)S(1)} %get-tuple-element.48.columns, f32[1024,1024]{1,0:T(8,128)S(1)} %get-tuple-element.70.distance, ...), custom_call_target="tpu_custom_call" | custom-call | flops 100000000 | bytes 200000 | tf_op jit(solution)/shard_map/pallas_call | solution.py:505
  30.7 0.1 collective-permute-done.6
  30.9 1.5 %collective-permute-start.7 = (f32[8,128]{1,0:T(8,128)S(1)}, f32[8,128]{1,0:T(8,128)S(1)}, u32[]{:S(2)}, u32[]{:S(2)}) collective-permute-start(f32[8,128]{1,0:T(8,128)S(1)} %min.17), channel_id=1, source_target_pairs={{0,8},{8,0},{16,24},{24,16},{1,9},{9,1},{17,25},{25,17},{2,10},{10... | collective-permute-start | bytes 12296 | tf_op jit(solution)/shard_map/ppermute | solution.py:518
  32.3 2.6 %shard_map.116 = (bf16[1024,1024]{1,0:T(8,128)(2,1)S(1)}, f32[512,1024]{1,0:T(8,128)S(1)}, f32[512,128]{1,0:T(8,128)S(1)}) custom-call(s32[8,8]{1,0:T(8,128)S(1)} %get-tuple-element.47.plan, f32[1024,384]{1,0:T(8,128)S(1)} %get-tuple-element.48.columns, f32[1024,1024]{1,0:T(8,128)S(1)} %get-tuple-element.70.distance, ...), custom_call_target="tpu_custom_call" | custom-call | flops 100000000 | bytes 200000 | tf_op jit(solution)/shard_map/pallas_call | solution.py:505
  34.9 0.0 collective-permute-done.7
  35.0 0.0 collective-permute-done.8.s0
  35.0 0.0 collective-permute-done.9.s1
  35.0 0.0 collective-permute-done.10.s2
  35.0 0.0 collective-permute-done.11.s3
  35.0 2.0 %collective-permute-start.12 = (f32[8,128]{1,0:T(8,128)S(1)}, f32[8,128]{1,0:T(8,128)S(1)}, u32[]{:S(2)}, u32[]{:S(2)}) collective-permute-start(f32[8,128]{1,0:T(8,128)S(1)} %min.18), channel_id=1, source_target_pairs={{0,2},{1,3},{2,0},{3,1},{4,6},{5,7},{6,4},{7,5},{8,10},{9,11},{10,... | collective-permute-start | bytes 12296 | tf_op jit(solution)/shard_map/ppermute | solution.py:518
  37.0 5.5 %shard_map.117 = (f32[3,1024]{1,0:T(4,128)}, f32[8,128]{1,0:T(8,128)}) custom-call(s32[8,8]{1,0:T(8,128)S(1)} %get-tuple-element.47.plan, bf16[1024,1024]{1,0:T(8,128)(2,1)S(1)} %get-tuple-element.66.weights_a, f32[512,1024]{1,0:T(8,128)S(1)} %get-tuple-element.67.damping_a, f32[512,128]{1,0:T(8,128)S(1)} %get-tuple-element.68.dens_col_a, ...), custom_call_target="tpu_custom_call" | custom-call | flops 5000000000 | bytes 200000 | tf_op jit(solution)/shard_map/pallas_call | solution.py:505
  42.5 0.0 collective-permute-done.12
  42.5 0.6 %divide_bitcast_fusion = f32[1024]{0:T(1024)} fusion(f32[8,128]{1,0:T(8,128)S(1)} %get-tuple-element.87, f32[8,128]{1,0:T(8,128)S(1)} %min.18, f32[8,128]{1,0:T(8,128)S(1)} %collective-permute-done.12), kind=kLoop, calls=%fused_computation | loop fusion | flops 2048 | bytes 16384 | tf_op jit(solution)/shard_map/reshape | solution.py:615
  (4 shorter events, 0.0 us)
Async XLA Ops:
  2.2 11.5 %collective-permute-start = (f32[72,128]{1,0:T(8,128)}, f32[72,128]{1,0:T(8,128)S(1)}, u32[]{:S(2)}, u32[]{:S(2)}) collective-permute-start(f32[72,128]{1,0:T(8,128)} %get-tuple-element.51), channel_id=1, source_target_pairs={{0,1},{1,0},{2,3},{3,2},{4,5},{5,4},{6,7},{7,6},{8,9},{9,8},{10,11... | collective-permute-start | bytes 110600 | tf_op jit(solution)/shard_map/ppermute | solution.py:38
  2.6 11.0 %collective-permute-start.1 = (f32[72,128]{1,0:T(8,128)}, f32[72,128]{1,0:T(8,128)S(1)}, u32[]{:S(2)}, u32[]{:S(2)}) collective-permute-start(f32[72,128]{1,0:T(8,128)} %get-tuple-element.52), channel_id=1, source_target_pairs={{0,8},{8,0},{16,24},{24,16},{1,9},{9,1},{17,25},{25,17},{2,10},{10... | collective-permute-start | bytes 110600 | tf_op jit(solution)/shard_map/ppermute | solution.py:38
  5.2 8.5 %collective-permute-start.2 = (f32[72,128]{1,0:T(8,128)}, f32[72,128]{1,0:T(8,128)S(1)}, u32[]{:S(2)}, u32[]{:S(2)}) collective-permute-start(f32[72,128]{1,0:T(8,128)} %get-tuple-element.53), channel_id=1, source_target_pairs={{0,7},{1,2},{2,1},{3,4},{4,3},{5,6},{6,5},{7,0},{8,15},{9,10},{10,... | collective-permute-start | bytes 110600 | tf_op jit(solution)/shard_map/ppermute | solution.py:38
  8.6 5.1 %collective-permute-start.3 = (f32[72,128]{1,0:T(8,128)}, f32[72,128]{1,0:T(8,128)S(1)}, u32[]{:S(2)}, u32[]{:S(2)}) collective-permute-start(f32[72,128]{1,0:T(8,128)} %get-tuple-element.54), channel_id=1, source_target_pairs={{0,24},{8,16},{16,8},{24,0},{1,25},{9,17},{17,9},{25,1},{2,26},{10... | collective-permute-start | bytes 110600 | tf_op jit(solution)/shard_map/ppermute | solution.py:38
  10.1 0.8 %copy-start = (f32[80,128]{1,0:T(8,128)S(1)}, f32[80,128]{1,0:T(8,128)}, u32[]{:S(2)}) copy-start(f32[80,128]{1,0:T(8,128)} %get-tuple-element.46.own) | copy-start | bytes 122884
  10.8 0.7 %copy-start.1 = (s32[8,8]{1,0:T(8,128)S(1)}, s32[8,8]{1,0:T(8,128)}, u32[]{:S(2)}) copy-start(s32[8,8]{1,0:T(8,128)} %pairs.1) | copy-start | bytes 772
  13.7 4.0 %copy-start.2 = (s32[4,1]{0,1:T(1,128)S(1)}, s32[4,1]{0,1:T(1,128)}, u32[]{:S(2)}) copy-start(s32[4,1]{0,1:T(1,128)} %param.13) | copy-start | bytes 52
  13.7 4.0 %copy-start.3 = (s32[4,1]{0,1:T(1,128)S(1)}, s32[4,1]{0,1:T(1,128)}, u32[]{:S(2)}) copy-start(s32[4,1]{0,1:T(1,128)} %param.14) | copy-start | bytes 52
  17.6 5.0 %collective-permute-start.4 = (f32[8,128]{1,0:T(8,128)S(1)}, f32[8,128]{1,0:T(8,128)S(1)}, u32[]{:S(2)}, u32[]{:S(2)}) collective-permute-start(f32[8,128]{1,0:T(8,128)S(1)} %get-tuple-element.57), channel_id=1, source_target_pairs={{0,4},{1,5},{2,6},{3,7},{4,0},{5,1},{6,2},{7,3},{8,12},{9,13},{10,... | collective-permute-start | bytes 12296 | tf_op jit(solution)/shard_map/ppermute | solution.py:518
  22.6 12.4 %collective-permute-start.8 = (f32[64,128]{1,0:T(8,128)S(1)}, f32[64,128]{1,0:T(8,128)S(1)}, u32[]{:S(2)}, u32[]{:S(2)}) collective-permute-start(f32[64,128]{1,0:T(8,128)S(1)} %get-tuple-element.76), channel_id=1, source_target_pairs={{0,1},{1,0},{2,3},{3,2},{4,5},{5,4},{6,7},{7,6},{8,9},{9,8},{10,11... | collective-permute-start | bytes 98312 | tf_op jit(solution)/shard_map/ppermute | solution.py:38
  22.9 12.1 %collective-permute-start.9 = (f32[64,128]{1,0:T(8,128)S(1)}, f32[64,128]{1,0:T(8,128)S(1)}, u32[]{:S(2)}, u32[]{:S(2)}) collective-permute-start(f32[64,128]{1,0:T(8,128)S(1)} %get-tuple-element.77), channel_id=1, source_target_pairs={{0,8},{8,0},{16,24},{24,16},{1,9},{9,1},{17,25},{25,17},{2,10},{10... | collective-permute-start | bytes 98312 | tf_op jit(solution)/shard_map/ppermute | solution.py:38
  24.4 10.6 %collective-permute-start.10 = (f32[64,128]{1,0:T(8,128)S(1)}, f32[64,128]{1,0:T(8,128)S(1)}, u32[]{:S(2)}, u32[]{:S(2)}) collective-permute-start(f32[64,128]{1,0:T(8,128)S(1)} %get-tuple-element.78), channel_id=1, source_target_pairs={{0,7},{1,2},{2,1},{3,4},{4,3},{5,6},{6,5},{7,0},{8,15},{9,10},{10,... | collective-permute-start | bytes 98312 | tf_op jit(solution)/shard_map/ppermute | solution.py:38
  25.1 9.9 %collective-permute-start.11 = (f32[64,128]{1,0:T(8,128)S(1)}, f32[64,128]{1,0:T(8,128)S(1)}, u32[]{:S(2)}, u32[]{:S(2)}) collective-permute-start(f32[64,128]{1,0:T(8,128)S(1)} %get-tuple-element.79), channel_id=1, source_target_pairs={{0,24},{8,16},{16,8},{24,0},{1,25},{9,17},{17,9},{25,1},{2,26},{10... | collective-permute-start | bytes 98312 | tf_op jit(solution)/shard_map/ppermute | solution.py:38
  26.1 1.2 %collective-permute-start.5 = (f32[8,128]{1,0:T(8,128)S(1)}, f32[8,128]{1,0:T(8,128)S(1)}, u32[]{:S(2)}, u32[]{:S(2)}) collective-permute-start(f32[8,128]{1,0:T(8,128)S(1)} %min.15), channel_id=1, source_target_pairs={{0,1},{1,0},{2,3},{3,2},{4,5},{5,4},{6,7},{7,6},{8,9},{9,8},{10,11... | collective-permute-start | bytes 12296 | tf_op jit(solution)/shard_map/ppermute | solution.py:518
  27.2 3.6 %collective-permute-start.6 = (f32[8,128]{1,0:T(8,128)S(1)}, f32[8,128]{1,0:T(8,128)S(1)}, u32[]{:S(2)}, u32[]{:S(2)}) collective-permute-start(f32[8,128]{1,0:T(8,128)S(1)} %min.16), channel_id=1, source_target_pairs={{0,16},{8,24},{16,0},{24,8},{1,17},{9,25},{17,1},{25,9},{2,18},{10... | collective-permute-start | bytes 12296 | tf_op jit(solution)/shard_map/ppermute | solution.py:518
  30.9 4.1 %collective-permute-start.7 = (f32[8,128]{1,0:T(8,128)S(1)}, f32[8,128]{1,0:T(8,128)S(1)}, u32[]{:S(2)}, u32[]{:S(2)}) collective-permute-start(f32[8,128]{1,0:T(8,128)S(1)} %min.17), channel_id=1, source_target_pairs={{0,8},{8,0},{16,24},{24,16},{1,9},{9,1},{17,25},{25,17},{2,10},{10... | collective-permute-start | bytes 12296 | tf_op jit(solution)/shard_map/ppermute | solution.py:518
  35.0 7.5 %collective-permute-start.12 = (f32[8,128]{1,0:T(8,128)S(1)}, f32[8,128]{1,0:T(8,128)S(1)}, u32[]{:S(2)}, u32[]{:S(2)}) collective-permute-start(f32[8,128]{1,0:T(8,128)S(1)} %min.18), channel_id=1, source_target_pairs={{0,2},{1,3},{2,0},{3,1},{4,6},{5,7},{6,4},{7,5},{8,10},{9,11},{10,... | collective-permute-start | bytes 12296 | tf_op jit(solution)/shard_map/ppermute | solution.py:518

commit v4 on v3

--- a/solution.py
+++ b/solution.py
@@ -149,9 +149,9 @@
         part = slice(block * lanes, (block + 1) * lanes)
         at = block * rows
         own[at : at + 3, :] = positions[:, part]
-        own[at + 3 : at + 4, :] = smoothing[block : block + 1, :]
         own[at + 4 : at + 7, :] = velocities[:, part]
-        own[at + 7 : at + 8, :] = sound[block : block + 1, :]
+    own[pl.ds(3, 8, stride=rows), :] = smoothing[...]
+    own[pl.ds(7, 8, stride=rows), :] = sound
     own[64:72, :] = mass[...]
     own[72:80, :] = energy[...]
     cut_windows(lambda r: offsets[0, r], lambda r: counts[0, r], own, outgoing, True)
@@ -331,9 +331,7 @@
     fields = [dens, pressure, cof_xx * inv_det, cof_yy * inv_det, cof_zz * inv_det]
     fields += [cof_xy * inv_det, cof_xz * inv_det, cof_yz * inv_det]
     for field in range(8):
-        for block in range(8):
-            at = block * rows + field
-            second[at : at + 1, :] = fields[field][block : block + 1, :]
+        second[pl.ds(field, 8, stride=rows), :] = fields[field]
     cut_windows(lambda r: offsets[0, r], lambda r: counts[0, r], second, outgoing, False)
 
 
@@ -370,11 +368,11 @@
                 weights[pl.ds(base + lanes, chunk), part] = low
         return 0
 
-    lax.fori_loop(0, 4, step, 0, unroll=2)
+    lax.fori_loop(0, 8, step, 0, unroll=2)
 
 
 def momentum_kernel(
-    plan, weights_a, damping_a, dens_col_a, weights_b, damping_b, dens_col_b,
+    plan, weights, damping, dens_col,
     own, m0, m1, m2, m3, second, s0, s1, s2, s3, accel, heating, *scratch
 ):
     table, masses, table2, sums, *scratch = scratch
@@ -383,12 +381,15 @@
     fill_mass(own, (m0, m1, m2, m3), masses)
     fill_table(second, (s0, s1, s2, s3), table2, rows)
     ids = row_ids()
+    picks = []
+    for picked in ((2, 5, 6, 2), (5, 3, 7, 3), (6, 7, 4, 4)):
+        places = jnp.full((rows, lanes), picked[3], jnp.int32)
+        for at in range(3):
+            places = jnp.where(lax.rem(ids, 4) == at, picked[at], places)
+        picks.append(places)
 
     def features(tile, extra, mass):
-        cols = [
-            jnp.concatenate([extra[i : i + 1] for i in picked], axis=0)
-            for picked in ((2, 5, 6, 2, 2, 5, 6, 2), (5, 3, 7, 3, 5, 3, 7, 3), (6, 7, 4, 4, 6, 7, 4, 4))
-        ]
+        cols = [jnp.take_along_axis(extra, places, axis=0) for places in picks]
         heavy = tile * mass
         applied = None
         for axis in range(3):
@@ -436,8 +437,7 @@
             at = pl.ds(pl.multiple_of(block * lanes + base, 64), 64)
             sums[at, :] = out[0:64] + out[64:128]
 
-    two_deep(prepare, functools.partial(finish_part, weights_a, damping_a, dens_col_a, 0), 0, 4)
-    two_deep(prepare, functools.partial(finish_part, weights_b, damping_b, dens_col_b, 4), 4, 8)
+    two_deep(prepare, functools.partial(finish_part, weights, damping, dens_col, 0))
 
     def mine(ref, field):
         return ref[pl.ds(field, 8, stride=rows), :]
@@ -581,17 +581,17 @@
     )
     smallest, outgoing2 = lax.optimization_barrier((smallest, outgoing2))
     received2 = [swap(value, axis, odd) for value, (axis, odd, _) in zip(outgoing2, swaps)]
-    smallest = fold(smallest, *steps[1])
     parts = []
-    for first in (0, 4):
-        smallest = fold(smallest, *steps[2 + first // 4])
+    smallest = fold(smallest, *steps[2])
+    for first in (0,):
+        smallest = fold(smallest, *steps[3])
         weights, damping, dens_col = call(
             functools.partial(weight_kernel, first),
-            [((8 * lanes, 8 * lanes), bf16), ((4 * lanes, 8 * lanes), f32), ((4 * lanes, lanes), f32)],
+            [((16 * lanes, 8 * lanes), bf16), ((8 * lanes, 8 * lanes), f32), ((8 * lanes, lanes), f32)],
             [table],
             1,
             (plan, columns, distance, rates, second, own, *received),
-            10**8,
+            10**9,
             20,
         )
         smallest, distance, weights = lax.optimization_barrier((smallest, distance, weights))
@@ -611,6 +611,8 @@
         20,
     )
     smallest = fold(smallest, *steps[-1])
+    smallest, accel = lax.optimization_barrier((smallest, accel))
+    smallest = fold(smallest, *steps[1])
     share = smallest / allowed
     return (density.reshape(points), accel, heating.reshape(points), share.reshape(points))
 

time: 43.4 us -> 41.7 us (0.961)
  Pallas kernels: 23 us -> 22 us
  starting transfers between devices: 16.3 us -> 15.8 us
    pallas_call x5 -> x4, Pallas kernels: 19.3 us -> 18.3 us  [call(): pl.pallas_call(kernel, out_shape=[jax.ShapeDtypeStruct(shape, kind) for s...]
    ppermute x8, starting transfers between devices: 11.4 us -> 10.6 us  [swap(): return lax.ppermute(value, axis, pairs)]
  transfers between devices with their start and end apart: 13 -> 13, of which waited for: 2 -> 1; matrix products, arithmetic and copies ran while one was open for 0% -> 0% of each run, Pallas kernels for 41% -> 40%
where the time goes in v4:
time: 41.7 us; the launch traced here: 41.4 us
  Pallas kernels  22 us (53%)
  starting transfers between devices  15.8 us (38%)
  local copies, waits for them, and re-layouts  1.48 us (4%)
  waiting for transfers between devices  0.86 us (2%)
  between operations  0.77 us (2%)
  other arithmetic  0.61 us (1%)
    pallas_call x4, Pallas kernels, call(): pl.pallas_call(kernel, out_shape=[jax.ShapeDtypeStruct(shape, kind) for s...  18.3 us
    ppermute x8, starting transfers between devices, swap(): return lax.ppermute(value, axis, pairs)  10.6 us
    ppermute x5, starting transfers between devices, fold(): lax.ppermute(value, axis, [(i, i ^ step) for i in range(size)])  5.18 us
    pallas_call x1, Pallas kernels, body(): pl.pallas_call(own_kernel, out_shape=[jax.ShapeDtypeStruct((8 * lanes, la...  2.13 us
    pallas_call x1, Pallas kernels, body(): pl.pallas_call(pack_kernel, out_shape=[jax.ShapeDtypeStruct((80, lanes),...  1.57 us
    unnamed x8, local copies, waits for them, and re-layouts  1.48 us
  transfers between devices with their start and end apart: 13, of which 1 were waited for; matrix products, arithmetic and copies ran while one was open for 0% of the time, Pallas kernels for 40%

profile of v4, /device:TPU:0, one launch (start us, length us, event | category | flops | bytes accessed | tf_op | source)
XLA Modules:
  0.0 41.4 jit_solution(16166784198631285915)
XLA Ops:
  0.6 1.6 %shard_map.111 = (f32[80,128]{1,0:T(8,128)}, f32[72,128]{1,0:T(8,128)}, f32[72,128]{1,0:T(8,128)}, f32[72,128]{1,0:T(8,128)}, f32[72,128]{1,0:T(8,128)}) custom-call(f32[3,1024]{1,0:T(4,128)} %positions.1, f32[3,1024]{1,0:T(4,128)} %velocities.1, f32[8,128]{1,0:T(8,128)} %bitcast.13, f32[8,128]{1,0:T(8,128)} %bitcast.14, f32[8,128]{1,0:T(8,128)} %bitcast.15, ...), custom_call_target="tpu_custom_call" | custom-call | tf_op jit(solution)/shard_map/pallas_call | solution.py:526
  2.2 0.5 %collective-permute-start = (f32[72,128]{1,0:T(8,128)}, f32[72,128]{1,0:T(8,128)S(1)}, u32[]{:S(2)}, u32[]{:S(2)}) collective-permute-start(f32[72,128]{1,0:T(8,128)} %get-tuple-element.47), channel_id=1, source_target_pairs={{0,1},{1,0},{2,3},{3,2},{4,5},{5,4},{6,7},{7,6},{8,9},{9,8},{10,11... | collective-permute-start | bytes 110600 | tf_op jit(solution)/shard_map/ppermute | solution.py:38
  2.7 2.5 %collective-permute-start.1 = (f32[72,128]{1,0:T(8,128)}, f32[72,128]{1,0:T(8,128)S(1)}, u32[]{:S(2)}, u32[]{:S(2)}) collective-permute-start(f32[72,128]{1,0:T(8,128)} %get-tuple-element.48), channel_id=1, source_target_pairs={{0,8},{8,0},{16,24},{24,16},{1,9},{9,1},{17,25},{25,17},{2,10},{10... | collective-permute-start | bytes 110600 | tf_op jit(solution)/shard_map/ppermute | solution.py:38
  5.2 3.4 %collective-permute-start.2 = (f32[72,128]{1,0:T(8,128)}, f32[72,128]{1,0:T(8,128)S(1)}, u32[]{:S(2)}, u32[]{:S(2)}) collective-permute-start(f32[72,128]{1,0:T(8,128)} %get-tuple-element.49), channel_id=1, source_target_pairs={{0,7},{1,2},{2,1},{3,4},{4,3},{5,6},{6,5},{7,0},{8,15},{9,10},{10,... | collective-permute-start | bytes 110600 | tf_op jit(solution)/shard_map/ppermute | solution.py:38
  8.6 1.5 %collective-permute-start.3 = (f32[72,128]{1,0:T(8,128)}, f32[72,128]{1,0:T(8,128)S(1)}, u32[]{:S(2)}, u32[]{:S(2)}) collective-permute-start(f32[72,128]{1,0:T(8,128)} %get-tuple-element.50), channel_id=1, source_target_pairs={{0,24},{8,16},{16,8},{24,0},{1,25},{9,17},{17,9},{25,1},{2,26},{10... | collective-permute-start | bytes 110600 | tf_op jit(solution)/shard_map/ppermute | solution.py:38
  10.1 0.0 copy-start
  10.1 0.8 %copy-done = f32[80,128]{1,0:T(8,128)S(1)} copy-done((f32[80,128]{1,0:T(8,128)S(1)}, f32[80,128]{1,0:T(8,128)}, u32[]{:S(2)}) %copy-start) | copy-done | bytes 40984
  10.8 0.0 copy-start.1
  10.9 0.7 %copy-done.1 = s32[8,8]{1,0:T(8,128)S(1)} copy-done((s32[8,8]{1,0:T(8,128)S(1)}, s32[8,8]{1,0:T(8,128)}, u32[]{:S(2)}) %copy-start.1) | copy-done | bytes 280
  11.5 2.1 %shard_map.112 = (bf16[1024,128]{1,0:T(8,128)(2,1)S(1)}, f32[1024,384]{1,0:T(8,128)S(1)}, f32[80,128]{1,0:T(8,128)S(1)}, s32[8,8]{1,0:T(8,128)S(1)}) custom-call(s32[8,8]{1,0:T(8,128)S(1)} %copy-done.1, f32[80,128]{1,0:T(8,128)S(1)} %copy-done), custom_call_target="tpu_custom_call" | custom-call | tf_op jit(solution)/shard_map/pallas_call | solution.py:545
  13.7 0.0 collective-permute-done.m0
  13.7 0.0 collective-permute-done.1.m1
  13.7 0.0 collective-permute-done.2.m2
  13.7 0.0 collective-permute-done.3.m3
  13.7 0.0 copy-start.2
  13.7 0.0 copy-start.3
  13.7 3.9 %shard_map.113 = (f32[8,128]{1,0:T(8,128)S(1)}, f32[8,128]{1,0:T(8,128)S(1)}, f32[1024,1024]{1,0:T(8,128)S(1)}, f32[1024,1024]{1,0:T(8,128)S(1)}) custom-call(s32[8,8]{1,0:T(8,128)S(1)} %get-tuple-element.43.plan, bf16[1024,128]{1,0:T(8,128)(2,1)S(1)} %get-tuple-element.45.left, f32[1024,384]{1,0:T(8,128)S(1)} %get-tuple-element.44.columns, ...), custom_call_target="tpu_custom_call" | custom-call | flops 3000000000 | bytes 200000 | tf_op jit(solution)/shard_map/pallas_call | solution.py:505
  17.6 0.1 collective-permute-start.4
  17.7 0.0 copy-done.2
  17.7 0.0 copy-done.3
  17.7 5.0 %shard_map.114 = (f32[8,128]{1,0:T(8,128)}, f32[64,128]{1,0:T(8,128)S(1)}, f32[64,128]{1,0:T(8,128)S(1)}, f32[64,128]{1,0:T(8,128)S(1)}, f32[64,128]{1,0:T(8,128)S(1)}, /*index=5*/f32[64,128]{1,0:T(8,128)S(1)}) custom-call(s32[8,8]{1,0:T(8,128)S(1)} %get-tuple-element.43.plan, s32[1,4]{1,0:T(1,128)S(1)} %bitcast.10, s32[1,4]{1,0:T(1,128)S(1)} %bitcast.12, ...), custom_call_target="tpu_custom_call" | custom-call | flops 5000000000 | bytes 200000 | tf_op jit(solution)/shard_map/pallas_call | solution.py:505
  22.7 0.0 collective-permute-done.4
  22.7 1.5 %collective-permute-start.5 = (f32[8,128]{1,0:T(8,128)S(1)}, f32[8,128]{1,0:T(8,128)S(1)}, u32[]{:S(2)}, u32[]{:S(2)}) collective-permute-start(f32[8,128]{1,0:T(8,128)S(1)} %min.15), channel_id=1, source_target_pairs={{0,16},{8,24},{16,0},{24,8},{1,17},{9,25},{17,1},{25,9},{2,18},{10... | collective-permute-start | bytes 12296 | tf_op jit(solution)/shard_map/ppermute | solution.py:518
  24.1 0.0 collective-permute-start.7
  24.1 0.6 %collective-permute-start.8 = (f32[64,128]{1,0:T(8,128)S(1)}, f32[64,128]{1,0:T(8,128)S(1)}, u32[]{:S(2)}, u32[]{:S(2)}) collective-permute-start(f32[64,128]{1,0:T(8,128)S(1)} %get-tuple-element.64), channel_id=1, source_target_pairs={{0,8},{8,0},{16,24},{24,16},{1,9},{9,1},{17,25},{25,17},{2,10},{10... | collective-permute-start | bytes 98312 | tf_op jit(solution)/shard_map/ppermute | solution.py:38
  24.7 0.7 %collective-permute-start.9 = (f32[64,128]{1,0:T(8,128)S(1)}, f32[64,128]{1,0:T(8,128)S(1)}, u32[]{:S(2)}, u32[]{:S(2)}) collective-permute-start(f32[64,128]{1,0:T(8,128)S(1)} %get-tuple-element.65), channel_id=1, source_target_pairs={{0,7},{1,2},{2,1},{3,4},{4,3},{5,6},{6,5},{7,0},{8,15},{9,10},{10,... | collective-permute-start | bytes 98312 | tf_op jit(solution)/shard_map/ppermute | solution.py:38
  25.4 1.5 %collective-permute-start.10 = (f32[64,128]{1,0:T(8,128)S(1)}, f32[64,128]{1,0:T(8,128)S(1)}, u32[]{:S(2)}, u32[]{:S(2)}) collective-permute-start(f32[64,128]{1,0:T(8,128)S(1)} %get-tuple-element.66), channel_id=1, source_target_pairs={{0,24},{8,16},{16,8},{24,0},{1,25},{9,17},{17,9},{25,1},{2,26},{10... | collective-permute-start | bytes 98312 | tf_op jit(solution)/shard_map/ppermute | solution.py:38
  26.9 0.0 collective-permute-done.5
  26.9 1.5 %collective-permute-start.6 = (f32[8,128]{1,0:T(8,128)S(1)}, f32[8,128]{1,0:T(8,128)S(1)}, u32[]{:S(2)}, u32[]{:S(2)}) collective-permute-start(f32[8,128]{1,0:T(8,128)S(1)} %min.16), channel_id=1, source_target_pairs={{0,8},{8,0},{16,24},{24,16},{1,9},{9,1},{17,25},{25,17},{2,10},{10... | collective-permute-start | bytes 12296 | tf_op jit(solution)/shard_map/ppermute | solution.py:518
  28.4 4.2 %shard_map.115 = (bf16[2048,1024]{1,0:T(8,128)(2,1)S(1)}, f32[1024,1024]{1,0:T(8,128)S(1)}, f32[1024,128]{1,0:T(8,128)S(1)}) custom-call(s32[8,8]{1,0:T(8,128)S(1)} %get-tuple-element.43.plan, f32[1024,384]{1,0:T(8,128)S(1)} %get-tuple-element.44.columns, f32[1024,1024]{1,0:T(8,128)S(1)} %get-tuple-element.51.distance, ...), custom_call_target="tpu_custom_call" | custom-call | flops 1000000000 | bytes 200000 | tf_op jit(solution)/shard_map/pallas_call | solution.py:505
  32.7 0.0 collective-permute-done.6
  32.7 0.0 collective-permute-done.7.s0
  32.7 0.0 collective-permute-done.8.s1
  32.7 0.0 collective-permute-done.9.s2
  32.7 0.0 collective-permute-done.10.s3
  32.7 1.2 %collective-permute-start.11 = (f32[8,128]{1,0:T(8,128)S(1)}, f32[8,128]{1,0:T(8,128)S(1)}, u32[]{:S(2)}, u32[]{:S(2)}) collective-permute-start(f32[8,128]{1,0:T(8,128)S(1)} %min.17), channel_id=1, source_target_pairs={{0,2},{1,3},{2,0},{3,1},{4,6},{5,7},{6,4},{7,5},{8,10},{9,11},{10,... | collective-permute-start | bytes 12296 | tf_op jit(solution)/shard_map/ppermute | solution.py:518
  33.9 5.2 %shard_map.116 = (f32[3,1024]{1,0:T(4,128)}, f32[8,128]{1,0:T(8,128)}) custom-call(s32[8,8]{1,0:T(8,128)S(1)} %get-tuple-element.43.plan, bf16[2048,1024]{1,0:T(8,128)(2,1)S(1)} %get-tuple-element.68.weights, f32[1024,1024]{1,0:T(8,128)S(1)} %get-tuple-element.69.damping, f32[1024,128]{1,0:T(8,128)S(1)} %get-tuple-element.70.dens_col, ...), custom_call_target="tpu_custom_call" | custom-call | flops 5000000000 | bytes 200000 | tf_op jit(solution)/shard_map/pallas_call | solution.py:505
  39.1 0.0 collective-permute-done.11
  39.1 0.9 %collective-permute-start.12 = (f32[8,128]{1,0:T(8,128)S(1)}, f32[8,128]{1,0:T(8,128)S(1)}, u32[]{:S(2)}, u32[]{:S(2)}) collective-permute-start(f32[8,128]{1,0:T(8,128)S(1)} %min.18), channel_id=1, source_target_pairs={{0,1},{1,0},{2,3},{3,2},{4,5},{5,4},{6,7},{7,6},{8,9},{9,8},{10,11... | collective-permute-start | bytes 12296 | tf_op jit(solution)/shard_map/ppermute | solution.py:518
  40.0 0.8 %collective-permute-done.12 = f32[8,128]{1,0:T(8,128)S(1)} collective-permute-done((f32[8,128]{1,0:T(8,128)S(1)}, f32[8,128]{1,0:T(8,128)S(1)}, u32[]{:S(2)}, u32[]{:S(2)}) %collective-permute-start.12) | collective-permute-done | bytes 4128 | tf_op jit(solution)/shard_map/ppermute | solution.py:518
  40.8 0.6 %divide_bitcast_fusion = f32[1024]{0:T(1024)} fusion(f32[8,128]{1,0:T(8,128)S(1)} %get-tuple-element.79, f32[8,128]{1,0:T(8,128)S(1)} %min.18, f32[8,128]{1,0:T(8,128)S(1)} %collective-permute-done.12), kind=kLoop, calls=%fused_computation | loop fusion | flops 2048 | bytes 16384 | tf_op jit(solution)/shard_map/reshape | solution.py:617
  (4 shorter events, 0.0 us)
Async XLA Ops:
  2.2 11.5 %collective-permute-start = (f32[72,128]{1,0:T(8,128)}, f32[72,128]{1,0:T(8,128)S(1)}, u32[]{:S(2)}, u32[]{:S(2)}) collective-permute-start(f32[72,128]{1,0:T(8,128)} %get-tuple-element.47), channel_id=1, source_target_pairs={{0,1},{1,0},{2,3},{3,2},{4,5},{5,4},{6,7},{7,6},{8,9},{9,8},{10,11... | collective-permute-start | bytes 110600 | tf_op jit(solution)/shard_map/ppermute | solution.py:38
  2.7 11.0 %collective-permute-start.1 = (f32[72,128]{1,0:T(8,128)}, f32[72,128]{1,0:T(8,128)S(1)}, u32[]{:S(2)}, u32[]{:S(2)}) collective-permute-start(f32[72,128]{1,0:T(8,128)} %get-tuple-element.48), channel_id=1, source_target_pairs={{0,8},{8,0},{16,24},{24,16},{1,9},{9,1},{17,25},{25,17},{2,10},{10... | collective-permute-start | bytes 110600 | tf_op jit(solution)/shard_map/ppermute | solution.py:38
  5.2 8.5 %collective-permute-start.2 = (f32[72,128]{1,0:T(8,128)}, f32[72,128]{1,0:T(8,128)S(1)}, u32[]{:S(2)}, u32[]{:S(2)}) collective-permute-start(f32[72,128]{1,0:T(8,128)} %get-tuple-element.49), channel_id=1, source_target_pairs={{0,7},{1,2},{2,1},{3,4},{4,3},{5,6},{6,5},{7,0},{8,15},{9,10},{10,... | collective-permute-start | bytes 110600 | tf_op jit(solution)/shard_map/ppermute | solution.py:38
  8.6 5.1 %collective-permute-start.3 = (f32[72,128]{1,0:T(8,128)}, f32[72,128]{1,0:T(8,128)S(1)}, u32[]{:S(2)}, u32[]{:S(2)}) collective-permute-start(f32[72,128]{1,0:T(8,128)} %get-tuple-element.50), channel_id=1, source_target_pairs={{0,24},{8,16},{16,8},{24,0},{1,25},{9,17},{17,9},{25,1},{2,26},{10... | collective-permute-start | bytes 110600 | tf_op jit(solution)/shard_map/ppermute | solution.py:38
  10.1 0.8 %copy-start = (f32[80,128]{1,0:T(8,128)S(1)}, f32[80,128]{1,0:T(8,128)}, u32[]{:S(2)}) copy-start(f32[80,128]{1,0:T(8,128)} %get-tuple-element.42.own) | copy-start | bytes 122884
  10.8 0.7 %copy-start.1 = (s32[8,8]{1,0:T(8,128)S(1)}, s32[8,8]{1,0:T(8,128)}, u32[]{:S(2)}) copy-start(s32[8,8]{1,0:T(8,128)} %pairs.1) | copy-start | bytes 772
  13.7 4.0 %copy-start.2 = (s32[4,1]{0,1:T(1,128)S(1)}, s32[4,1]{0,1:T(1,128)}, u32[]{:S(2)}) copy-start(s32[4,1]{0,1:T(1,128)} %param.13) | copy-start | bytes 52
  13.7 4.0 %copy-start.3 = (s32[4,1]{0,1:T(1,128)S(1)}, s32[4,1]{0,1:T(1,128)}, u32[]{:S(2)}) copy-start(s32[4,1]{0,1:T(1,128)} %param.14) | copy-start | bytes 52
  17.6 5.1 %collective-permute-start.4 = (f32[8,128]{1,0:T(8,128)S(1)}, f32[8,128]{1,0:T(8,128)S(1)}, u32[]{:S(2)}, u32[]{:S(2)}) collective-permute-start(f32[8,128]{1,0:T(8,128)S(1)} %get-tuple-element.53), channel_id=1, source_target_pairs={{0,4},{1,5},{2,6},{3,7},{4,0},{5,1},{6,2},{7,3},{8,12},{9,13},{10,... | collective-permute-start | bytes 12296 | tf_op jit(solution)/shard_map/ppermute | solution.py:518
  22.7 4.2 %collective-permute-start.5 = (f32[8,128]{1,0:T(8,128)S(1)}, f32[8,128]{1,0:T(8,128)S(1)}, u32[]{:S(2)}, u32[]{:S(2)}) collective-permute-start(f32[8,128]{1,0:T(8,128)S(1)} %min.15), channel_id=1, source_target_pairs={{0,16},{8,24},{16,0},{24,8},{1,17},{9,25},{17,1},{25,9},{2,18},{10... | collective-permute-start | bytes 12296 | tf_op jit(solution)/shard_map/ppermute | solution.py:518
  24.1 8.5 %collective-permute-start.7 = (f32[64,128]{1,0:T(8,128)S(1)}, f32[64,128]{1,0:T(8,128)S(1)}, u32[]{:S(2)}, u32[]{:S(2)}) collective-permute-start(f32[64,128]{1,0:T(8,128)S(1)} %get-tuple-element.63), channel_id=1, source_target_pairs={{0,1},{1,0},{2,3},{3,2},{4,5},{5,4},{6,7},{7,6},{8,9},{9,8},{10,11... | collective-permute-start | bytes 98312 | tf_op jit(solution)/shard_map/ppermute | solution.py:38
  24.1 8.6 %collective-permute-start.8 = (f32[64,128]{1,0:T(8,128)S(1)}, f32[64,128]{1,0:T(8,128)S(1)}, u32[]{:S(2)}, u32[]{:S(2)}) collective-permute-start(f32[64,128]{1,0:T(8,128)S(1)} %get-tuple-element.64), channel_id=1, source_target_pairs={{0,8},{8,0},{16,24},{24,16},{1,9},{9,1},{17,25},{25,17},{2,10},{10... | collective-permute-start | bytes 98312 | tf_op jit(solution)/shard_map/ppermute | solution.py:38
  24.7 8.0 %collective-permute-start.9 = (f32[64,128]{1,0:T(8,128)S(1)}, f32[64,128]{1,0:T(8,128)S(1)}, u32[]{:S(2)}, u32[]{:S(2)}) collective-permute-start(f32[64,128]{1,0:T(8,128)S(1)} %get-tuple-element.65), channel_id=1, source_target_pairs={{0,7},{1,2},{2,1},{3,4},{4,3},{5,6},{6,5},{7,0},{8,15},{9,10},{10,... | collective-permute-start | bytes 98312 | tf_op jit(solution)/shard_map/ppermute | solution.py:38
  25.4 7.3 %collective-permute-start.10 = (f32[64,128]{1,0:T(8,128)S(1)}, f32[64,128]{1,0:T(8,128)S(1)}, u32[]{:S(2)}, u32[]{:S(2)}) collective-permute-start(f32[64,128]{1,0:T(8,128)S(1)} %get-tuple-element.66), channel_id=1, source_target_pairs={{0,24},{8,16},{16,8},{24,0},{1,25},{9,17},{17,9},{25,1},{2,26},{10... | collective-permute-start | bytes 98312 | tf_op jit(solution)/shard_map/ppermute | solution.py:38
  26.9 5.8 %collective-permute-start.6 = (f32[8,128]{1,0:T(8,128)S(1)}, f32[8,128]{1,0:T(8,128)S(1)}, u32[]{:S(2)}, u32[]{:S(2)}) collective-permute-start(f32[8,128]{1,0:T(8,128)S(1)} %min.16), channel_id=1, source_target_pairs={{0,8},{8,0},{16,24},{24,16},{1,9},{9,1},{17,25},{25,17},{2,10},{10... | collective-permute-start | bytes 12296 | tf_op jit(solution)/shard_map/ppermute | solution.py:518
  32.7 6.4 %collective-permute-start.11 = (f32[8,128]{1,0:T(8,128)S(1)}, f32[8,128]{1,0:T(8,128)S(1)}, u32[]{:S(2)}, u32[]{:S(2)}) collective-permute-start(f32[8,128]{1,0:T(8,128)S(1)} %min.17), channel_id=1, source_target_pairs={{0,2},{1,3},{2,0},{3,1},{4,6},{5,7},{6,4},{7,5},{8,10},{9,11},{10,... | collective-permute-start | bytes 12296 | tf_op jit(solution)/shard_map/ppermute | solution.py:518
  39.1 1.7 %collective-permute-start.12 = (f32[8,128]{1,0:T(8,128)S(1)}, f32[8,128]{1,0:T(8,128)S(1)}, u32[]{:S(2)}, u32[]{:S(2)}) collective-permute-start(f32[8,128]{1,0:T(8,128)S(1)} %min.18), channel_id=1, source_target_pairs={{0,1},{1,0},{2,3},{3,2},{4,5},{5,4},{6,7},{7,6},{8,9},{9,8},{10,11... | collective-permute-start | bytes 12296 | tf_op jit(solution)/shard_map/ppermute | solution.py:518

commit v5 on v4

--- a/solution.py
+++ b/solution.py
@@ -188,7 +188,7 @@
         columns[at, 2 * lanes :] = jnp.broadcast_to(0.5 / length, (lanes, lanes))
         return 0
 
-    lax.fori_loop(0, 8, step, 0)
+    lax.fori_loop(0, 8, step, 0, unroll=True)
 
 
 def put_near(near, k, tile):
@@ -203,8 +203,8 @@
         near[...] = jnp.zeros(near.shape, bf16)
 
 
-def pair_dots(left, near, block, start, k):
-    at = pl.ds(pl.multiple_of(block * lanes + start, chunk), chunk)
+def pair_dots(left, near, block, k):
+    at = pl.ds(pl.multiple_of(block * lanes, lanes), lanes)
     part = slice(2 * k * lanes, 2 * (k + 1) * lanes)
     both = jnp.dot(left[at, :], near[:, part], preferred_element_type=f32)
     return both[:, 0:lanes], both[:, lanes:]
@@ -222,25 +222,23 @@
             put_near(near[buf], k, tile_at(table, plan[k, block]) - centre)
 
     def finish(block, buf):
-        tops = [None] * (lanes // chunk)
+        best = None
         sounds = None
         for k in range(8):
             tile = tile_at(table, plan[k, block])
             len_row, sound_row = tile[3:4] * 0.05, tile[7:8]
             sounds = sound_row if k == 0 else jnp.maximum(sounds, sound_row)
             part = slice(k * lanes, (k + 1) * lanes)
-            for c in range(lanes // chunk):
-                start = c * chunk
-                at = pl.ds(pl.multiple_of(block * lanes + start, chunk), chunk)
-                dist_sq, closing = pair_dots(left, near[buf], block, start, k)
-                dist_sq = jnp.maximum(dist_sq, tiny)
-                distance[at, part] = dist_sq * lax.rsqrt(dist_sq)
-                mean_len = columns[at, 0:lanes] + len_row
-                rate = closing * mean_len / (dist_sq + mean_len * mean_len)
-                rates[at, part] = rate
-                signal = sound_row - rate
-                tops[c] = signal if k == 0 else jnp.maximum(tops[c], signal)
-        top = jnp.max(jnp.concatenate(tops, axis=0).T, axis=0, keepdims=True)
+            at = pl.ds(pl.multiple_of(block * lanes, lanes), lanes)
+            dist_sq, closing = pair_dots(left, near[buf], block, k)
+            dist_sq = jnp.maximum(dist_sq, tiny)
+            distance[at, part] = dist_sq * lax.rsqrt(dist_sq)
+            mean_len = columns[at, 0:lanes] + len_row
+            rate = closing * mean_len / (dist_sq + mean_len * mean_len)
+            rates[at, part] = rate
+            signal = sound_row - rate
+            best = signal if k == 0 else jnp.maximum(best, signal)
+        top = jnp.max(best.T, axis=0, keepdims=True)
         top = jnp.maximum(top, jnp.max(sounds, axis=1, keepdims=True))
         own_tile = tile_at(table, block)
         allowed[pl.ds(block, 1), :] = courant * own_tile[3:4] / (own_tile[7:8] + top)
@@ -275,8 +273,8 @@
             feats[buf][32:64, part] = low
 
     def finish(block, buf):
-        for start in range(0, lanes, chunk):
-            at = pl.ds(pl.multiple_of(block * lanes + start, chunk), chunk)
+        for start in range(0, lanes, 2 * chunk):
+            at = pl.ds(pl.multiple_of(block * lanes + start, 2 * chunk), 2 * chunk)
             scale = columns[at, 2 * lanes :]
             for k in range(8):
                 part = slice(k * lanes, (k + 1) * lanes)
@@ -285,8 +283,8 @@
                 narrow = jnp.maximum(0.5 - ratio, 0.0)
                 twice = narrow + narrow
                 high, low = split2(wide * wide * wide - twice * twice * narrow)
-                weights[buf][start : start + chunk, part] = high
-                weights[buf][lanes + start : lanes + start + chunk, part] = low
+                weights[buf][start : start + 2 * chunk, part] = high
+                weights[buf][lanes + start : lanes + start + 2 * chunk, part] = low
         out = lax.dot_general(
             weights[buf][...], feats[buf][...], (((1,), (1,)), ((), ())), preferred_element_type=f32
         )
@@ -431,11 +429,11 @@
         own_weights = weights[pl.ds(pl.multiple_of(place * 2 * lanes, lanes), 2 * lanes), :]
         for base, value in ((0, own_weights), (64, damped[buf][...])):
             out = lax.dot_general(
-                value, feats[buf][...], (((1,), (1,)), ((), ())), preferred_element_type=f32
+                feats[buf][...], value, (((1,), (1,)), ((), ())), preferred_element_type=f32
             )
-            out = (out[0:lanes] + out[lanes:]).T
+            out = out[0:64] + out[64:128]
             at = pl.ds(pl.multiple_of(block * lanes + base, 64), 64)
-            sums[at, :] = out[0:64] + out[64:128]
+            sums[at, :] = out[:, 0:lanes] + out[:, lanes:]
 
     two_deep(prepare, functools.partial(finish_part, weights, damping, dens_col, 0))
 
@@ -538,10 +536,9 @@
         send_counts,
     )
     received = [swap(value, axis, odd) for value, (axis, odd, _) in zip(outgoing, swaps)]
-    steps = [("dom", 1 << bit) for bit in range(lax.axis_size("dom").bit_length() - 1)]
-    steps = steps[::-1][:1] + steps[:-1]
+    last = (1, 2, 3)
+    steps = [("dom", 1 << bit) for bit in range(2, lax.axis_size("dom").bit_length() - 1)]
     steps += [("slab", 1 << bit) for bit in reversed(range(lax.axis_size("slab").bit_length() - 1))]
-    steps = steps[:2] + steps[3:] + steps[2:3]
     left, columns, own, plan = pl.pallas_call(
         own_kernel,
         out_shape=[
@@ -572,8 +569,8 @@
     smallest = fold(smallest, *steps[0])
     density, second, *outgoing2 = call(
         density_kernel,
-        [tile] + [((64, lanes), f32)] * 5,
-        [table, masses, ((8 * 32, lanes), f32)] + [feats] * 2 + [halves] * 2,
+        [tile] + [packed] + [((64, lanes), f32)] * 4,
+        [table, masses, ((9 * 32, lanes), f32)] + [feats] * 2 + [halves] * 2,
         3,
         (plan, send_offsets, send_counts, columns, distance, own, *received),
         5 * 10**9,
@@ -582,9 +579,9 @@
     smallest, outgoing2 = lax.optimization_barrier((smallest, outgoing2))
     received2 = [swap(value, axis, odd) for value, (axis, odd, _) in zip(outgoing2, swaps)]
     parts = []
-    smallest = fold(smallest, *steps[2])
+    smallest = fold(smallest, *steps[1])
     for first in (0,):
-        smallest = fold(smallest, *steps[3])
+        smallest = fold(smallest, *steps[2])
         weights, damping, dens_col = call(
             functools.partial(weight_kernel, first),
             [((16 * lanes, 8 * lanes), bf16), ((8 * lanes, 8 * lanes), f32), ((8 * lanes, lanes), f32)],
@@ -596,13 +593,13 @@
         )
         smallest, distance, weights = lax.optimization_barrier((smallest, distance, weights))
         parts += [weights, damping, dens_col]
-    for step in steps[4:-1]:
+    for step in steps[3:]:
         smallest = fold(smallest, *step)
     smallest, received2 = lax.optimization_barrier((smallest, received2))
     accel, heating = call(
         momentum_kernel,
         [((3, points), f32), tile],
-        [table, masses, table, ((8 * lanes, lanes), f32)]
+        [table, masses, table, ((9 * lanes, lanes), f32)]
         + [((lanes, 8 * lanes), bf16)] * 2
         + [halves] * 2,
         1,
@@ -610,9 +607,12 @@
         5 * 10**9,
         20,
     )
-    smallest = fold(smallest, *steps[-1])
-    smallest, accel = lax.optimization_barrier((smallest, accel))
-    smallest = fold(smallest, *steps[1])
+    size = lax.axis_size("dom")
+    moved = [
+        lax.ppermute(smallest, "dom", [(i, i ^ step) for i in range(size)]) for step in last
+    ]
+    for value in moved:
+        smallest = jnp.minimum(smallest, value)
     share = smallest / allowed
     return (density.reshape(points), accel, heating.reshape(points), share.reshape(points))
 

time: 41.7 us -> 39.3 us (0.942)
  Pallas kernels: 22 us -> 20.1 us
  starting transfers between devices: 15.8 us -> 14.8 us
    ppermute x5 -> x3, starting transfers between devices: 5.18 us -> 2.07 us  [fold(): lax.ppermute(value, axis, [(i, i ^ step) for i in range(size)])]
    ppermute x0 -> x3, starting transfers between devices: none -> 2.36 us  [body(): lax.ppermute(smallest, 'dom', [(i, i ^ step) for i in range(size)])]
    pallas_call x1, Pallas kernels: 2.13 us -> 0.88 us  [body(): pl.pallas_call(own_kernel, out_shape=[jax.ShapeDtypeStruct((8 * lanes, la...]
    ppermute x8, waiting for transfers between devices: 0.02 us -> 1.21 us  [swap(): return lax.ppermute(value, axis, pairs)]
    ppermute x5 -> x3, waiting for transfers between devices: 0.83 us -> 0.01 us  [fold(): lax.ppermute(value, axis, [(i, i ^ step) for i in range(size)])]
    pallas_call x4, Pallas kernels: 18.3 us -> 17.7 us  [call(): pl.pallas_call(kernel, out_shape=[jax.ShapeDtypeStruct(shape, kind) for s...]
  transfers between devices with their start and end apart: 13 -> 14, of which waited for: 1 -> 1; matrix products, arithmetic and copies ran while one was open for 0% -> 0% of each run, Pallas kernels for 40% -> 38%
where the time goes in v5:
time: 39.3 us; the launch traced here: 39 us
  Pallas kernels  20.1 us (51%)
  starting transfers between devices  14.8 us (38%)
  local copies, waits for them, and re-layouts  1.47 us (4%)
  waiting for transfers between devices  1.22 us (3%)
  between operations  0.77 us (2%)
  other arithmetic  0.61 us (2%)
    pallas_call x4, Pallas kernels, call(): pl.pallas_call(kernel, out_shape=[jax.ShapeDtypeStruct(shape, kind) for s...  17.7 us
    ppermute x8, starting transfers between devices, swap(): return lax.ppermute(value, axis, pairs)  10.4 us
    ppermute x3, starting transfers between devices, body(): lax.ppermute(smallest, 'dom', [(i, i ^ step) for i in range(size)])  2.36 us
    ppermute x3, starting transfers between devices, fold(): lax.ppermute(value, axis, [(i, i ^ step) for i in range(size)])  2.07 us
    pallas_call x1, Pallas kernels, body(): pl.pallas_call(pack_kernel, out_shape=[jax.ShapeDtypeStruct((80, lanes),...  1.56 us
    unnamed x8, local copies, waits for them, and re-layouts  1.47 us
    ppermute x8, waiting for transfers between devices, swap(): return lax.ppermute(value, axis, pairs)  1.21 us
    pallas_call x1, Pallas kernels, body(): pl.pallas_call(own_kernel, out_shape=[jax.ShapeDtypeStruct((8 * lanes, la...  0.88 us
  transfers between devices with their start and end apart: 14, of which 1 were waited for; matrix products, arithmetic and copies ran while one was open for 0% of the time, Pallas kernels for 38%

profile of v5, /device:TPU:0, one launch (start us, length us, event | category | flops | bytes accessed | tf_op | source)
XLA Modules:
  0.0 39.0 jit_solution(591005960029030693)
XLA Ops:
  0.6 1.6 %shard_map.111 = (f32[80,128]{1,0:T(8,128)}, f32[72,128]{1,0:T(8,128)}, f32[72,128]{1,0:T(8,128)}, f32[72,128]{1,0:T(8,128)}, f32[72,128]{1,0:T(8,128)}) custom-call(f32[3,1024]{1,0:T(4,128)} %positions.1, f32[3,1024]{1,0:T(4,128)} %velocities.1, f32[8,128]{1,0:T(8,128)} %bitcast.13, f32[8,128]{1,0:T(8,128)} %bitcast.14, f32[8,128]{1,0:T(8,128)} %bitcast.15, ...), custom_call_target="tpu_custom_call" | custom-call | tf_op jit(solution)/shard_map/pallas_call | solution.py:524
  2.2 0.5 %collective-permute-start = (f32[72,128]{1,0:T(8,128)}, f32[72,128]{1,0:T(8,128)S(1)}, u32[]{:S(2)}, u32[]{:S(2)}) collective-permute-start(f32[72,128]{1,0:T(8,128)} %get-tuple-element.45), channel_id=1, source_target_pairs={{0,1},{1,0},{2,3},{3,2},{4,5},{5,4},{6,7},{7,6},{8,9},{9,8},{10,11... | collective-permute-start | bytes 110600 | tf_op jit(solution)/shard_map/ppermute | solution.py:38
  2.6 2.5 %collective-permute-start.1 = (f32[72,128]{1,0:T(8,128)}, f32[72,128]{1,0:T(8,128)S(1)}, u32[]{:S(2)}, u32[]{:S(2)}) collective-permute-start(f32[72,128]{1,0:T(8,128)} %get-tuple-element.46), channel_id=1, source_target_pairs={{0,8},{8,0},{16,24},{24,16},{1,9},{9,1},{17,25},{25,17},{2,10},{10... | collective-permute-start | bytes 110600 | tf_op jit(solution)/shard_map/ppermute | solution.py:38
  5.2 3.4 %collective-permute-start.2 = (f32[72,128]{1,0:T(8,128)}, f32[72,128]{1,0:T(8,128)S(1)}, u32[]{:S(2)}, u32[]{:S(2)}) collective-permute-start(f32[72,128]{1,0:T(8,128)} %get-tuple-element.47), channel_id=1, source_target_pairs={{0,7},{1,2},{2,1},{3,4},{4,3},{5,6},{6,5},{7,0},{8,15},{9,10},{10,... | collective-permute-start | bytes 110600 | tf_op jit(solution)/shard_map/ppermute | solution.py:38
  8.6 1.5 %collective-permute-start.3 = (f32[72,128]{1,0:T(8,128)}, f32[72,128]{1,0:T(8,128)S(1)}, u32[]{:S(2)}, u32[]{:S(2)}) collective-permute-start(f32[72,128]{1,0:T(8,128)} %get-tuple-element.48), channel_id=1, source_target_pairs={{0,24},{8,16},{16,8},{24,0},{1,25},{9,17},{17,9},{25,1},{2,26},{10... | collective-permute-start | bytes 110600 | tf_op jit(solution)/shard_map/ppermute | solution.py:38
  10.1 0.0 copy-start
  10.1 0.8 %copy-done = f32[80,128]{1,0:T(8,128)S(1)} copy-done((f32[80,128]{1,0:T(8,128)S(1)}, f32[80,128]{1,0:T(8,128)}, u32[]{:S(2)}) %copy-start) | copy-done | bytes 40984
  10.8 0.0 copy-start.1
  10.8 0.7 %copy-done.1 = s32[8,8]{1,0:T(8,128)S(1)} copy-done((s32[8,8]{1,0:T(8,128)S(1)}, s32[8,8]{1,0:T(8,128)}, u32[]{:S(2)}) %copy-start.1) | copy-done | bytes 280
  11.5 0.9 %shard_map.112 = (bf16[1024,128]{1,0:T(8,128)(2,1)S(1)}, f32[1024,384]{1,0:T(8,128)S(1)}, f32[80,128]{1,0:T(8,128)S(1)}, s32[8,8]{1,0:T(8,128)S(1)}) custom-call(s32[8,8]{1,0:T(8,128)S(1)} %copy-done.1, f32[80,128]{1,0:T(8,128)S(1)} %copy-done), custom_call_target="tpu_custom_call" | custom-call | tf_op jit(solution)/shard_map/pallas_call | solution.py:542
  12.4 0.0 collective-permute-done.m0
  12.4 0.0 collective-permute-done.1.m1
  12.4 0.0 collective-permute-done.2.m2
  12.4 1.2 %collective-permute-done.3.m3 = f32[72,128]{1,0:T(8,128)S(1)} collective-permute-done((f32[72,128]{1,0:T(8,128)}, f32[72,128]{1,0:T(8,128)S(1)}, u32[]{:S(2)}, u32[]{:S(2)}) %collective-permute-start.3) | collective-permute-done | bytes 36896 | tf_op jit(solution)/shard_map/ppermute | solution.py:38
  13.6 0.0 copy-start.2
  13.6 0.0 copy-start.3
  13.6 3.6 %shard_map.113 = (f32[8,128]{1,0:T(8,128)S(1)}, f32[8,128]{1,0:T(8,128)S(1)}, f32[1024,1024]{1,0:T(8,128)S(1)}, f32[1024,1024]{1,0:T(8,128)S(1)}) custom-call(s32[8,8]{1,0:T(8,128)S(1)} %get-tuple-element.41.plan, bf16[1024,128]{1,0:T(8,128)(2,1)S(1)} %get-tuple-element.43.left, f32[1024,384]{1,0:T(8,128)S(1)} %get-tuple-element.42.columns, ...), custom_call_target="tpu_custom_call" | custom-call | flops 3000000000 | bytes 200000 | tf_op jit(solution)/shard_map/pallas_call | solution.py:503
  17.2 0.1 collective-permute-start.4
  17.3 0.0 copy-done.2
  17.3 0.0 copy-done.3
  17.3 5.0 %shard_map.114 = (f32[8,128]{1,0:T(8,128)}, f32[72,128]{1,0:T(8,128)S(1)}, f32[64,128]{1,0:T(8,128)S(1)}, f32[64,128]{1,0:T(8,128)S(1)}, f32[64,128]{1,0:T(8,128)S(1)}, /*index=5*/f32[64,128]{1,0:T(8,128)S(1)}) custom-call(s32[8,8]{1,0:T(8,128)S(1)} %get-tuple-element.41.plan, s32[1,4]{1,0:T(1,128)S(1)} %bitcast.10, s32[1,4]{1,0:T(1,128)S(1)} %bitcast.12, ...), custom_call_target="tpu_custom_call" | custom-call | flops 5000000000 | bytes 200000 | tf_op jit(solution)/shard_map/pallas_call | solution.py:503
  22.3 0.0 collective-permute-done.4
  22.3 1.5 %collective-permute-start.5 = (f32[8,128]{1,0:T(8,128)S(1)}, f32[8,128]{1,0:T(8,128)S(1)}, u32[]{:S(2)}, u32[]{:S(2)}) collective-permute-start(f32[8,128]{1,0:T(8,128)S(1)} %min.18), channel_id=1, source_target_pairs={{0,16},{8,24},{16,0},{24,8},{1,17},{9,25},{17,1},{25,9},{2,18},{10... | collective-permute-start | bytes 12296 | tf_op jit(solution)/shard_map/ppermute | solution.py:516
  23.8 0.0 collective-permute-start.7
  23.8 0.5 %collective-permute-start.8 = (f32[64,128]{1,0:T(8,128)S(1)}, f32[64,128]{1,0:T(8,128)S(1)}, u32[]{:S(2)}, u32[]{:S(2)}) collective-permute-start(f32[64,128]{1,0:T(8,128)S(1)} %get-tuple-element.65), channel_id=1, source_target_pairs={{0,8},{8,0},{16,24},{24,16},{1,9},{9,1},{17,25},{25,17},{2,10},{10... | collective-permute-start | bytes 98312 | tf_op jit(solution)/shard_map/ppermute | solution.py:38
  24.4 0.6 %collective-permute-start.9 = (f32[64,128]{1,0:T(8,128)S(1)}, f32[64,128]{1,0:T(8,128)S(1)}, u32[]{:S(2)}, u32[]{:S(2)}) collective-permute-start(f32[64,128]{1,0:T(8,128)S(1)} %get-tuple-element.66), channel_id=1, source_target_pairs={{0,7},{1,2},{2,1},{3,4},{4,3},{5,6},{6,5},{7,0},{8,15},{9,10},{10,... | collective-permute-start | bytes 98312 | tf_op jit(solution)/shard_map/ppermute | solution.py:38
  25.0 1.4 %collective-permute-start.10 = (f32[64,128]{1,0:T(8,128)S(1)}, f32[64,128]{1,0:T(8,128)S(1)}, u32[]{:S(2)}, u32[]{:S(2)}) collective-permute-start(f32[64,128]{1,0:T(8,128)S(1)} %get-tuple-element.67), channel_id=1, source_target_pairs={{0,24},{8,16},{16,8},{24,0},{1,25},{9,17},{17,9},{25,1},{2,26},{10... | collective-permute-start | bytes 98312 | tf_op jit(solution)/shard_map/ppermute | solution.py:38
  26.4 0.0 collective-permute-done.5
  26.4 0.5 %collective-permute-start.6 = (f32[8,128]{1,0:T(8,128)S(1)}, f32[8,128]{1,0:T(8,128)S(1)}, u32[]{:S(2)}, u32[]{:S(2)}) collective-permute-start(f32[8,128]{1,0:T(8,128)S(1)} %min.19), channel_id=1, source_target_pairs={{0,8},{8,0},{16,24},{24,16},{1,9},{9,1},{17,25},{25,17},{2,10},{10... | collective-permute-start | bytes 12296 | tf_op jit(solution)/shard_map/ppermute | solution.py:516
  26.9 4.2 %shard_map.115 = (bf16[2048,1024]{1,0:T(8,128)(2,1)S(1)}, f32[1024,1024]{1,0:T(8,128)S(1)}, f32[1024,128]{1,0:T(8,128)S(1)}) custom-call(s32[8,8]{1,0:T(8,128)S(1)} %get-tuple-element.41.plan, f32[1024,384]{1,0:T(8,128)S(1)} %get-tuple-element.42.columns, f32[1024,1024]{1,0:T(8,128)S(1)} %get-tuple-element.49.distance, ...), custom_call_target="tpu_custom_call" | custom-call | flops 1000000000 | bytes 200000 | tf_op jit(solution)/shard_map/pallas_call | solution.py:503
  31.1 0.0 collective-permute-done.6
  31.1 0.0 collective-permute-done.7.s0
  31.1 0.0 collective-permute-done.8.s1
  31.1 0.0 collective-permute-done.9.s2
  31.2 0.0 collective-permute-done.10.s3
  31.2 2.2 %collective-permute-start.13 = (f32[8,128]{1,0:T(8,128)S(1)}, f32[8,128]{1,0:T(8,128)S(1)}, u32[]{:S(2)}, u32[]{:S(2)}) collective-permute-start(f32[8,128]{1,0:T(8,128)S(1)} %min.20), channel_id=1, source_target_pairs={{0,3},{1,2},{2,1},{3,0},{4,7},{5,6},{6,5},{7,4},{8,11},{9,10},{10,... | collective-permute-start | bytes 12296 | tf_op jit(solution)/shard_map/ppermute | solution.py:612
  33.3 0.0 collective-permute-start.12
  33.3 0.2 collective-permute-start.11
  33.5 4.9 %shard_map.116 = (f32[3,1024]{1,0:T(4,128)}, f32[8,128]{1,0:T(8,128)}) custom-call(s32[8,8]{1,0:T(8,128)S(1)} %get-tuple-element.41.plan, bf16[2048,1024]{1,0:T(8,128)(2,1)S(1)} %get-tuple-element.60.weights, f32[1024,1024]{1,0:T(8,128)S(1)} %get-tuple-element.61.damping, f32[1024,128]{1,0:T(8,128)S(1)} %get-tuple-element.62.dens_col, ...), custom_call_target="tpu_custom_call" | custom-call | flops 5000000000 | bytes 200000 | tf_op jit(solution)/shard_map/pallas_call | solution.py:503
  38.4 0.0 collective-permute-done.13
  38.4 0.0 collective-permute-done.12
  38.4 0.0 collective-permute-done.11
  38.4 0.6 %divide_bitcast_fusion = f32[1024]{0:T(1024)} fusion(f32[8,128]{1,0:T(8,128)S(1)} %get-tuple-element.75, f32[8,128]{1,0:T(8,128)S(1)} %collective-permute-done.13, f32[8,128]{1,0:T(8,128)S(1)} %collective-permute-done.12, f32[8,128]{1,0:T(8,128)S(1)} %min.20, f32[8,128]{1,0:T(8,128)S(1)} %collective-permute-done.11), kind=kLoop, calls=%fused_computation | loop fusion | flops 4096 | bytes 24576 | tf_op jit(solution)/shard_map/reshape | solution.py:617
  (3 shorter events, 0.0 us)
Async XLA Ops:
  2.2 10.2 %collective-permute-start = (f32[72,128]{1,0:T(8,128)}, f32[72,128]{1,0:T(8,128)S(1)}, u32[]{:S(2)}, u32[]{:S(2)}) collective-permute-start(f32[72,128]{1,0:T(8,128)} %get-tuple-element.45), channel_id=1, source_target_pairs={{0,1},{1,0},{2,3},{3,2},{4,5},{5,4},{6,7},{7,6},{8,9},{9,8},{10,11... | collective-permute-start | bytes 110600 | tf_op jit(solution)/shard_map/ppermute | solution.py:38
  2.6 9.8 %collective-permute-start.1 = (f32[72,128]{1,0:T(8,128)}, f32[72,128]{1,0:T(8,128)S(1)}, u32[]{:S(2)}, u32[]{:S(2)}) collective-permute-start(f32[72,128]{1,0:T(8,128)} %get-tuple-element.46), channel_id=1, source_target_pairs={{0,8},{8,0},{16,24},{24,16},{1,9},{9,1},{17,25},{25,17},{2,10},{10... | collective-permute-start | bytes 110600 | tf_op jit(solution)/shard_map/ppermute | solution.py:38
  5.2 7.2 %collective-permute-start.2 = (f32[72,128]{1,0:T(8,128)}, f32[72,128]{1,0:T(8,128)S(1)}, u32[]{:S(2)}, u32[]{:S(2)}) collective-permute-start(f32[72,128]{1,0:T(8,128)} %get-tuple-element.47), channel_id=1, source_target_pairs={{0,7},{1,2},{2,1},{3,4},{4,3},{5,6},{6,5},{7,0},{8,15},{9,10},{10,... | collective-permute-start | bytes 110600 | tf_op jit(solution)/shard_map/ppermute | solution.py:38
  8.6 5.1 %collective-permute-start.3 = (f32[72,128]{1,0:T(8,128)}, f32[72,128]{1,0:T(8,128)S(1)}, u32[]{:S(2)}, u32[]{:S(2)}) collective-permute-start(f32[72,128]{1,0:T(8,128)} %get-tuple-element.48), channel_id=1, source_target_pairs={{0,24},{8,16},{16,8},{24,0},{1,25},{9,17},{17,9},{25,1},{2,26},{10... | collective-permute-start | bytes 110600 | tf_op jit(solution)/shard_map/ppermute | solution.py:38
  10.1 0.8 %copy-start = (f32[80,128]{1,0:T(8,128)S(1)}, f32[80,128]{1,0:T(8,128)}, u32[]{:S(2)}) copy-start(f32[80,128]{1,0:T(8,128)} %get-tuple-element.40.own) | copy-start | bytes 122884
  10.8 0.7 %copy-start.1 = (s32[8,8]{1,0:T(8,128)S(1)}, s32[8,8]{1,0:T(8,128)}, u32[]{:S(2)}) copy-start(s32[8,8]{1,0:T(8,128)} %pairs.1) | copy-start | bytes 772
  13.6 3.7 %copy-start.2 = (s32[4,1]{0,1:T(1,128)S(1)}, s32[4,1]{0,1:T(1,128)}, u32[]{:S(2)}) copy-start(s32[4,1]{0,1:T(1,128)} %param.13) | copy-start | bytes 52
  13.6 3.7 %copy-start.3 = (s32[4,1]{0,1:T(1,128)S(1)}, s32[4,1]{0,1:T(1,128)}, u32[]{:S(2)}) copy-start(s32[4,1]{0,1:T(1,128)} %param.14) | copy-start | bytes 52
  17.2 5.1 %collective-permute-start.4 = (f32[8,128]{1,0:T(8,128)S(1)}, f32[8,128]{1,0:T(8,128)S(1)}, u32[]{:S(2)}, u32[]{:S(2)}) collective-permute-start(f32[8,128]{1,0:T(8,128)S(1)} %get-tuple-element.51), channel_id=1, source_target_pairs={{0,4},{1,5},{2,6},{3,7},{4,0},{5,1},{6,2},{7,3},{8,12},{9,13},{10,... | collective-permute-start | bytes 12296 | tf_op jit(solution)/shard_map/ppermute | solution.py:516
  22.3 4.1 %collective-permute-start.5 = (f32[8,128]{1,0:T(8,128)S(1)}, f32[8,128]{1,0:T(8,128)S(1)}, u32[]{:S(2)}, u32[]{:S(2)}) collective-permute-start(f32[8,128]{1,0:T(8,128)S(1)} %min.18), channel_id=1, source_target_pairs={{0,16},{8,24},{16,0},{24,8},{1,17},{9,25},{17,1},{25,9},{2,18},{10... | collective-permute-start | bytes 12296 | tf_op jit(solution)/shard_map/ppermute | solution.py:516
  23.8 7.3 %collective-permute-start.7 = (f32[64,128]{1,0:T(8,128)S(1)}, f32[64,128]{1,0:T(8,128)S(1)}, u32[]{:S(2)}, u32[]{:S(2)}) collective-permute-start(f32[64,128]{1,0:T(8,128)S(1)} %get-tuple-element.64), channel_id=1, source_target_pairs={{0,1},{1,0},{2,3},{3,2},{4,5},{5,4},{6,7},{7,6},{8,9},{9,8},{10,11... | collective-permute-start | bytes 98312 | tf_op jit(solution)/shard_map/ppermute | solution.py:38
  23.8 7.3 %collective-permute-start.8 = (f32[64,128]{1,0:T(8,128)S(1)}, f32[64,128]{1,0:T(8,128)S(1)}, u32[]{:S(2)}, u32[]{:S(2)}) collective-permute-start(f32[64,128]{1,0:T(8,128)S(1)} %get-tuple-element.65), channel_id=1, source_target_pairs={{0,8},{8,0},{16,24},{24,16},{1,9},{9,1},{17,25},{25,17},{2,10},{10... | collective-permute-start | bytes 98312 | tf_op jit(solution)/shard_map/ppermute | solution.py:38
  24.4 6.8 %collective-permute-start.9 = (f32[64,128]{1,0:T(8,128)S(1)}, f32[64,128]{1,0:T(8,128)S(1)}, u32[]{:S(2)}, u32[]{:S(2)}) collective-permute-start(f32[64,128]{1,0:T(8,128)S(1)} %get-tuple-element.66), channel_id=1, source_target_pairs={{0,7},{1,2},{2,1},{3,4},{4,3},{5,6},{6,5},{7,0},{8,15},{9,10},{10,... | collective-permute-start | bytes 98312 | tf_op jit(solution)/shard_map/ppermute | solution.py:38
  25.0 6.2 %collective-permute-start.10 = (f32[64,128]{1,0:T(8,128)S(1)}, f32[64,128]{1,0:T(8,128)S(1)}, u32[]{:S(2)}, u32[]{:S(2)}) collective-permute-start(f32[64,128]{1,0:T(8,128)S(1)} %get-tuple-element.67), channel_id=1, source_target_pairs={{0,24},{8,16},{16,8},{24,0},{1,25},{9,17},{17,9},{25,1},{2,26},{10... | collective-permute-start | bytes 98312 | tf_op jit(solution)/shard_map/ppermute | solution.py:38
  26.4 4.7 %collective-permute-start.6 = (f32[8,128]{1,0:T(8,128)S(1)}, f32[8,128]{1,0:T(8,128)S(1)}, u32[]{:S(2)}, u32[]{:S(2)}) collective-permute-start(f32[8,128]{1,0:T(8,128)S(1)} %min.19), channel_id=1, source_target_pairs={{0,8},{8,0},{16,24},{24,16},{1,9},{9,1},{17,25},{25,17},{2,10},{10... | collective-permute-start | bytes 12296 | tf_op jit(solution)/shard_map/ppermute | solution.py:516
  31.2 7.3 %collective-permute-start.13 = (f32[8,128]{1,0:T(8,128)S(1)}, f32[8,128]{1,0:T(8,128)S(1)}, u32[]{:S(2)}, u32[]{:S(2)}) collective-permute-start(f32[8,128]{1,0:T(8,128)S(1)} %min.20), channel_id=1, source_target_pairs={{0,3},{1,2},{2,1},{3,0},{4,7},{5,6},{6,5},{7,4},{8,11},{9,10},{10,... | collective-permute-start | bytes 12296 | tf_op jit(solution)/shard_map/ppermute | solution.py:612
  33.3 5.1 %collective-permute-start.12 = (f32[8,128]{1,0:T(8,128)S(1)}, f32[8,128]{1,0:T(8,128)S(1)}, u32[]{:S(2)}, u32[]{:S(2)}) collective-permute-start(f32[8,128]{1,0:T(8,128)S(1)} %min.20), channel_id=1, source_target_pairs={{0,2},{1,3},{2,0},{3,1},{4,6},{5,7},{6,4},{7,5},{8,10},{9,11},{10,... | collective-permute-start | bytes 12296 | tf_op jit(solution)/shard_map/ppermute | solution.py:612
  33.3 5.1 %collective-permute-start.11 = (f32[8,128]{1,0:T(8,128)S(1)}, f32[8,128]{1,0:T(8,128)S(1)}, u32[]{:S(2)}, u32[]{:S(2)}) collective-permute-start(f32[8,128]{1,0:T(8,128)S(1)} %min.20), channel_id=1, source_target_pairs={{0,1},{1,0},{2,3},{3,2},{4,5},{5,4},{6,7},{7,6},{8,9},{9,8},{10,11... | collective-permute-start | bytes 12296 | tf_op jit(solution)/shard_map/ppermute | solution.py:612

commit v6 on v5

--- a/solution.py
+++ b/solution.py
@@ -249,7 +249,7 @@
 
 
 def density_kernel(
-    plan, offsets, counts, columns, distance, own, m0, m1, m2, m3, density, second, *rest
+    plan, offsets, counts, columns, distance, own, m0, m1, m2, m3, second, *rest
 ):
     outgoing = rest[0:4]
     table, masses, sums, *scratch = rest[4:]
@@ -286,16 +286,15 @@
                 weights[buf][start : start + 2 * chunk, part] = high
                 weights[buf][lanes + start : lanes + start + 2 * chunk, part] = low
         out = lax.dot_general(
-            weights[buf][...], feats[buf][...], (((1,), (1,)), ((), ())), preferred_element_type=f32
+            feats[buf][...], weights[buf][...], (((1,), (1,)), ((), ())), preferred_element_type=f32
         )
-        out = (out[0:lanes] + out[lanes:]).T
-        at = pl.ds(pl.multiple_of(block * 32, 32), 32)
-        sums[at, :] = out[0:32] + out[32:64]
+        out = out[0:32] + out[32:64]
+        sums[pl.ds(block, 32, stride=8), :] = out[:, 0:lanes] + out[:, lanes:]
 
     two_deep(prepare, finish)
 
     def total(field):
-        return sums[pl.ds(field, 8, stride=32), :]
+        return sums[field * 8 : (field + 1) * 8, :]
 
     def mine(field):
         return own[pl.ds(field, 8, stride=rows), :]
@@ -324,7 +323,6 @@
     cof_xz = axy * ayz - ayy * axz
     cof_yz = axy * axz - axx * ayz
     inv_det = 1.0 / (axx * cof_xx + axy * cof_xy + axz * cof_xz)
-    density[...] = dens
     pressure = (gas_gamma - 1.0) * own[72:80, :] / dens
     fields = [dens, pressure, cof_xx * inv_det, cof_yy * inv_det, cof_zz * inv_det]
     fields += [cof_xy * inv_det, cof_xz * inv_det, cof_yz * inv_det]
@@ -371,7 +369,7 @@
 
 def momentum_kernel(
     plan, weights, damping, dens_col,
-    own, m0, m1, m2, m3, second, s0, s1, s2, s3, accel, heating, *scratch
+    own, m0, m1, m2, m3, second, s0, s1, s2, s3, accel, heating, density, *scratch
 ):
     table, masses, table2, sums, *scratch = scratch
     feats, damped = scratch[0:2], scratch[2:4]
@@ -432,8 +430,7 @@
                 feats[buf][...], value, (((1,), (1,)), ((), ())), preferred_element_type=f32
             )
             out = out[0:64] + out[64:128]
-            at = pl.ds(pl.multiple_of(block * lanes + base, 64), 64)
-            sums[at, :] = out[:, 0:lanes] + out[:, lanes:]
+            sums[pl.ds(base * 8 + block, 64, stride=8), :] = out[:, 0:lanes] + out[:, lanes:]
 
     two_deep(prepare, functools.partial(finish_part, weights, damping, dens_col, 0))
 
@@ -443,13 +440,14 @@
     place = [mine(own, a) for a in range(3)]
     place = [value - (jnp.floor(value[:, 0:1]) + 0.5) for value in place]
     speed = [mine(own, 4 + a) for a in range(3)]
+    density[...] = mine(second, 0)
     pressure = mine(second, 1)
     order = ((2, 5, 6), (5, 3, 7), (6, 7, 4))
     matrix = [[mine(second, order[a][b]) for b in range(3)] for a in range(3)]
 
     def pieces(base):
         def total(field):
-            return sums[pl.ds(base + field, 8, stride=lanes), :]
+            return sums[(base + field) * 8 : (base + field + 1) * 8, :]
 
         mass = total(3)
         offset = [total(a) - place[a] * mass for a in range(3)]
@@ -567,9 +565,9 @@
         20,
     )
     smallest = fold(smallest, *steps[0])
-    density, second, *outgoing2 = call(
+    second, *outgoing2 = call(
         density_kernel,
-        [tile] + [packed] + [((64, lanes), f32)] * 4,
+        [packed] + [((64, lanes), f32)] * 4,
         [table, masses, ((9 * 32, lanes), f32)] + [feats] * 2 + [halves] * 2,
         3,
         (plan, send_offsets, send_counts, columns, distance, own, *received),
@@ -596,9 +594,9 @@
     for step in steps[3:]:
         smallest = fold(smallest, *step)
     smallest, received2 = lax.optimization_barrier((smallest, received2))
-    accel, heating = call(
+    accel, heating, density = call(
         momentum_kernel,
-        [((3, points), f32), tile],
+        [((3, points), f32), tile, tile],
         [table, masses, table, ((9 * lanes, lanes), f32)]
         + [((lanes, 8 * lanes), bf16)] * 2
         + [halves] * 2,

time: 39.3 us -> 38.8 us (0.987)
  Pallas kernels: 20.1 us -> 19.5 us
    pallas_call x4, Pallas kernels: 17.7 us -> 17.1 us  [call(): pl.pallas_call(kernel, out_shape=[jax.ShapeDtypeStruct(shape, kind) for s...]
  transfers between devices with their start and end apart: 14 -> 14, of which waited for: 1 -> 2; matrix products, arithmetic and copies ran while one was open for 0% -> 0% of each run, Pallas kernels for 38% -> 37%
where the time goes in v6:
time: 38.8 us; the launch traced here: 38.5 us
  Pallas kernels  19.5 us (50%)
  starting transfers between devices  14.8 us (38%)
  local copies, waits for them, and re-layouts  1.47 us (4%)
  waiting for transfers between devices  1.35 us (3%)
  between operations  0.78 us (2%)
  other arithmetic  0.61 us (2%)
    pallas_call x4, Pallas kernels, call(): pl.pallas_call(kernel, out_shape=[jax.ShapeDtypeStruct(shape, kind) for s...  17.1 us
    ppermute x8, starting transfers between devices, swap(): return lax.ppermute(value, axis, pairs)  10.4 us
    ppermute x3, starting transfers between devices, body(): lax.ppermute(smallest, 'dom', [(i, i ^ step) for i in range(size)])  2.37 us
    ppermute x3, starting transfers between devices, fold(): lax.ppermute(value, axis, [(i, i ^ step) for i in range(size)])  2.05 us
    pallas_call x1, Pallas kernels, body(): pl.pallas_call(pack_kernel, out_shape=[jax.ShapeDtypeStruct((80, lanes),...  1.56 us
    unnamed x8, local copies, waits for them, and re-layouts  1.47 us
    ppermute x8, waiting for transfers between devices, swap(): return lax.ppermute(value, axis, pairs)  1.21 us
    pallas_call x1, Pallas kernels, body(): pl.pallas_call(own_kernel, out_shape=[jax.ShapeDtypeStruct((8 * lanes, la...  0.88 us
  transfers between devices with their start and end apart: 14, of which 2 were waited for; matrix products, arithmetic and copies ran while one was open for 0% of the time, Pallas kernels for 37%

profile of v6, /device:TPU:0, one launch (start us, length us, event | category | flops | bytes accessed | tf_op | source)
XLA Modules:
  0.0 38.5 jit_solution(5801117108374519341)
XLA Ops:
  0.6 1.6 %shard_map.111 = (f32[80,128]{1,0:T(8,128)}, f32[72,128]{1,0:T(8,128)}, f32[72,128]{1,0:T(8,128)}, f32[72,128]{1,0:T(8,128)}, f32[72,128]{1,0:T(8,128)}) custom-call(f32[3,1024]{1,0:T(4,128)} %positions.1, f32[3,1024]{1,0:T(4,128)} %velocities.1, f32[8,128]{1,0:T(8,128)} %bitcast.13, f32[8,128]{1,0:T(8,128)} %bitcast.14, f32[8,128]{1,0:T(8,128)} %bitcast.15, ...), custom_call_target="tpu_custom_call" | custom-call | tf_op jit(solution)/shard_map/pallas_call | solution.py:522
  2.2 0.5 %collective-permute-start = (f32[72,128]{1,0:T(8,128)}, f32[72,128]{1,0:T(8,128)S(1)}, u32[]{:S(2)}, u32[]{:S(2)}) collective-permute-start(f32[72,128]{1,0:T(8,128)} %get-tuple-element.45), channel_id=1, source_target_pairs={{0,1},{1,0},{2,3},{3,2},{4,5},{5,4},{6,7},{7,6},{8,9},{9,8},{10,11... | collective-permute-start | bytes 110600 | tf_op jit(solution)/shard_map/ppermute | solution.py:38
  2.6 2.5 %collective-permute-start.1 = (f32[72,128]{1,0:T(8,128)}, f32[72,128]{1,0:T(8,128)S(1)}, u32[]{:S(2)}, u32[]{:S(2)}) collective-permute-start(f32[72,128]{1,0:T(8,128)} %get-tuple-element.46), channel_id=1, source_target_pairs={{0,8},{8,0},{16,24},{24,16},{1,9},{9,1},{17,25},{25,17},{2,10},{10... | collective-permute-start | bytes 110600 | tf_op jit(solution)/shard_map/ppermute | solution.py:38
  5.2 3.4 %collective-permute-start.2 = (f32[72,128]{1,0:T(8,128)}, f32[72,128]{1,0:T(8,128)S(1)}, u32[]{:S(2)}, u32[]{:S(2)}) collective-permute-start(f32[72,128]{1,0:T(8,128)} %get-tuple-element.47), channel_id=1, source_target_pairs={{0,7},{1,2},{2,1},{3,4},{4,3},{5,6},{6,5},{7,0},{8,15},{9,10},{10,... | collective-permute-start | bytes 110600 | tf_op jit(solution)/shard_map/ppermute | solution.py:38
  8.6 1.5 %collective-permute-start.3 = (f32[72,128]{1,0:T(8,128)}, f32[72,128]{1,0:T(8,128)S(1)}, u32[]{:S(2)}, u32[]{:S(2)}) collective-permute-start(f32[72,128]{1,0:T(8,128)} %get-tuple-element.48), channel_id=1, source_target_pairs={{0,24},{8,16},{16,8},{24,0},{1,25},{9,17},{17,9},{25,1},{2,26},{10... | collective-permute-start | bytes 110600 | tf_op jit(solution)/shard_map/ppermute | solution.py:38
  10.1 0.0 copy-start
  10.1 0.8 %copy-done = f32[80,128]{1,0:T(8,128)S(1)} copy-done((f32[80,128]{1,0:T(8,128)S(1)}, f32[80,128]{1,0:T(8,128)}, u32[]{:S(2)}) %copy-start) | copy-done | bytes 40984
  10.8 0.0 copy-start.1
  10.8 0.7 %copy-done.1 = s32[8,8]{1,0:T(8,128)S(1)} copy-done((s32[8,8]{1,0:T(8,128)S(1)}, s32[8,8]{1,0:T(8,128)}, u32[]{:S(2)}) %copy-start.1) | copy-done | bytes 280
  11.5 0.9 %shard_map.112 = (bf16[1024,128]{1,0:T(8,128)(2,1)S(1)}, f32[1024,384]{1,0:T(8,128)S(1)}, f32[80,128]{1,0:T(8,128)S(1)}, s32[8,8]{1,0:T(8,128)S(1)}) custom-call(s32[8,8]{1,0:T(8,128)S(1)} %copy-done.1, f32[80,128]{1,0:T(8,128)S(1)} %copy-done), custom_call_target="tpu_custom_call" | custom-call | tf_op jit(solution)/shard_map/pallas_call | solution.py:540
  12.4 0.0 collective-permute-done.m0
  12.4 0.0 collective-permute-done.1.m1
  12.4 0.0 collective-permute-done.2.m2
  12.4 1.2 %collective-permute-done.3.m3 = f32[72,128]{1,0:T(8,128)S(1)} collective-permute-done((f32[72,128]{1,0:T(8,128)}, f32[72,128]{1,0:T(8,128)S(1)}, u32[]{:S(2)}, u32[]{:S(2)}) %collective-permute-start.3) | collective-permute-done | bytes 36896 | tf_op jit(solution)/shard_map/ppermute | solution.py:38
  13.6 0.0 copy-start.2
  13.6 0.0 copy-start.3
  13.6 3.6 %shard_map.113 = (f32[8,128]{1,0:T(8,128)S(1)}, f32[8,128]{1,0:T(8,128)S(1)}, f32[1024,1024]{1,0:T(8,128)S(1)}, f32[1024,1024]{1,0:T(8,128)S(1)}) custom-call(s32[8,8]{1,0:T(8,128)S(1)} %get-tuple-element.41.plan, bf16[1024,128]{1,0:T(8,128)(2,1)S(1)} %get-tuple-element.42.left, f32[1024,384]{1,0:T(8,128)S(1)} %get-tuple-element.43.columns, ...), custom_call_target="tpu_custom_call" | custom-call | flops 3000000000 | bytes 200000 | tf_op jit(solution)/shard_map/pallas_call | solution.py:501
  17.2 0.1 collective-permute-start.4
  17.3 0.0 copy-done.2
  17.3 0.0 copy-done.3
  17.3 4.3 %shard_map.114 = (f32[72,128]{1,0:T(8,128)S(1)}, f32[64,128]{1,0:T(8,128)S(1)}, f32[64,128]{1,0:T(8,128)S(1)}, f32[64,128]{1,0:T(8,128)S(1)}, f32[64,128]{1,0:T(8,128)S(1)}) custom-call(s32[8,8]{1,0:T(8,128)S(1)} %get-tuple-element.41.plan, s32[1,4]{1,0:T(1,128)S(1)} %bitcast.10, s32[1,4]{1,0:T(1,128)S(1)} %bitcast.12, ...), custom_call_target="tpu_custom_call" | custom-call | flops 5000000000 | bytes 200000 | tf_op jit(solution)/shard_map/pallas_call | solution.py:501
  21.7 0.1 collective-permute-done.4
  21.8 1.5 %collective-permute-start.5 = (f32[8,128]{1,0:T(8,128)S(1)}, f32[8,128]{1,0:T(8,128)S(1)}, u32[]{:S(2)}, u32[]{:S(2)}) collective-permute-start(f32[8,128]{1,0:T(8,128)S(1)} %min.18), channel_id=1, source_target_pairs={{0,16},{8,24},{16,0},{24,8},{1,17},{9,25},{17,1},{25,9},{2,18},{10... | collective-permute-start | bytes 12296 | tf_op jit(solution)/shard_map/ppermute | solution.py:514
  23.3 0.0 collective-permute-start.7
  23.3 0.5 %collective-permute-start.8 = (f32[64,128]{1,0:T(8,128)S(1)}, f32[64,128]{1,0:T(8,128)S(1)}, u32[]{:S(2)}, u32[]{:S(2)}) collective-permute-start(f32[64,128]{1,0:T(8,128)S(1)} %get-tuple-element.64), channel_id=1, source_target_pairs={{0,8},{8,0},{16,24},{24,16},{1,9},{9,1},{17,25},{25,17},{2,10},{10... | collective-permute-start | bytes 98312 | tf_op jit(solution)/shard_map/ppermute | solution.py:38
  23.9 0.5 %collective-permute-start.9 = (f32[64,128]{1,0:T(8,128)S(1)}, f32[64,128]{1,0:T(8,128)S(1)}, u32[]{:S(2)}, u32[]{:S(2)}) collective-permute-start(f32[64,128]{1,0:T(8,128)S(1)} %get-tuple-element.65), channel_id=1, source_target_pairs={{0,7},{1,2},{2,1},{3,4},{4,3},{5,6},{6,5},{7,0},{8,15},{9,10},{10,... | collective-permute-start | bytes 98312 | tf_op jit(solution)/shard_map/ppermute | solution.py:38
  24.4 1.4 %collective-permute-start.10 = (f32[64,128]{1,0:T(8,128)S(1)}, f32[64,128]{1,0:T(8,128)S(1)}, u32[]{:S(2)}, u32[]{:S(2)}) collective-permute-start(f32[64,128]{1,0:T(8,128)S(1)} %get-tuple-element.66), channel_id=1, source_target_pairs={{0,24},{8,16},{16,8},{24,0},{1,25},{9,17},{17,9},{25,1},{2,26},{10... | collective-permute-start | bytes 98312 | tf_op jit(solution)/shard_map/ppermute | solution.py:38
  25.8 0.0 collective-permute-done.5
  25.8 0.5 %collective-permute-start.6 = (f32[8,128]{1,0:T(8,128)S(1)}, f32[8,128]{1,0:T(8,128)S(1)}, u32[]{:S(2)}, u32[]{:S(2)}) collective-permute-start(f32[8,128]{1,0:T(8,128)S(1)} %min.19), channel_id=1, source_target_pairs={{0,8},{8,0},{16,24},{24,16},{1,9},{9,1},{17,25},{25,17},{2,10},{10... | collective-permute-start | bytes 12296 | tf_op jit(solution)/shard_map/ppermute | solution.py:514
  26.3 4.2 %shard_map.115 = (bf16[2048,1024]{1,0:T(8,128)(2,1)S(1)}, f32[1024,1024]{1,0:T(8,128)S(1)}, f32[1024,128]{1,0:T(8,128)S(1)}) custom-call(s32[8,8]{1,0:T(8,128)S(1)} %get-tuple-element.41.plan, f32[1024,384]{1,0:T(8,128)S(1)} %get-tuple-element.43.columns, f32[1024,1024]{1,0:T(8,128)S(1)} %get-tuple-element.50.distance, ...), custom_call_target="tpu_custom_call" | custom-call | flops 1000000000 | bytes 200000 | tf_op jit(solution)/shard_map/pallas_call | solution.py:501
  30.5 0.0 collective-permute-done.6
  30.6 0.0 collective-permute-done.7.s0
  30.6 0.0 collective-permute-done.8.s1
  30.6 0.0 collective-permute-done.9.s2
  30.6 0.0 collective-permute-done.10.s3
  30.6 2.2 %collective-permute-start.13 = (f32[8,128]{1,0:T(8,128)S(1)}, f32[8,128]{1,0:T(8,128)S(1)}, u32[]{:S(2)}, u32[]{:S(2)}) collective-permute-start(f32[8,128]{1,0:T(8,128)S(1)} %min.20), channel_id=1, source_target_pairs={{0,3},{1,2},{2,1},{3,0},{4,7},{5,6},{6,5},{7,4},{8,11},{9,10},{10,... | collective-permute-start | bytes 12296 | tf_op jit(solution)/shard_map/ppermute | solution.py:610
  32.8 0.0 collective-permute-start.12
  32.8 0.2 collective-permute-start.11
  33.0 4.9 %shard_map.116 = (f32[3,1024]{1,0:T(4,128)}, f32[8,128]{1,0:T(8,128)}, f32[8,128]{1,0:T(8,128)}) custom-call(s32[8,8]{1,0:T(8,128)S(1)} %get-tuple-element.41.plan, bf16[2048,1024]{1,0:T(8,128)(2,1)S(1)} %get-tuple-element.59.weights, f32[1024,1024]{1,0:T(8,128)S(1)} %get-tuple-element.60.damping, f32[1024,128]{1,0:T(8,128)S(1)} %get-tuple-element.61.dens_col, ...), custom_call_target="tpu_custom_call" | custom-call | flops 5000000000 | bytes 200000 | tf_op jit(solution)/shard_map/pallas_call | solution.py:501
  37.9 0.0 collective-permute-done.13
  37.9 0.0 collective-permute-done.12
  37.9 0.0 collective-permute-done.11
  37.9 0.6 %divide_bitcast_fusion = f32[1024]{0:T(1024)} fusion(f32[8,128]{1,0:T(8,128)S(1)} %get-tuple-element.75, f32[8,128]{1,0:T(8,128)S(1)} %collective-permute-done.13, f32[8,128]{1,0:T(8,128)S(1)} %collective-permute-done.12, f32[8,128]{1,0:T(8,128)S(1)} %min.20, f32[8,128]{1,0:T(8,128)S(1)} %collective-permute-done.11), kind=kLoop, calls=%fused_computation | loop fusion | flops 4096 | bytes 24576 | tf_op jit(solution)/shard_map/reshape | solution.py:615
  (3 shorter events, 0.0 us)
Async XLA Ops:
  2.2 10.2 %collective-permute-start = (f32[72,128]{1,0:T(8,128)}, f32[72,128]{1,0:T(8,128)S(1)}, u32[]{:S(2)}, u32[]{:S(2)}) collective-permute-start(f32[72,128]{1,0:T(8,128)} %get-tuple-element.45), channel_id=1, source_target_pairs={{0,1},{1,0},{2,3},{3,2},{4,5},{5,4},{6,7},{7,6},{8,9},{9,8},{10,11... | collective-permute-start | bytes 110600 | tf_op jit(solution)/shard_map/ppermute | solution.py:38
  2.6 9.8 %collective-permute-start.1 = (f32[72,128]{1,0:T(8,128)}, f32[72,128]{1,0:T(8,128)S(1)}, u32[]{:S(2)}, u32[]{:S(2)}) collective-permute-start(f32[72,128]{1,0:T(8,128)} %get-tuple-element.46), channel_id=1, source_target_pairs={{0,8},{8,0},{16,24},{24,16},{1,9},{9,1},{17,25},{25,17},{2,10},{10... | collective-permute-start | bytes 110600 | tf_op jit(solution)/shard_map/ppermute | solution.py:38
  5.2 7.2 %collective-permute-start.2 = (f32[72,128]{1,0:T(8,128)}, f32[72,128]{1,0:T(8,128)S(1)}, u32[]{:S(2)}, u32[]{:S(2)}) collective-permute-start(f32[72,128]{1,0:T(8,128)} %get-tuple-element.47), channel_id=1, source_target_pairs={{0,7},{1,2},{2,1},{3,4},{4,3},{5,6},{6,5},{7,0},{8,15},{9,10},{10,... | collective-permute-start | bytes 110600 | tf_op jit(solution)/shard_map/ppermute | solution.py:38
  8.6 5.1 %collective-permute-start.3 = (f32[72,128]{1,0:T(8,128)}, f32[72,128]{1,0:T(8,128)S(1)}, u32[]{:S(2)}, u32[]{:S(2)}) collective-permute-start(f32[72,128]{1,0:T(8,128)} %get-tuple-element.48), channel_id=1, source_target_pairs={{0,24},{8,16},{16,8},{24,0},{1,25},{9,17},{17,9},{25,1},{2,26},{10... | collective-permute-start | bytes 110600 | tf_op jit(solution)/shard_map/ppermute | solution.py:38
  10.1 0.8 %copy-start = (f32[80,128]{1,0:T(8,128)S(1)}, f32[80,128]{1,0:T(8,128)}, u32[]{:S(2)}) copy-start(f32[80,128]{1,0:T(8,128)} %get-tuple-element.40.own) | copy-start | bytes 122884
  10.8 0.7 %copy-start.1 = (s32[8,8]{1,0:T(8,128)S(1)}, s32[8,8]{1,0:T(8,128)}, u32[]{:S(2)}) copy-start(s32[8,8]{1,0:T(8,128)} %pairs.1) | copy-start | bytes 772
  13.6 3.7 %copy-start.2 = (s32[4,1]{0,1:T(1,128)S(1)}, s32[4,1]{0,1:T(1,128)}, u32[]{:S(2)}) copy-start(s32[4,1]{0,1:T(1,128)} %param.13) | copy-start | bytes 52
  13.6 3.7 %copy-start.3 = (s32[4,1]{0,1:T(1,128)S(1)}, s32[4,1]{0,1:T(1,128)}, u32[]{:S(2)}) copy-start(s32[4,1]{0,1:T(1,128)} %param.14) | copy-start | bytes 52
  17.2 4.6 %collective-permute-start.4 = (f32[8,128]{1,0:T(8,128)S(1)}, f32[8,128]{1,0:T(8,128)S(1)}, u32[]{:S(2)}, u32[]{:S(2)}) collective-permute-start(f32[8,128]{1,0:T(8,128)S(1)} %get-tuple-element.49), channel_id=1, source_target_pairs={{0,4},{1,5},{2,6},{3,7},{4,0},{5,1},{6,2},{7,3},{8,12},{9,13},{10,... | collective-permute-start | bytes 12296 | tf_op jit(solution)/shard_map/ppermute | solution.py:514
  21.8 4.0 %collective-permute-start.5 = (f32[8,128]{1,0:T(8,128)S(1)}, f32[8,128]{1,0:T(8,128)S(1)}, u32[]{:S(2)}, u32[]{:S(2)}) collective-permute-start(f32[8,128]{1,0:T(8,128)S(1)} %min.18), channel_id=1, source_target_pairs={{0,16},{8,24},{16,0},{24,8},{1,17},{9,25},{17,1},{25,9},{2,18},{10... | collective-permute-start | bytes 12296 | tf_op jit(solution)/shard_map/ppermute | solution.py:514
  23.3 7.2 %collective-permute-start.7 = (f32[64,128]{1,0:T(8,128)S(1)}, f32[64,128]{1,0:T(8,128)S(1)}, u32[]{:S(2)}, u32[]{:S(2)}) collective-permute-start(f32[64,128]{1,0:T(8,128)S(1)} %get-tuple-element.63), channel_id=1, source_target_pairs={{0,1},{1,0},{2,3},{3,2},{4,5},{5,4},{6,7},{7,6},{8,9},{9,8},{10,11... | collective-permute-start | bytes 98312 | tf_op jit(solution)/shard_map/ppermute | solution.py:38
  23.3 7.2 %collective-permute-start.8 = (f32[64,128]{1,0:T(8,128)S(1)}, f32[64,128]{1,0:T(8,128)S(1)}, u32[]{:S(2)}, u32[]{:S(2)}) collective-permute-start(f32[64,128]{1,0:T(8,128)S(1)} %get-tuple-element.64), channel_id=1, source_target_pairs={{0,8},{8,0},{16,24},{24,16},{1,9},{9,1},{17,25},{25,17},{2,10},{10... | collective-permute-start | bytes 98312 | tf_op jit(solution)/shard_map/ppermute | solution.py:38
  23.9 6.7 %collective-permute-start.9 = (f32[64,128]{1,0:T(8,128)S(1)}, f32[64,128]{1,0:T(8,128)S(1)}, u32[]{:S(2)}, u32[]{:S(2)}) collective-permute-start(f32[64,128]{1,0:T(8,128)S(1)} %get-tuple-element.65), channel_id=1, source_target_pairs={{0,7},{1,2},{2,1},{3,4},{4,3},{5,6},{6,5},{7,0},{8,15},{9,10},{10,... | collective-permute-start | bytes 98312 | tf_op jit(solution)/shard_map/ppermute | solution.py:38
  24.4 6.2 %collective-permute-start.10 = (f32[64,128]{1,0:T(8,128)S(1)}, f32[64,128]{1,0:T(8,128)S(1)}, u32[]{:S(2)}, u32[]{:S(2)}) collective-permute-start(f32[64,128]{1,0:T(8,128)S(1)} %get-tuple-element.66), channel_id=1, source_target_pairs={{0,24},{8,16},{16,8},{24,0},{1,25},{9,17},{17,9},{25,1},{2,26},{10... | collective-permute-start | bytes 98312 | tf_op jit(solution)/shard_map/ppermute | solution.py:38
  25.8 4.7 %collective-permute-start.6 = (f32[8,128]{1,0:T(8,128)S(1)}, f32[8,128]{1,0:T(8,128)S(1)}, u32[]{:S(2)}, u32[]{:S(2)}) collective-permute-start(f32[8,128]{1,0:T(8,128)S(1)} %min.19), channel_id=1, source_target_pairs={{0,8},{8,0},{16,24},{24,16},{1,9},{9,1},{17,25},{25,17},{2,10},{10... | collective-permute-start | bytes 12296 | tf_op jit(solution)/shard_map/ppermute | solution.py:514
  30.6 7.3 %collective-permute-start.13 = (f32[8,128]{1,0:T(8,128)S(1)}, f32[8,128]{1,0:T(8,128)S(1)}, u32[]{:S(2)}, u32[]{:S(2)}) collective-permute-start(f32[8,128]{1,0:T(8,128)S(1)} %min.20), channel_id=1, source_target_pairs={{0,3},{1,2},{2,1},{3,0},{4,7},{5,6},{6,5},{7,4},{8,11},{9,10},{10,... | collective-permute-start | bytes 12296 | tf_op jit(solution)/shard_map/ppermute | solution.py:610
  32.8 5.1 %collective-permute-start.12 = (f32[8,128]{1,0:T(8,128)S(1)}, f32[8,128]{1,0:T(8,128)S(1)}, u32[]{:S(2)}, u32[]{:S(2)}) collective-permute-start(f32[8,128]{1,0:T(8,128)S(1)} %min.20), channel_id=1, source_target_pairs={{0,2},{1,3},{2,0},{3,1},{4,6},{5,7},{6,4},{7,5},{8,10},{9,11},{10,... | collective-permute-start | bytes 12296 | tf_op jit(solution)/shard_map/ppermute | solution.py:610
  32.8 5.1 %collective-permute-start.11 = (f32[8,128]{1,0:T(8,128)S(1)}, f32[8,128]{1,0:T(8,128)S(1)}, u32[]{:S(2)}, u32[]{:S(2)}) collective-permute-start(f32[8,128]{1,0:T(8,128)S(1)} %min.20), channel_id=1, source_target_pairs={{0,1},{1,0},{2,3},{3,2},{4,5},{5,4},{6,7},{7,6},{8,9},{9,8},{10,11... | collective-permute-start | bytes 12296 | tf_op jit(solution)/shard_map/ppermute | solution.py:610

commit v7 on v6

--- a/solution.py
+++ b/solution.py
@@ -16,6 +16,7 @@
 lanes = 128
 tiny = 1e-12
 chunk = 32
+narrow_rows = 16
 swaps = (("dom", 0, 2), ("slab", 0, 0), ("dom", 1, 2), ("slab", 1, 0))
 vmem_spec = pl.BlockSpec(memory_space=pltpu.VMEM)
 smem_spec = pl.BlockSpec(memory_space=pltpu.SMEM)
@@ -171,7 +172,27 @@
     lax.fori_loop(0, (last - first) // 2, step, 0, unroll=True)
 
 
-def own_kernel(pairs, own, left, columns, table, plan):
+def spline(ratio):
+    wide = jnp.maximum(1.0 - ratio, 0.0)
+    narrow = jnp.maximum(0.5 - ratio, 0.0)
+    twice = narrow + narrow
+    return wide * wide * wide - twice * twice * narrow
+
+
+def pair_weight(dist, rate, mean_len, sounds):
+    inv_len = 1.0 / mean_len
+    ratio = dist * inv_len
+    wide = jnp.maximum(20.0 - ratio, 0.0) * inv_len
+    narrow = jnp.maximum(10.0 - ratio, 0.0) * inv_len
+    twice = narrow + narrow
+    weight = wide * wide * wide - twice * twice * narrow
+    rate = jnp.minimum(rate, 0.0)
+    return weight, weight * rate * (rate - sounds)
+
+
+def own_kernel(
+    pairs, own, left, columns, table, plan, self_kernel, self_signal, self_weight, self_damping
+):
     table[...] = own[...]
     plan[...] = pairs[...]
 
@@ -180,12 +201,35 @@
         centred = tile - centre_of(tile)
         stacked = jnp.concatenate([own_distance(centred), own_closing(centred, 30.0)], axis=0)
         at = pl.ds(pl.multiple_of(block * lanes, lanes), lanes)
-        left[at, :] = stacked.T.astype(bf16)
+        operand = stacked.T.astype(bf16)
+        left[at, :] = operand
         turned = tile.T
         length = turned[:, 3:4]
         columns[at, 0:lanes] = jnp.broadcast_to(length * 0.05, (lanes, lanes))
         columns[at, lanes : 2 * lanes] = jnp.broadcast_to(turned[:, 7:8] * 0.75, (lanes, lanes))
         columns[at, 2 * lanes :] = jnp.broadcast_to(0.5 / length, (lanes, lanes))
+        near = near_operand(centred)
+        empty = jnp.zeros_like(near)
+        near = jnp.concatenate(
+            [jnp.concatenate([near, empty], axis=1), jnp.concatenate([empty, near], axis=1)], axis=0
+        )
+        both = jnp.dot(operand, near, preferred_element_type=f32)
+        dist_sq = jnp.maximum(both[:, 0:lanes], tiny)
+        dist = dist_sq * lax.rsqrt(dist_sq)
+        mean_len = columns[at, 0:lanes] + tile[3:4] * 0.05
+        rate = both[:, lanes:] * mean_len / (dist_sq + mean_len * mean_len)
+        to = pl.multiple_of(block * 2 * lanes, lanes)
+        high, low = split2(spline(dist * columns[at, 2 * lanes :]))
+        self_kernel[pl.ds(to, lanes), :] = high
+        self_kernel[pl.ds(to + lanes, lanes), :] = low
+        self_signal[at, :] = tile[7:8] - rate
+        weight, damping = pair_weight(
+            dist, rate, mean_len, columns[at, lanes : 2 * lanes] + tile[7:8] * 0.75
+        )
+        self_damping[at, :] = damping
+        high, low = split2(weight)
+        self_weight[pl.ds(to, lanes), :] = high
+        self_weight[pl.ds(to + lanes, lanes), :] = low
         return 0
 
     lax.fori_loop(0, 8, step, 0, unroll=True)
@@ -199,8 +243,11 @@
 
 
 def clear_near(buffers):
+    empty = jnp.zeros((64, lanes), bf16)
     for near in buffers:
-        near[...] = jnp.zeros(near.shape, bf16)
+        for k in range(8):
+            near[0:64, (2 * k + 1) * lanes : (2 * k + 2) * lanes] = empty
+            near[64:128, 2 * k * lanes : (2 * k + 1) * lanes] = empty
 
 
 def pair_dots(left, near, block, k):
@@ -211,25 +258,26 @@
 
 
 def signal_kernel(
-    plan, left, columns, own, m0, m1, m2, m3, allowed, smallest, distance, rates, table, *near
+    plan, left, columns, self_signal, own, m0, m1, m2, m3,
+    allowed, smallest, distance, rates, table, *near
 ):
     clear_near(near)
     fill_table(own, (m0, m1, m2, m3), table, rows)
 
     def prepare(block, buf):
         centre = centre_of(tile_at(table, block))
-        for k in range(8):
+        for k in range(1, 8):
             put_near(near[buf], k, tile_at(table, plan[k, block]) - centre)
 
     def finish(block, buf):
-        best = None
-        sounds = None
-        for k in range(8):
+        at = pl.ds(pl.multiple_of(block * lanes, lanes), lanes)
+        best = self_signal[at, :]
+        sounds = tile_at(table, block)[7:8]
+        for k in range(1, 8):
             tile = tile_at(table, plan[k, block])
             len_row, sound_row = tile[3:4] * 0.05, tile[7:8]
-            sounds = sound_row if k == 0 else jnp.maximum(sounds, sound_row)
+            sounds = jnp.maximum(sounds, sound_row)
             part = slice(k * lanes, (k + 1) * lanes)
-            at = pl.ds(pl.multiple_of(block * lanes, lanes), lanes)
             dist_sq, closing = pair_dots(left, near[buf], block, k)
             dist_sq = jnp.maximum(dist_sq, tiny)
             distance[at, part] = dist_sq * lax.rsqrt(dist_sq)
@@ -237,7 +285,7 @@
             rate = closing * mean_len / (dist_sq + mean_len * mean_len)
             rates[at, part] = rate
             signal = sound_row - rate
-            best = signal if k == 0 else jnp.maximum(best, signal)
+            best = jnp.maximum(best, signal)
         top = jnp.max(best.T, axis=0, keepdims=True)
         top = jnp.maximum(top, jnp.max(sounds, axis=1, keepdims=True))
         own_tile = tile_at(table, block)
@@ -249,7 +297,7 @@
 
 
 def density_kernel(
-    plan, offsets, counts, columns, distance, own, m0, m1, m2, m3, second, *rest
+    plan, offsets, counts, columns, distance, self_kernel, own, m0, m1, m2, m3, second, *rest
 ):
     outgoing = rest[0:4]
     table, masses, sums, *scratch = rest[4:]
@@ -273,16 +321,14 @@
             feats[buf][32:64, part] = low
 
     def finish(block, buf):
+        both = pl.ds(pl.multiple_of(block * 2 * lanes, lanes), 2 * lanes)
+        weights[buf][:, 0:lanes] = self_kernel[both, :]
         for start in range(0, lanes, 2 * chunk):
             at = pl.ds(pl.multiple_of(block * lanes + start, 2 * chunk), 2 * chunk)
             scale = columns[at, 2 * lanes :]
-            for k in range(8):
+            for k in range(1, 8):
                 part = slice(k * lanes, (k + 1) * lanes)
-                ratio = distance[at, part] * scale
-                wide = jnp.maximum(1.0 - ratio, 0.0)
-                narrow = jnp.maximum(0.5 - ratio, 0.0)
-                twice = narrow + narrow
-                high, low = split2(wide * wide * wide - twice * twice * narrow)
+                high, low = split2(spline(distance[at, part] * scale))
                 weights[buf][start : start + 2 * chunk, part] = high
                 weights[buf][lanes + start : lanes + start + 2 * chunk, part] = low
         out = lax.dot_general(
@@ -332,7 +378,7 @@
 
 
 def weight_kernel(
-    first, plan, columns, distance, rates, second, own, m0, m1, m2, m3,
+    first, plan, columns, distance, rates, self_weight, self_damping, second, own, m0, m1, m2, m3,
     weights, damping, dens_col, table
 ):
     fill_table(own, (m0, m1, m2, m3), table, rows)
@@ -342,26 +388,27 @@
         turned = jnp.broadcast_to(second[pl.ds(block * rows, 1), :], (lanes, lanes)).T
         dens_col[pl.ds(pl.multiple_of(place * lanes, lanes), lanes), :] = turned
         tiles = [tile_at(table, plan[k, block]) for k in range(8)]
-        for start in range(0, lanes, chunk):
-            at = pl.ds(pl.multiple_of(block * lanes + start, chunk), chunk)
-            to = pl.ds(pl.multiple_of(place * lanes + start, chunk), chunk)
+        for start in range(0, lanes, narrow_rows):
+            at = pl.ds(pl.multiple_of(block * lanes + start, narrow_rows), narrow_rows)
+            to = pl.ds(pl.multiple_of(place * lanes + start, narrow_rows), narrow_rows)
             len_own = columns[at, 0:lanes]
             sound_own = columns[at, lanes : 2 * lanes]
-            for k in range(8):
+            damping[to, 0:lanes] = self_damping[at, :]
+            for k in range(1, 8):
                 part = slice(k * lanes, (k + 1) * lanes)
-                inv_len = 1.0 / (len_own + tiles[k][3:4] * 0.05)
-                ratio = distance[at, part] * inv_len
-                wide = jnp.maximum(20.0 - ratio, 0.0) * inv_len
-                narrow = jnp.maximum(10.0 - ratio, 0.0) * inv_len
-                twice = narrow + narrow
-                weight = wide * wide * wide - twice * twice * narrow
-                rate = jnp.minimum(rates[at, part], 0.0)
-                sounds = sound_own + tiles[k][7:8] * 0.75
-                damping[to, part] = weight * rate * (rate - sounds)
+                weight, damped = pair_weight(
+                    distance[at, part],
+                    rates[at, part],
+                    len_own + tiles[k][3:4] * 0.05,
+                    sound_own + tiles[k][7:8] * 0.75,
+                )
+                damping[to, part] = damped
                 high, low = split2(weight)
-                base = pl.multiple_of(place * 2 * lanes + start, chunk)
-                weights[pl.ds(base, chunk), part] = high
-                weights[pl.ds(base + lanes, chunk), part] = low
+                base = pl.multiple_of(place * 2 * lanes + start, narrow_rows)
+                weights[pl.ds(base, narrow_rows), part] = high
+                weights[pl.ds(base + lanes, narrow_rows), part] = low
+        both = pl.ds(pl.multiple_of(place * 2 * lanes, lanes), 2 * lanes)
+        weights[both, 0:lanes] = self_weight[both, :]
         return 0
 
     lax.fori_loop(0, 8, step, 0, unroll=2)
@@ -537,16 +584,20 @@
     last = (1, 2, 3)
     steps = [("dom", 1 << bit) for bit in range(2, lax.axis_size("dom").bit_length() - 1)]
     steps += [("slab", 1 << bit) for bit in reversed(range(lax.axis_size("slab").bit_length() - 1))]
-    left, columns, own, plan = pl.pallas_call(
+    left, columns, own, plan, self_kernel, self_signal, self_weight, self_damping = pl.pallas_call(
         own_kernel,
         out_shape=[
             jax.ShapeDtypeStruct((8 * lanes, lanes), bf16),
             jax.ShapeDtypeStruct((8 * lanes, 3 * lanes), f32),
             jax.ShapeDtypeStruct((80, lanes), f32),
             jax.ShapeDtypeStruct(pair_blocks.shape, jnp.int32),
+            jax.ShapeDtypeStruct((16 * lanes, lanes), bf16),
+            jax.ShapeDtypeStruct((8 * lanes, lanes), f32),
+            jax.ShapeDtypeStruct((16 * lanes, lanes), bf16),
+            jax.ShapeDtypeStruct((8 * lanes, lanes), f32),
         ],
         in_specs=[vmem_spec] * 2,
-        out_specs=[vmem_spec] * 4,
+        out_specs=[vmem_spec] * 8,
         compiler_params=pltpu.CompilerParams(vmem_limit_bytes=8 * 1024 * 1024),
     )(pair_blocks, own)
     table = ((328, lanes), f32)
@@ -560,7 +611,7 @@
         [tile, tile, square, square],
         [table, near, near],
         1,
-        (plan, left, columns, own, *received),
+        (plan, left, columns, self_signal, own, *received),
         3 * 10**9,
         20,
     )
@@ -570,7 +621,7 @@
         [packed] + [((64, lanes), f32)] * 4,
         [table, masses, ((9 * 32, lanes), f32)] + [feats] * 2 + [halves] * 2,
         3,
-        (plan, send_offsets, send_counts, columns, distance, own, *received),
+        (plan, send_offsets, send_counts, columns, distance, self_kernel, own, *received),
         5 * 10**9,
         20,
     )
@@ -585,7 +636,7 @@
             [((16 * lanes, 8 * lanes), bf16), ((8 * lanes, 8 * lanes), f32), ((8 * lanes, lanes), f32)],
             [table],
             1,
-            (plan, columns, distance, rates, second, own, *received),
+            (plan, columns, distance, rates, self_weight, self_damping, second, own, *received),
             10**9,
             20,
         )

time: 38.8 us -> 38.3 us (0.987)
    pallas_call x4, Pallas kernels: 17.1 us -> 16.2 us  [call(): pl.pallas_call(kernel, out_shape=[jax.ShapeDtypeStruct(shape, kind) for s...]
    ppermute x3, starting transfers between devices: 2.05 us -> 2.64 us  [fold(): lax.ppermute(value, axis, [(i, i ^ step) for i in range(size)])]
    ppermute x8, waiting for transfers between devices: 1.21 us -> 0.64 us  [swap(): return lax.ppermute(value, axis, pairs)]
    pallas_call x1, Pallas kernels: 0.88 us -> 1.45 us  [body(): pl.pallas_call(own_kernel, out_shape=[jax.ShapeDtypeStruct((8 * lanes, la...]
  transfers between devices with their start and end apart: 14 -> 14, of which waited for: 2 -> 2; matrix products, arithmetic and copies ran while one was open for 0% -> 0% of each run, Pallas kernels for 37% -> 38%
where the time goes in v7:
time: 38.3 us; the launch traced here: 38.1 us
  Pallas kernels  19.3 us (50%)
  starting transfers between devices  14.9 us (39%)
  local copies, waits for them, and re-layouts  1.47 us (4%)
  waiting for transfers between devices  1.04 us (3%)
  between operations  0.78 us (2%)
  other arithmetic  0.61 us (2%)
    pallas_call x4, Pallas kernels, call(): pl.pallas_call(kernel, out_shape=[jax.ShapeDtypeStruct(shape, kind) for s...  16.2 us
    ppermute x8, starting transfers between devices, swap(): return lax.ppermute(value, axis, pairs)  10.1 us
    ppermute x3, starting transfers between devices, fold(): lax.ppermute(value, axis, [(i, i ^ step) for i in range(size)])  2.64 us
    ppermute x3, starting transfers between devices, body(): lax.ppermute(smallest, 'dom', [(i, i ^ step) for i in range(size)])  2.15 us
    pallas_call x1, Pallas kernels, body(): pl.pallas_call(pack_kernel, out_shape=[jax.ShapeDtypeStruct((80, lanes),...  1.56 us
    unnamed x8, local copies, waits for them, and re-layouts  1.47 us
    pallas_call x1, Pallas kernels, body(): pl.pallas_call(own_kernel, out_shape=[jax.ShapeDtypeStruct((8 * lanes, la...  1.45 us
  transfers between devices with their start and end apart: 14, of which 2 were waited for; matrix products, arithmetic and copies ran while one was open for 0% of the time, Pallas kernels for 38%

profile of v7, /device:TPU:0, one launch (start us, length us, event | category | flops | bytes accessed | tf_op | source)
XLA Modules:
  0.0 38.1 jit_solution(13205425456435909911)
XLA Ops:
  0.6 1.6 %shard_map.111 = (f32[80,128]{1,0:T(8,128)}, f32[72,128]{1,0:T(8,128)}, f32[72,128]{1,0:T(8,128)}, f32[72,128]{1,0:T(8,128)}, f32[72,128]{1,0:T(8,128)}) custom-call(f32[3,1024]{1,0:T(4,128)} %positions.1, f32[3,1024]{1,0:T(4,128)} %velocities.1, f32[8,128]{1,0:T(8,128)} %bitcast.13, f32[8,128]{1,0:T(8,128)} %bitcast.14, f32[8,128]{1,0:T(8,128)} %bitcast.15, ...), custom_call_target="tpu_custom_call" | custom-call | tf_op jit(solution)/shard_map/pallas_call | solution.py:569
  2.2 0.5 %collective-permute-start = (f32[72,128]{1,0:T(8,128)}, f32[72,128]{1,0:T(8,128)S(1)}, u32[]{:S(2)}, u32[]{:S(2)}) collective-permute-start(f32[72,128]{1,0:T(8,128)} %get-tuple-element.50), channel_id=1, source_target_pairs={{0,1},{1,0},{2,3},{3,2},{4,5},{5,4},{6,7},{7,6},{8,9},{9,8},{10,11... | collective-permute-start | bytes 110600 | tf_op jit(solution)/shard_map/ppermute | solution.py:39
  2.6 2.5 %collective-permute-start.1 = (f32[72,128]{1,0:T(8,128)}, f32[72,128]{1,0:T(8,128)S(1)}, u32[]{:S(2)}, u32[]{:S(2)}) collective-permute-start(f32[72,128]{1,0:T(8,128)} %get-tuple-element.51), channel_id=1, source_target_pairs={{0,8},{8,0},{16,24},{24,16},{1,9},{9,1},{17,25},{25,17},{2,10},{10... | collective-permute-start | bytes 110600 | tf_op jit(solution)/shard_map/ppermute | solution.py:39
  5.2 3.4 %collective-permute-start.2 = (f32[72,128]{1,0:T(8,128)}, f32[72,128]{1,0:T(8,128)S(1)}, u32[]{:S(2)}, u32[]{:S(2)}) collective-permute-start(f32[72,128]{1,0:T(8,128)} %get-tuple-element.52), channel_id=1, source_target_pairs={{0,7},{1,2},{2,1},{3,4},{4,3},{5,6},{6,5},{7,0},{8,15},{9,10},{10,... | collective-permute-start | bytes 110600 | tf_op jit(solution)/shard_map/ppermute | solution.py:39
  8.6 1.5 %collective-permute-start.3 = (f32[72,128]{1,0:T(8,128)}, f32[72,128]{1,0:T(8,128)S(1)}, u32[]{:S(2)}, u32[]{:S(2)}) collective-permute-start(f32[72,128]{1,0:T(8,128)} %get-tuple-element.53), channel_id=1, source_target_pairs={{0,24},{8,16},{16,8},{24,0},{1,25},{9,17},{17,9},{25,1},{2,26},{10... | collective-permute-start | bytes 110600 | tf_op jit(solution)/shard_map/ppermute | solution.py:39
  10.1 0.0 copy-start
  10.1 0.8 %copy-done = f32[80,128]{1,0:T(8,128)S(1)} copy-done((f32[80,128]{1,0:T(8,128)S(1)}, f32[80,128]{1,0:T(8,128)}, u32[]{:S(2)}) %copy-start) | copy-done | bytes 40984
  10.8 0.0 copy-start.1
  10.8 0.7 %copy-done.1 = s32[8,8]{1,0:T(8,128)S(1)} copy-done((s32[8,8]{1,0:T(8,128)S(1)}, s32[8,8]{1,0:T(8,128)}, u32[]{:S(2)}) %copy-start.1) | copy-done | bytes 280
  11.5 1.4 %shard_map.112 = (bf16[1024,128]{1,0:T(8,128)(2,1)S(1)}, f32[1024,384]{1,0:T(8,128)S(1)}, f32[80,128]{1,0:T(8,128)S(1)}, s32[8,8]{1,0:T(8,128)S(1)}, bf16[2048,1...) custom-call(s32[8,8]{1,0:T(8,128)S(1)} %copy-done.1, ...), custom_call_target="tpu_custom_call" | custom-call | tf_op jit(solution)/shard_map/pallas_call | solution.py:587
  13.0 0.0 collective-permute-done.m0
  13.0 0.0 collective-permute-done.1.m1
  13.0 0.0 collective-permute-done.2.m2
  13.0 0.6 %collective-permute-done.3.m3 = f32[72,128]{1,0:T(8,128)S(1)} collective-permute-done((f32[72,128]{1,0:T(8,128)}, f32[72,128]{1,0:T(8,128)S(1)}, u32[]{:S(2)}, u32[]{:S(2)}) %collective-permute-start.3) | collective-permute-done | bytes 36896 | tf_op jit(solution)/shard_map/ppermute | solution.py:39
  13.6 0.0 copy-start.2
  13.6 0.0 copy-start.3
  13.6 3.3 %shard_map.113 = (f32[8,128]{1,0:T(8,128)S(1)}, f32[8,128]{1,0:T(8,128)S(1)}, f32[1024,1024]{1,0:T(8,128)S(1)}, f32[1024,1024]{1,0:T(8,128)S(1)}) custom-call(s32[8,8]{1,0:T(8,128)S(1)} %get-tuple-element.45.plan, bf16[1024,128]{1,0:T(8,128)(2,1)S(1)} %get-tuple-element.46.left, f32[1024,384]{1,0:T(8,128)S(1)} %get-tuple-element.47.columns, ...), custom_call_target="tpu_custom_call" | custom-call | flops 3000000000 | bytes 200000 | tf_op jit(solution)/shard_map/pallas_call | solution.py:548
  17.0 0.1 collective-permute-start.4
  17.0 0.0 copy-done.2
  17.0 0.0 copy-done.3
  17.1 4.1 %shard_map.114 = (f32[72,128]{1,0:T(8,128)S(1)}, f32[64,128]{1,0:T(8,128)S(1)}, f32[64,128]{1,0:T(8,128)S(1)}, f32[64,128]{1,0:T(8,128)S(1)}, f32[64,128]{1,0:T(8,128)S(1)}) custom-call(s32[8,8]{1,0:T(8,128)S(1)} %get-tuple-element.45.plan, s32[1,4]{1,0:T(1,128)S(1)} %bitcast.10, s32[1,4]{1,0:T(1,128)S(1)} %bitcast.12, ...), custom_call_target="tpu_custom_call" | custom-call | flops 5000000000 | bytes 200000 | tf_op jit(solution)/shard_map/pallas_call | solution.py:548
  21.1 0.4 %collective-permute-done.4 = f32[8,128]{1,0:T(8,128)S(1)} collective-permute-done((f32[8,128]{1,0:T(8,128)S(1)}, f32[8,128]{1,0:T(8,128)S(1)}, u32[]{:S(2)}, u32[]{:S(2)}) %collective-permute-start.4) | collective-permute-done | bytes 4128 | tf_op jit(solution)/shard_map/ppermute | solution.py:561
  21.5 1.5 %collective-permute-start.5 = (f32[8,128]{1,0:T(8,128)S(1)}, f32[8,128]{1,0:T(8,128)S(1)}, u32[]{:S(2)}, u32[]{:S(2)}) collective-permute-start(f32[8,128]{1,0:T(8,128)S(1)} %min.18), channel_id=1, source_target_pairs={{0,16},{8,24},{16,0},{24,8},{1,17},{9,25},{17,1},{25,9},{2,18},{10... | collective-permute-start | bytes 12296 | tf_op jit(solution)/shard_map/ppermute | solution.py:561
  23.1 0.0 collective-permute-start.7
  23.1 0.5 %collective-permute-start.8 = (f32[64,128]{1,0:T(8,128)S(1)}, f32[64,128]{1,0:T(8,128)S(1)}, u32[]{:S(2)}, u32[]{:S(2)}) collective-permute-start(f32[64,128]{1,0:T(8,128)S(1)} %get-tuple-element.72), channel_id=1, source_target_pairs={{0,8},{8,0},{16,24},{24,16},{1,9},{9,1},{17,25},{25,17},{2,10},{10... | collective-permute-start | bytes 98312 | tf_op jit(solution)/shard_map/ppermute | solution.py:39
  23.6 0.3 collective-permute-start.9
  23.9 1.4 %collective-permute-start.10 = (f32[64,128]{1,0:T(8,128)S(1)}, f32[64,128]{1,0:T(8,128)S(1)}, u32[]{:S(2)}, u32[]{:S(2)}) collective-permute-start(f32[64,128]{1,0:T(8,128)S(1)} %get-tuple-element.74), channel_id=1, source_target_pairs={{0,24},{8,16},{16,8},{24,0},{1,25},{9,17},{17,9},{25,1},{2,26},{10... | collective-permute-start | bytes 98312 | tf_op jit(solution)/shard_map/ppermute | solution.py:39
  25.3 0.0 collective-permute-done.5
  25.3 1.0 %collective-permute-start.6 = (f32[8,128]{1,0:T(8,128)S(1)}, f32[8,128]{1,0:T(8,128)S(1)}, u32[]{:S(2)}, u32[]{:S(2)}) collective-permute-start(f32[8,128]{1,0:T(8,128)S(1)} %min.19), channel_id=1, source_target_pairs={{0,8},{8,0},{16,24},{24,16},{1,9},{9,1},{17,25},{25,17},{2,10},{10... | collective-permute-start | bytes 12296 | tf_op jit(solution)/shard_map/ppermute | solution.py:561
  26.4 3.9 %shard_map.115 = (bf16[2048,1024]{1,0:T(8,128)(2,1)S(1)}, f32[1024,1024]{1,0:T(8,128)S(1)}, f32[1024,128]{1,0:T(8,128)S(1)}) custom-call(s32[8,8]{1,0:T(8,128)S(1)} %get-tuple-element.45.plan, f32[1024,384]{1,0:T(8,128)S(1)} %get-tuple-element.47.columns, f32[1024,1024]{1,0:T(8,128)S(1)} %get-tuple-element.55.distance, ...), custom_call_target="tpu_custom_call" | custom-call | flops 1000000000 | bytes 200000 | tf_op jit(solution)/shard_map/pallas_call | solution.py:548
  30.3 0.0 collective-permute-done.6
  30.3 0.0 collective-permute-done.7.s0
  30.3 0.0 collective-permute-done.8.s1
  30.3 0.0 collective-permute-done.9.s2
  30.3 0.0 collective-permute-done.10.s3
  30.3 2.0 %collective-permute-start.13 = (f32[8,128]{1,0:T(8,128)S(1)}, f32[8,128]{1,0:T(8,128)S(1)}, u32[]{:S(2)}, u32[]{:S(2)}) collective-permute-start(f32[8,128]{1,0:T(8,128)S(1)} %min.20), channel_id=1, source_target_pairs={{0,3},{1,2},{2,1},{3,0},{4,7},{5,6},{6,5},{7,4},{8,11},{9,10},{10,... | collective-permute-start | bytes 12296 | tf_op jit(solution)/shard_map/ppermute | solution.py:661
  32.3 0.0 collective-permute-start.12
  32.3 0.2 collective-permute-start.11
  32.5 5.0 %shard_map.116 = (f32[3,1024]{1,0:T(4,128)}, f32[8,128]{1,0:T(8,128)}, f32[8,128]{1,0:T(8,128)}) custom-call(s32[8,8]{1,0:T(8,128)S(1)} %get-tuple-element.45.plan, bf16[2048,1024]{1,0:T(8,128)(2,1)S(1)} %get-tuple-element.67.weights, f32[1024,1024]{1,0:T(8,128)S(1)} %get-tuple-element.68.damping, f32[1024,128]{1,0:T(8,128)S(1)} %get-tuple-element.69.dens_col, ...), custom_call_target="tpu_custom_call" | custom-call | flops 5000000000 | bytes 200000 | tf_op jit(solution)/shard_map/pallas_call | solution.py:548
  37.5 0.0 collective-permute-done.13
  37.5 0.0 collective-permute-done.12
  37.5 0.0 collective-permute-done.11
  37.5 0.6 %divide_bitcast_fusion = f32[1024]{0:T(1024)} fusion(f32[8,128]{1,0:T(8,128)S(1)} %get-tuple-element.83, f32[8,128]{1,0:T(8,128)S(1)} %collective-permute-done.13, f32[8,128]{1,0:T(8,128)S(1)} %collective-permute-done.12, f32[8,128]{1,0:T(8,128)S(1)} %min.20, f32[8,128]{1,0:T(8,128)S(1)} %collective-permute-done.11), kind=kLoop, calls=%fused_computation | loop fusion | flops 4096 | bytes 24576 | tf_op jit(solution)/shard_map/reshape | solution.py:666
  (3 shorter events, 0.0 us)
Async XLA Ops:
  2.2 10.8 %collective-permute-start = (f32[72,128]{1,0:T(8,128)}, f32[72,128]{1,0:T(8,128)S(1)}, u32[]{:S(2)}, u32[]{:S(2)}) collective-permute-start(f32[72,128]{1,0:T(8,128)} %get-tuple-element.50), channel_id=1, source_target_pairs={{0,1},{1,0},{2,3},{3,2},{4,5},{5,4},{6,7},{7,6},{8,9},{9,8},{10,11... | collective-permute-start | bytes 110600 | tf_op jit(solution)/shard_map/ppermute | solution.py:39
  2.6 10.3 %collective-permute-start.1 = (f32[72,128]{1,0:T(8,128)}, f32[72,128]{1,0:T(8,128)S(1)}, u32[]{:S(2)}, u32[]{:S(2)}) collective-permute-start(f32[72,128]{1,0:T(8,128)} %get-tuple-element.51), channel_id=1, source_target_pairs={{0,8},{8,0},{16,24},{24,16},{1,9},{9,1},{17,25},{25,17},{2,10},{10... | collective-permute-start | bytes 110600 | tf_op jit(solution)/shard_map/ppermute | solution.py:39
  5.2 7.8 %collective-permute-start.2 = (f32[72,128]{1,0:T(8,128)}, f32[72,128]{1,0:T(8,128)S(1)}, u32[]{:S(2)}, u32[]{:S(2)}) collective-permute-start(f32[72,128]{1,0:T(8,128)} %get-tuple-element.52), channel_id=1, source_target_pairs={{0,7},{1,2},{2,1},{3,4},{4,3},{5,6},{6,5},{7,0},{8,15},{9,10},{10,... | collective-permute-start | bytes 110600 | tf_op jit(solution)/shard_map/ppermute | solution.py:39
  8.6 5.1 %collective-permute-start.3 = (f32[72,128]{1,0:T(8,128)}, f32[72,128]{1,0:T(8,128)S(1)}, u32[]{:S(2)}, u32[]{:S(2)}) collective-permute-start(f32[72,128]{1,0:T(8,128)} %get-tuple-element.53), channel_id=1, source_target_pairs={{0,24},{8,16},{16,8},{24,0},{1,25},{9,17},{17,9},{25,1},{2,26},{10... | collective-permute-start | bytes 110600 | tf_op jit(solution)/shard_map/ppermute | solution.py:39
  10.1 0.8 %copy-start = (f32[80,128]{1,0:T(8,128)S(1)}, f32[80,128]{1,0:T(8,128)}, u32[]{:S(2)}) copy-start(f32[80,128]{1,0:T(8,128)} %get-tuple-element.44.own) | copy-start | bytes 122884
  10.8 0.7 %copy-start.1 = (s32[8,8]{1,0:T(8,128)S(1)}, s32[8,8]{1,0:T(8,128)}, u32[]{:S(2)}) copy-start(s32[8,8]{1,0:T(8,128)} %pairs.1) | copy-start | bytes 772
  13.6 3.4 %copy-start.2 = (s32[4,1]{0,1:T(1,128)S(1)}, s32[4,1]{0,1:T(1,128)}, u32[]{:S(2)}) copy-start(s32[4,1]{0,1:T(1,128)} %param.13) | copy-start | bytes 52
  13.6 3.4 %copy-start.3 = (s32[4,1]{0,1:T(1,128)S(1)}, s32[4,1]{0,1:T(1,128)}, u32[]{:S(2)}) copy-start(s32[4,1]{0,1:T(1,128)} %param.14) | copy-start | bytes 52
  17.0 4.6 %collective-permute-start.4 = (f32[8,128]{1,0:T(8,128)S(1)}, f32[8,128]{1,0:T(8,128)S(1)}, u32[]{:S(2)}, u32[]{:S(2)}) collective-permute-start(f32[8,128]{1,0:T(8,128)S(1)} %get-tuple-element.54), channel_id=1, source_target_pairs={{0,4},{1,5},{2,6},{3,7},{4,0},{5,1},{6,2},{7,3},{8,12},{9,13},{10,... | collective-permute-start | bytes 12296 | tf_op jit(solution)/shard_map/ppermute | solution.py:561
  21.5 3.8 %collective-permute-start.5 = (f32[8,128]{1,0:T(8,128)S(1)}, f32[8,128]{1,0:T(8,128)S(1)}, u32[]{:S(2)}, u32[]{:S(2)}) collective-permute-start(f32[8,128]{1,0:T(8,128)S(1)} %min.18), channel_id=1, source_target_pairs={{0,16},{8,24},{16,0},{24,8},{1,17},{9,25},{17,1},{25,9},{2,18},{10... | collective-permute-start | bytes 12296 | tf_op jit(solution)/shard_map/ppermute | solution.py:561
  23.1 7.2 %collective-permute-start.7 = (f32[64,128]{1,0:T(8,128)S(1)}, f32[64,128]{1,0:T(8,128)S(1)}, u32[]{:S(2)}, u32[]{:S(2)}) collective-permute-start(f32[64,128]{1,0:T(8,128)S(1)} %get-tuple-element.71), channel_id=1, source_target_pairs={{0,1},{1,0},{2,3},{3,2},{4,5},{5,4},{6,7},{7,6},{8,9},{9,8},{10,11... | collective-permute-start | bytes 98312 | tf_op jit(solution)/shard_map/ppermute | solution.py:39
  23.1 7.2 %collective-permute-start.8 = (f32[64,128]{1,0:T(8,128)S(1)}, f32[64,128]{1,0:T(8,128)S(1)}, u32[]{:S(2)}, u32[]{:S(2)}) collective-permute-start(f32[64,128]{1,0:T(8,128)S(1)} %get-tuple-element.72), channel_id=1, source_target_pairs={{0,8},{8,0},{16,24},{24,16},{1,9},{9,1},{17,25},{25,17},{2,10},{10... | collective-permute-start | bytes 98312 | tf_op jit(solution)/shard_map/ppermute | solution.py:39
  23.6 6.7 %collective-permute-start.9 = (f32[64,128]{1,0:T(8,128)S(1)}, f32[64,128]{1,0:T(8,128)S(1)}, u32[]{:S(2)}, u32[]{:S(2)}) collective-permute-start(f32[64,128]{1,0:T(8,128)S(1)} %get-tuple-element.73), channel_id=1, source_target_pairs={{0,7},{1,2},{2,1},{3,4},{4,3},{5,6},{6,5},{7,0},{8,15},{9,10},{10,... | collective-permute-start | bytes 98312 | tf_op jit(solution)/shard_map/ppermute | solution.py:39
  23.9 6.5 %collective-permute-start.10 = (f32[64,128]{1,0:T(8,128)S(1)}, f32[64,128]{1,0:T(8,128)S(1)}, u32[]{:S(2)}, u32[]{:S(2)}) collective-permute-start(f32[64,128]{1,0:T(8,128)S(1)} %get-tuple-element.74), channel_id=1, source_target_pairs={{0,24},{8,16},{16,8},{24,0},{1,25},{9,17},{17,9},{25,1},{2,26},{10... | collective-permute-start | bytes 98312 | tf_op jit(solution)/shard_map/ppermute | solution.py:39
  25.3 4.9 %collective-permute-start.6 = (f32[8,128]{1,0:T(8,128)S(1)}, f32[8,128]{1,0:T(8,128)S(1)}, u32[]{:S(2)}, u32[]{:S(2)}) collective-permute-start(f32[8,128]{1,0:T(8,128)S(1)} %min.19), channel_id=1, source_target_pairs={{0,8},{8,0},{16,24},{24,16},{1,9},{9,1},{17,25},{25,17},{2,10},{10... | collective-permute-start | bytes 12296 | tf_op jit(solution)/shard_map/ppermute | solution.py:561
  30.3 7.1 %collective-permute-start.13 = (f32[8,128]{1,0:T(8,128)S(1)}, f32[8,128]{1,0:T(8,128)S(1)}, u32[]{:S(2)}, u32[]{:S(2)}) collective-permute-start(f32[8,128]{1,0:T(8,128)S(1)} %min.20), channel_id=1, source_target_pairs={{0,3},{1,2},{2,1},{3,0},{4,7},{5,6},{6,5},{7,4},{8,11},{9,10},{10,... | collective-permute-start | bytes 12296 | tf_op jit(solution)/shard_map/ppermute | solution.py:661
  32.3 5.2 %collective-permute-start.12 = (f32[8,128]{1,0:T(8,128)S(1)}, f32[8,128]{1,0:T(8,128)S(1)}, u32[]{:S(2)}, u32[]{:S(2)}) collective-permute-start(f32[8,128]{1,0:T(8,128)S(1)} %min.20), channel_id=1, source_target_pairs={{0,2},{1,3},{2,0},{3,1},{4,6},{5,7},{6,4},{7,5},{8,10},{9,11},{10,... | collective-permute-start | bytes 12296 | tf_op jit(solution)/shard_map/ppermute | solution.py:661
  32.3 5.2 %collective-permute-start.11 = (f32[8,128]{1,0:T(8,128)S(1)}, f32[8,128]{1,0:T(8,128)S(1)}, u32[]{:S(2)}, u32[]{:S(2)}) collective-permute-start(f32[8,128]{1,0:T(8,128)S(1)} %min.20), channel_id=1, source_target_pairs={{0,1},{1,0},{2,3},{3,2},{4,5},{5,4},{6,7},{7,6},{8,9},{9,8},{10,11... | collective-permute-start | bytes 12296 | tf_op jit(solution)/shard_map/ppermute | solution.py:661

commit v8 on v7

--- a/solution.py
+++ b/solution.py
@@ -581,7 +581,7 @@
         send_counts,
     )
     received = [swap(value, axis, odd) for value, (axis, odd, _) in zip(outgoing, swaps)]
-    last = (1, 2, 3)
+    last = (2, 3, 1)
     steps = [("dom", 1 << bit) for bit in range(2, lax.axis_size("dom").bit_length() - 1)]
     steps += [("slab", 1 << bit) for bit in reversed(range(lax.axis_size("slab").bit_length() - 1))]
     left, columns, own, plan, self_kernel, self_signal, self_weight, self_damping = pl.pallas_call(

time: 38.3 us -> 38.6 us (level)
  no operation moved by 1% of the time
where the time goes in v8:
time: 38.6 us; the launch traced here: 38.3 us
  Pallas kernels  19.3 us (50%)
  starting transfers between devices  15.1 us (39%)
  local copies, waits for them, and re-layouts  1.47 us (4%)
  waiting for transfers between devices  1.04 us (3%)
  between operations  0.79 us (2%)
  other arithmetic  0.61 us (2%)
    pallas_call x4, Pallas kernels, call(): pl.pallas_call(kernel, out_shape=[jax.ShapeDtypeStruct(shape, kind) for s...  16.3 us
    ppermute x8, starting transfers between devices, swap(): return lax.ppermute(value, axis, pairs)  10.1 us
    ppermute x3, starting transfers between devices, fold(): lax.ppermute(value, axis, [(i, i ^ step) for i in range(size)])  2.66 us
    ppermute x3, starting transfers between devices, body(): lax.ppermute(smallest, 'dom', [(i, i ^ step) for i in range(size)])  2.36 us
    pallas_call x1, Pallas kernels, body(): pl.pallas_call(pack_kernel, out_shape=[jax.ShapeDtypeStruct((80, lanes),...  1.56 us
    unnamed x8, local copies, waits for them, and re-layouts  1.47 us
    pallas_call x1, Pallas kernels, body(): pl.pallas_call(own_kernel, out_shape=[jax.ShapeDtypeStruct((8 * lanes, la...  1.45 us
  transfers between devices with their start and end apart: 14, of which 2 were waited for; matrix products, arithmetic and copies ran while one was open for 0% of the time, Pallas kernels for 38%

profile of v8, /device:TPU:0, one launch (start us, length us, event | category | flops | bytes accessed | tf_op | source)
XLA Modules:
  0.0 38.3 jit_solution(8142494549695562093)
XLA Ops:
  0.6 1.6 %shard_map.111 = (f32[80,128]{1,0:T(8,128)}, f32[72,128]{1,0:T(8,128)}, f32[72,128]{1,0:T(8,128)}, f32[72,128]{1,0:T(8,128)}, f32[72,128]{1,0:T(8,128)}) custom-call(f32[3,1024]{1,0:T(4,128)} %positions.1, f32[3,1024]{1,0:T(4,128)} %velocities.1, f32[8,128]{1,0:T(8,128)} %bitcast.13, f32[8,128]{1,0:T(8,128)} %bitcast.14, f32[8,128]{1,0:T(8,128)} %bitcast.15, ...), custom_call_target="tpu_custom_call" | custom-call | tf_op jit(solution)/shard_map/pallas_call | solution.py:569
  2.2 0.5 %collective-permute-start = (f32[72,128]{1,0:T(8,128)}, f32[72,128]{1,0:T(8,128)S(1)}, u32[]{:S(2)}, u32[]{:S(2)}) collective-permute-start(f32[72,128]{1,0:T(8,128)} %get-tuple-element.50), channel_id=1, source_target_pairs={{0,1},{1,0},{2,3},{3,2},{4,5},{5,4},{6,7},{7,6},{8,9},{9,8},{10,11... | collective-permute-start | bytes 110600 | tf_op jit(solution)/shard_map/ppermute | solution.py:39
  2.6 2.5 %collective-permute-start.1 = (f32[72,128]{1,0:T(8,128)}, f32[72,128]{1,0:T(8,128)S(1)}, u32[]{:S(2)}, u32[]{:S(2)}) collective-permute-start(f32[72,128]{1,0:T(8,128)} %get-tuple-element.51), channel_id=1, source_target_pairs={{0,8},{8,0},{16,24},{24,16},{1,9},{9,1},{17,25},{25,17},{2,10},{10... | collective-permute-start | bytes 110600 | tf_op jit(solution)/shard_map/ppermute | solution.py:39
  5.2 3.4 %collective-permute-start.2 = (f32[72,128]{1,0:T(8,128)}, f32[72,128]{1,0:T(8,128)S(1)}, u32[]{:S(2)}, u32[]{:S(2)}) collective-permute-start(f32[72,128]{1,0:T(8,128)} %get-tuple-element.52), channel_id=1, source_target_pairs={{0,7},{1,2},{2,1},{3,4},{4,3},{5,6},{6,5},{7,0},{8,15},{9,10},{10,... | collective-permute-start | bytes 110600 | tf_op jit(solution)/shard_map/ppermute | solution.py:39
  8.6 1.5 %collective-permute-start.3 = (f32[72,128]{1,0:T(8,128)}, f32[72,128]{1,0:T(8,128)S(1)}, u32[]{:S(2)}, u32[]{:S(2)}) collective-permute-start(f32[72,128]{1,0:T(8,128)} %get-tuple-element.53), channel_id=1, source_target_pairs={{0,24},{8,16},{16,8},{24,0},{1,25},{9,17},{17,9},{25,1},{2,26},{10... | collective-permute-start | bytes 110600 | tf_op jit(solution)/shard_map/ppermute | solution.py:39
  10.1 0.0 copy-start
  10.1 0.8 %copy-done = f32[80,128]{1,0:T(8,128)S(1)} copy-done((f32[80,128]{1,0:T(8,128)S(1)}, f32[80,128]{1,0:T(8,128)}, u32[]{:S(2)}) %copy-start) | copy-done | bytes 40984
  10.8 0.0 copy-start.1
  10.8 0.7 %copy-done.1 = s32[8,8]{1,0:T(8,128)S(1)} copy-done((s32[8,8]{1,0:T(8,128)S(1)}, s32[8,8]{1,0:T(8,128)}, u32[]{:S(2)}) %copy-start.1) | copy-done | bytes 280
  11.5 1.4 %shard_map.112 = (bf16[1024,128]{1,0:T(8,128)(2,1)S(1)}, f32[1024,384]{1,0:T(8,128)S(1)}, f32[80,128]{1,0:T(8,128)S(1)}, s32[8,8]{1,0:T(8,128)S(1)}, bf16[2048,1...) custom-call(s32[8,8]{1,0:T(8,128)S(1)} %copy-done.1, ...), custom_call_target="tpu_custom_call" | custom-call | tf_op jit(solution)/shard_map/pallas_call | solution.py:587
  13.0 0.0 collective-permute-done.m0
  13.0 0.0 collective-permute-done.1.m1
  13.0 0.0 collective-permute-done.2.m2
  13.0 0.6 %collective-permute-done.3.m3 = f32[72,128]{1,0:T(8,128)S(1)} collective-permute-done((f32[72,128]{1,0:T(8,128)}, f32[72,128]{1,0:T(8,128)S(1)}, u32[]{:S(2)}, u32[]{:S(2)}) %collective-permute-start.3) | collective-permute-done | bytes 36896 | tf_op jit(solution)/shard_map/ppermute | solution.py:39
  13.6 0.0 copy-start.2
  13.6 0.0 copy-start.3
  13.6 3.3 %shard_map.113 = (f32[8,128]{1,0:T(8,128)S(1)}, f32[8,128]{1,0:T(8,128)S(1)}, f32[1024,1024]{1,0:T(8,128)S(1)}, f32[1024,1024]{1,0:T(8,128)S(1)}) custom-call(s32[8,8]{1,0:T(8,128)S(1)} %get-tuple-element.45.plan, bf16[1024,128]{1,0:T(8,128)(2,1)S(1)} %get-tuple-element.46.left, f32[1024,384]{1,0:T(8,128)S(1)} %get-tuple-element.47.columns, ...), custom_call_target="tpu_custom_call" | custom-call | flops 3000000000 | bytes 200000 | tf_op jit(solution)/shard_map/pallas_call | solution.py:548
  17.0 0.1 collective-permute-start.4
  17.0 0.0 copy-done.2
  17.1 0.0 copy-done.3
  17.1 4.1 %shard_map.114 = (f32[72,128]{1,0:T(8,128)S(1)}, f32[64,128]{1,0:T(8,128)S(1)}, f32[64,128]{1,0:T(8,128)S(1)}, f32[64,128]{1,0:T(8,128)S(1)}, f32[64,128]{1,0:T(8,128)S(1)}) custom-call(s32[8,8]{1,0:T(8,128)S(1)} %get-tuple-element.45.plan, s32[1,4]{1,0:T(1,128)S(1)} %bitcast.10, s32[1,4]{1,0:T(1,128)S(1)} %bitcast.12, ...), custom_call_target="tpu_custom_call" | custom-call | flops 5000000000 | bytes 200000 | tf_op jit(solution)/shard_map/pallas_call | solution.py:548
  21.2 0.4 collective-permute-done.4
  21.5 1.5 %collective-permute-start.5 = (f32[8,128]{1,0:T(8,128)S(1)}, f32[8,128]{1,0:T(8,128)S(1)}, u32[]{:S(2)}, u32[]{:S(2)}) collective-permute-start(f32[8,128]{1,0:T(8,128)S(1)} %min.18), channel_id=1, source_target_pairs={{0,16},{8,24},{16,0},{24,8},{1,17},{9,25},{17,1},{25,9},{2,18},{10... | collective-permute-start | bytes 12296 | tf_op jit(solution)/shard_map/ppermute | solution.py:561
  23.1 0.0 collective-permute-start.7
  23.1 0.5 %collective-permute-start.8 = (f32[64,128]{1,0:T(8,128)S(1)}, f32[64,128]{1,0:T(8,128)S(1)}, u32[]{:S(2)}, u32[]{:S(2)}) collective-permute-start(f32[64,128]{1,0:T(8,128)S(1)} %get-tuple-element.72), channel_id=1, source_target_pairs={{0,8},{8,0},{16,24},{24,16},{1,9},{9,1},{17,25},{25,17},{2,10},{10... | collective-permute-start | bytes 98312 | tf_op jit(solution)/shard_map/ppermute | solution.py:39
  23.6 0.3 collective-permute-start.9
  23.9 1.4 %collective-permute-start.10 = (f32[64,128]{1,0:T(8,128)S(1)}, f32[64,128]{1,0:T(8,128)S(1)}, u32[]{:S(2)}, u32[]{:S(2)}) collective-permute-start(f32[64,128]{1,0:T(8,128)S(1)} %get-tuple-element.74), channel_id=1, source_target_pairs={{0,24},{8,16},{16,8},{24,0},{1,25},{9,17},{17,9},{25,1},{2,26},{10... | collective-permute-start | bytes 98312 | tf_op jit(solution)/shard_map/ppermute | solution.py:39
  25.3 0.0 collective-permute-done.5
  25.3 1.1 %collective-permute-start.6 = (f32[8,128]{1,0:T(8,128)S(1)}, f32[8,128]{1,0:T(8,128)S(1)}, u32[]{:S(2)}, u32[]{:S(2)}) collective-permute-start(f32[8,128]{1,0:T(8,128)S(1)} %min.19), channel_id=1, source_target_pairs={{0,8},{8,0},{16,24},{24,16},{1,9},{9,1},{17,25},{25,17},{2,10},{10... | collective-permute-start | bytes 12296 | tf_op jit(solution)/shard_map/ppermute | solution.py:561
  26.4 3.9 %shard_map.115 = (bf16[2048,1024]{1,0:T(8,128)(2,1)S(1)}, f32[1024,1024]{1,0:T(8,128)S(1)}, f32[1024,128]{1,0:T(8,128)S(1)}) custom-call(s32[8,8]{1,0:T(8,128)S(1)} %get-tuple-element.45.plan, f32[1024,384]{1,0:T(8,128)S(1)} %get-tuple-element.47.columns, f32[1024,1024]{1,0:T(8,128)S(1)} %get-tuple-element.55.distance, ...), custom_call_target="tpu_custom_call" | custom-call | flops 1000000000 | bytes 200000 | tf_op jit(solution)/shard_map/pallas_call | solution.py:548
  30.3 0.0 collective-permute-done.6
  30.3 0.0 collective-permute-done.7.s0
  30.3 0.0 collective-permute-done.8.s1
  30.3 0.0 collective-permute-done.9.s2
  30.4 0.0 collective-permute-done.10.s3
  30.4 0.1 collective-permute-start.13
  30.4 1.9 %collective-permute-start.12 = (f32[8,128]{1,0:T(8,128)S(1)}, f32[8,128]{1,0:T(8,128)S(1)}, u32[]{:S(2)}, u32[]{:S(2)}) collective-permute-start(f32[8,128]{1,0:T(8,128)S(1)} %min.20), channel_id=1, source_target_pairs={{0,3},{1,2},{2,1},{3,0},{4,7},{5,6},{6,5},{7,4},{8,11},{9,10},{10,... | collective-permute-start | bytes 12296 | tf_op jit(solution)/shard_map/ppermute | solution.py:661
  32.4 0.3 collective-permute-start.11
  32.7 5.0 %shard_map.116 = (f32[3,1024]{1,0:T(4,128)}, f32[8,128]{1,0:T(8,128)}, f32[8,128]{1,0:T(8,128)}) custom-call(s32[8,8]{1,0:T(8,128)S(1)} %get-tuple-element.45.plan, bf16[2048,1024]{1,0:T(8,128)(2,1)S(1)} %get-tuple-element.67.weights, f32[1024,1024]{1,0:T(8,128)S(1)} %get-tuple-element.68.damping, f32[1024,128]{1,0:T(8,128)S(1)} %get-tuple-element.69.dens_col, ...), custom_call_target="tpu_custom_call" | custom-call | flops 5000000000 | bytes 200000 | tf_op jit(solution)/shard_map/pallas_call | solution.py:548
  37.7 0.0 collective-permute-done.13
  37.7 0.0 collective-permute-done.12
  37.7 0.0 collective-permute-done.11
  37.7 0.6 %divide_bitcast_fusion = f32[1024]{0:T(1024)} fusion(f32[8,128]{1,0:T(8,128)S(1)} %get-tuple-element.83, f32[8,128]{1,0:T(8,128)S(1)} %collective-permute-done.13, f32[8,128]{1,0:T(8,128)S(1)} %collective-permute-done.12, f32[8,128]{1,0:T(8,128)S(1)} %min.20, f32[8,128]{1,0:T(8,128)S(1)} %collective-permute-done.11), kind=kLoop, calls=%fused_computation | loop fusion | flops 4096 | bytes 24576 | tf_op jit(solution)/shard_map/reshape | solution.py:666
  (3 shorter events, 0.0 us)
Async XLA Ops:
  2.2 10.8 %collective-permute-start = (f32[72,128]{1,0:T(8,128)}, f32[72,128]{1,0:T(8,128)S(1)}, u32[]{:S(2)}, u32[]{:S(2)}) collective-permute-start(f32[72,128]{1,0:T(8,128)} %get-tuple-element.50), channel_id=1, source_target_pairs={{0,1},{1,0},{2,3},{3,2},{4,5},{5,4},{6,7},{7,6},{8,9},{9,8},{10,11... | collective-permute-start | bytes 110600 | tf_op jit(solution)/shard_map/ppermute | solution.py:39
  2.6 10.3 %collective-permute-start.1 = (f32[72,128]{1,0:T(8,128)}, f32[72,128]{1,0:T(8,128)S(1)}, u32[]{:S(2)}, u32[]{:S(2)}) collective-permute-start(f32[72,128]{1,0:T(8,128)} %get-tuple-element.51), channel_id=1, source_target_pairs={{0,8},{8,0},{16,24},{24,16},{1,9},{9,1},{17,25},{25,17},{2,10},{10... | collective-permute-start | bytes 110600 | tf_op jit(solution)/shard_map/ppermute | solution.py:39
  5.2 7.8 %collective-permute-start.2 = (f32[72,128]{1,0:T(8,128)}, f32[72,128]{1,0:T(8,128)S(1)}, u32[]{:S(2)}, u32[]{:S(2)}) collective-permute-start(f32[72,128]{1,0:T(8,128)} %get-tuple-element.52), channel_id=1, source_target_pairs={{0,7},{1,2},{2,1},{3,4},{4,3},{5,6},{6,5},{7,0},{8,15},{9,10},{10,... | collective-permute-start | bytes 110600 | tf_op jit(solution)/shard_map/ppermute | solution.py:39
  8.6 5.1 %collective-permute-start.3 = (f32[72,128]{1,0:T(8,128)}, f32[72,128]{1,0:T(8,128)S(1)}, u32[]{:S(2)}, u32[]{:S(2)}) collective-permute-start(f32[72,128]{1,0:T(8,128)} %get-tuple-element.53), channel_id=1, source_target_pairs={{0,24},{8,16},{16,8},{24,0},{1,25},{9,17},{17,9},{25,1},{2,26},{10... | collective-permute-start | bytes 110600 | tf_op jit(solution)/shard_map/ppermute | solution.py:39
  10.1 0.8 %copy-start = (f32[80,128]{1,0:T(8,128)S(1)}, f32[80,128]{1,0:T(8,128)}, u32[]{:S(2)}) copy-start(f32[80,128]{1,0:T(8,128)} %get-tuple-element.44.own) | copy-start | bytes 122884
  10.8 0.7 %copy-start.1 = (s32[8,8]{1,0:T(8,128)S(1)}, s32[8,8]{1,0:T(8,128)}, u32[]{:S(2)}) copy-start(s32[8,8]{1,0:T(8,128)} %pairs.1) | copy-start | bytes 772
  13.6 3.4 %copy-start.2 = (s32[4,1]{0,1:T(1,128)S(1)}, s32[4,1]{0,1:T(1,128)}, u32[]{:S(2)}) copy-start(s32[4,1]{0,1:T(1,128)} %param.13) | copy-start | bytes 52
  13.6 3.4 %copy-start.3 = (s32[4,1]{0,1:T(1,128)S(1)}, s32[4,1]{0,1:T(1,128)}, u32[]{:S(2)}) copy-start(s32[4,1]{0,1:T(1,128)} %param.14) | copy-start | bytes 52
  17.0 4.6 %collective-permute-start.4 = (f32[8,128]{1,0:T(8,128)S(1)}, f32[8,128]{1,0:T(8,128)S(1)}, u32[]{:S(2)}, u32[]{:S(2)}) collective-permute-start(f32[8,128]{1,0:T(8,128)S(1)} %get-tuple-element.54), channel_id=1, source_target_pairs={{0,4},{1,5},{2,6},{3,7},{4,0},{5,1},{6,2},{7,3},{8,12},{9,13},{10,... | collective-permute-start | bytes 12296 | tf_op jit(solution)/shard_map/ppermute | solution.py:561
  21.5 3.8 %collective-permute-start.5 = (f32[8,128]{1,0:T(8,128)S(1)}, f32[8,128]{1,0:T(8,128)S(1)}, u32[]{:S(2)}, u32[]{:S(2)}) collective-permute-start(f32[8,128]{1,0:T(8,128)S(1)} %min.18), channel_id=1, source_target_pairs={{0,16},{8,24},{16,0},{24,8},{1,17},{9,25},{17,1},{25,9},{2,18},{10... | collective-permute-start | bytes 12296 | tf_op jit(solution)/shard_map/ppermute | solution.py:561
  23.1 7.3 %collective-permute-start.7 = (f32[64,128]{1,0:T(8,128)S(1)}, f32[64,128]{1,0:T(8,128)S(1)}, u32[]{:S(2)}, u32[]{:S(2)}) collective-permute-start(f32[64,128]{1,0:T(8,128)S(1)} %get-tuple-element.71), channel_id=1, source_target_pairs={{0,1},{1,0},{2,3},{3,2},{4,5},{5,4},{6,7},{7,6},{8,9},{9,8},{10,11... | collective-permute-start | bytes 98312 | tf_op jit(solution)/shard_map/ppermute | solution.py:39
  23.1 7.3 %collective-permute-start.8 = (f32[64,128]{1,0:T(8,128)S(1)}, f32[64,128]{1,0:T(8,128)S(1)}, u32[]{:S(2)}, u32[]{:S(2)}) collective-permute-start(f32[64,128]{1,0:T(8,128)S(1)} %get-tuple-element.72), channel_id=1, source_target_pairs={{0,8},{8,0},{16,24},{24,16},{1,9},{9,1},{17,25},{25,17},{2,10},{10... | collective-permute-start | bytes 98312 | tf_op jit(solution)/shard_map/ppermute | solution.py:39
  23.6 6.7 %collective-permute-start.9 = (f32[64,128]{1,0:T(8,128)S(1)}, f32[64,128]{1,0:T(8,128)S(1)}, u32[]{:S(2)}, u32[]{:S(2)}) collective-permute-start(f32[64,128]{1,0:T(8,128)S(1)} %get-tuple-element.73), channel_id=1, source_target_pairs={{0,7},{1,2},{2,1},{3,4},{4,3},{5,6},{6,5},{7,0},{8,15},{9,10},{10,... | collective-permute-start | bytes 98312 | tf_op jit(solution)/shard_map/ppermute | solution.py:39
  23.9 6.5 %collective-permute-start.10 = (f32[64,128]{1,0:T(8,128)S(1)}, f32[64,128]{1,0:T(8,128)S(1)}, u32[]{:S(2)}, u32[]{:S(2)}) collective-permute-start(f32[64,128]{1,0:T(8,128)S(1)} %get-tuple-element.74), channel_id=1, source_target_pairs={{0,24},{8,16},{16,8},{24,0},{1,25},{9,17},{17,9},{25,1},{2,26},{10... | collective-permute-start | bytes 98312 | tf_op jit(solution)/shard_map/ppermute | solution.py:39
  25.3 5.0 %collective-permute-start.6 = (f32[8,128]{1,0:T(8,128)S(1)}, f32[8,128]{1,0:T(8,128)S(1)}, u32[]{:S(2)}, u32[]{:S(2)}) collective-permute-start(f32[8,128]{1,0:T(8,128)S(1)} %min.19), channel_id=1, source_target_pairs={{0,8},{8,0},{16,24},{24,16},{1,9},{9,1},{17,25},{25,17},{2,10},{10... | collective-permute-start | bytes 12296 | tf_op jit(solution)/shard_map/ppermute | solution.py:561
  30.4 7.3 %collective-permute-start.13 = (f32[8,128]{1,0:T(8,128)S(1)}, f32[8,128]{1,0:T(8,128)S(1)}, u32[]{:S(2)}, u32[]{:S(2)}) collective-permute-start(f32[8,128]{1,0:T(8,128)S(1)} %min.20), channel_id=1, source_target_pairs={{0,1},{1,0},{2,3},{3,2},{4,5},{5,4},{6,7},{7,6},{8,9},{9,8},{10,11... | collective-permute-start | bytes 12296 | tf_op jit(solution)/shard_map/ppermute | solution.py:661
  30.4 7.3 %collective-permute-start.12 = (f32[8,128]{1,0:T(8,128)S(1)}, f32[8,128]{1,0:T(8,128)S(1)}, u32[]{:S(2)}, u32[]{:S(2)}) collective-permute-start(f32[8,128]{1,0:T(8,128)S(1)} %min.20), channel_id=1, source_target_pairs={{0,3},{1,2},{2,1},{3,0},{4,7},{5,6},{6,5},{7,4},{8,11},{9,10},{10,... | collective-permute-start | bytes 12296 | tf_op jit(solution)/shard_map/ppermute | solution.py:661
  32.4 5.3 %collective-permute-start.11 = (f32[8,128]{1,0:T(8,128)S(1)}, f32[8,128]{1,0:T(8,128)S(1)}, u32[]{:S(2)}, u32[]{:S(2)}) collective-permute-start(f32[8,128]{1,0:T(8,128)S(1)} %min.20), channel_id=1, source_target_pairs={{0,2},{1,3},{2,0},{3,1},{4,6},{5,7},{6,4},{7,5},{8,10},{9,11},{10,... | collective-permute-start | bytes 12296 | tf_op jit(solution)/shard_map/ppermute | solution.py:661
